TPU v7x, 32 devices: a whole 2x2x4 slice. The times are simulated.
32 devices in a mesh: sub: 8 (over y, x, core), rep: 4 (over z).
Axes of the slice: x: 2, y: 2, z: 4, core: 2. Of those that a mesh axis runs over, the one named last changes fastest.
Arguments:
- dual_ops: bfloat16 [32, 1024, 1024], P(('sub', 'rep'))
- mode_traces: float32 [32, 6, 1024], P(('sub', 'rep')), may hold values from -0.046875 to 0.046875
- route: int32 [32, 1024], P(('sub', 'rep')), may hold values from 0 to 1023, each once within a row
- mode_block: int32 [32, 1], replicated, may hold values from 0 to 1
- local_gap: float32 [32, 32768], P(None, ('sub', 'rep')), may hold values from -6 to 6
Outputs:
- multipliers: float32 [32, 32768], P(None, ('sub', 'rep'))
- amplitudes: float32 [32, 12], replicated
Inputs may be any that keep to these rules, and one draw needn't show every extreme that they name: Each row of route lists every number below 1024 once. `mode_block`: every aggregate holds at least one subdomain.
All inputs are finite; a program needn't handle non-finite values.
Results may differ from a plain program's by a relative error of at most 0.003.
Values sent between devices are 32-bit elements; how exact they have to be, the bound alone decides.
No kernel may reach another device: no remote copies, remote signals or barrier semaphores. Data moves between devices by JAX's collectives and lax.ppermute only.
A program may use at most 64 MiB of HBM per device.

v0:
```python
import functools

import jax
import jax.numpy as jnp
from jax import lax
from jax.experimental import pallas as pl
from jax.experimental.pallas import tpu as pltpu
from jax.sharding import PartitionSpec as P

MODES = 6
AGG_SUBS = 16
ITERS = 2
GROUP = 8
SCALAR_LANES = (MODES, MODES + 1, GROUP + MODES, GROUP + MODES + 1, 2 * GROUP + MODES)

HIGHEST = lax.Precision.HIGHEST
VMEM = pl.BlockSpec(memory_space=pltpu.VMEM)
HBM = pl.BlockSpec(memory_space=pltpu.HBM)
NN = (((1,), (0,)), ((), ()))
NT = (((1,), (1,)), ((), ()))


def split(values):
    high = values.astype(jnp.bfloat16).astype(jnp.float32)
    return jnp.concatenate([high, values - high], axis=0).astype(jnp.bfloat16)


def split_dot(values, matrix, dims):
    rows = values.shape[0]
    both = lax.dot_general(split(values), matrix, dims, preferred_element_type=jnp.float32)
    return both[:rows] + both[rows:]


def small_dot(left, right):
    return jnp.dot(left, right, precision=HIGHEST, preferred_element_type=jnp.float32)


def send_far(values, far_ref, *pair_refs):
    height = values.shape[0]
    per_peer = pair_refs[0].shape[1]
    slots = split_dot(values, far_ref[...], NN)
    for at, ref in enumerate(reversed(pair_refs)):
        start = 2 * at * per_peer
        ref[:height] = slots[:, start + per_peer : start + 2 * per_peer]
        ref[height:] = slots[:, start : start + per_peer]


def send_near(values, edge_ref, near_ref, back_ref, stay_ref):
    per_peer = back_ref.shape[1]
    slots = split_dot(values, edge_ref[...], NN)
    for at, ref in enumerate((near_ref, back_ref, stay_ref)):
        ref[...] = slots[:, at * per_peer : (at + 1) * per_peer]


def straight(last_ref, pair_refs):
    height = last_ref.shape[0]
    return jnp.concatenate([*(ref[:height] for ref in pair_refs), last_ref[...]], axis=1)


def for_other(near_ref, pair_refs):
    height = near_ref.shape[0]
    return jnp.concatenate([near_ref[...], *(ref[height:] for ref in pair_refs)], axis=1)


def handed(got_ref, height):
    return jnp.concatenate([got_ref[at : at + height] for at in range(0, got_ref.shape[0], height)], axis=1)


def spread(values, loads, groups):
    modes = values[loads:]
    label = modes[MODES : MODES + 1]
    used = lax.broadcasted_iota(jnp.int32, modes.shape, 0) < MODES
    parts = [jnp.where(used & (label == group), modes, 0.0) for group in range(groups)]
    return jnp.concatenate([values[:loads], *parts], axis=0)


def one_hot(route_ref, peer, per_peer):
    start = pl.multiple_of(peer * per_peer, per_peer)
    row_ids = lax.broadcasted_iota(jnp.int32, (route_ref.shape[1], per_peer), 0)
    return jnp.where(row_ids == route_ref[:, pl.ds(start, per_peer)], 1.0, 0.0).astype(jnp.bfloat16)


def place_kernel(
    route_hbm, block_hbm, gap_hbm, traces_hbm, operator_hbm,
    far_ref, values_ref, operator_ref, route_ref, *refs,
):
    *pair_refs, block_ref, traces_ref, sems = refs
    loads, rows = gap_hbm.shape
    per_peer = pair_refs[0].shape[1]
    peers = rows // per_peer
    copies = [
        pltpu.make_async_copy(source, target, sems.at[at])
        for at, (source, target) in enumerate(
            (
                (route_hbm, route_ref),
                (block_hbm, block_ref),
                (traces_hbm, traces_ref),
                (gap_hbm, values_ref.at[pl.ds(0, loads)]),
                (operator_hbm, operator_ref),
            )
        )
    ]
    for copy in copies:
        copy.start()
    own_index = lax.axis_index("sub")
    device = own_index * lax.axis_size("rep") + lax.axis_index("rep")
    copies[0].wait()
    for offset in range(2, peers):
        at = (offset - 2) * per_peer
        far_ref[:, at : at + per_peer] = one_hot(route_ref, own_index ^ offset, per_peer)
    copies[1].wait()
    copies[2].wait()
    blocks = block_ref[...]
    lane = lax.broadcasted_iota(jnp.int32, blocks.shape, 1)
    own_block = jnp.sum(jnp.where(lane == device, blocks, 0), axis=1, keepdims=True)
    modes = traces_ref.shape[0]
    label = jnp.broadcast_to(own_block.astype(jnp.float32), (1, rows))
    for mode in range(modes):
        values_ref[loads + mode : loads + mode + 1] = traces_ref[mode]
    values_ref[loads + modes : loads + modes + 1] = label
    values_ref[loads + modes + 1 :] = jnp.zeros((GROUP - modes - 1, rows), jnp.float32)
    copies[3].wait()
    send_far(values_ref[...], far_ref, *pair_refs)
    copies[4].wait()


def ready_kernel(
    route_ref, far_ref, values_ref, operator_ref,
    edge_ref, slots_ref, placed_ref, near_ref, back_ref, stay_ref,
):
    per_peer = back_ref.shape[1]
    peers = far_ref.shape[1] // per_peer + 2
    own_index = lax.axis_index("sub")
    low = lax.broadcasted_iota(jnp.int32, (per_peer, per_peer), 0)
    high = lax.broadcasted_iota(jnp.int32, (per_peer, per_peer), 1)
    reverse = jnp.where(low + high == per_peer - 1, 1.0, 0.0).astype(jnp.bfloat16)
    own_columns = one_hot(route_ref, own_index, per_peer)
    near_columns = one_hot(route_ref, own_index ^ 1, per_peer)
    reversed_columns = jnp.dot(own_columns, reverse, preferred_element_type=jnp.float32).astype(jnp.bfloat16)
    edge_ref[...] = jnp.concatenate([near_columns, reversed_columns, own_columns], axis=1)
    for at in range(peers // 2 - 1):
        start = (peers - 4 - 2 * at) * per_peer
        slots_ref[0, :, at * per_peer : (at + 1) * per_peer] = far_ref[:, start + per_peer : start + 2 * per_peer]
        slots_ref[1, :, (at + 1) * per_peer : (at + 2) * per_peer] = far_ref[:, start : start + per_peer]
    slots_ref[0, :, (peers // 2 - 1) * per_peer :] = own_columns
    slots_ref[1, :, :per_peer] = near_columns
    send_near(values_ref[...], edge_ref, near_ref, back_ref, stay_ref)
    operator = operator_ref[0]
    for half in range(2):
        placed_ref[half] = jnp.dot(
            operator, slots_ref[half], preferred_element_type=jnp.float32
        ).astype(operator.dtype)


def first_half_kernel(placed_ref, stay_ref, back_ref, *refs):
    *pair_refs, jump_ref, image_ref = refs
    sent_refs, got_refs = pair_refs[: len(pair_refs) // 2], pair_refs[len(pair_refs) // 2 :]
    loads = stay_ref.shape[0] - GROUP
    groups = (jump_ref.shape[0] - loads) // GROUP
    own, got = (spread(straight(*refs), loads, groups) for refs in ((stay_ref, sent_refs), (back_ref, got_refs)))
    jump_ref[...] = own - got
    image_ref[...] = split_dot(own - got, placed_ref[0], NT)


def first_kernel(far_ref, placed_ref, half_ref, got_ref, near_ref, *refs):
    sent_refs, (jump_ref, image_ref, *pair_refs) = refs[: len(refs) // 2 - 1], refs[len(refs) // 2 - 1 :]
    height = near_ref.shape[0]
    loads = height - GROUP
    groups = (image_ref.shape[0] - loads) // GROUP
    own, got = (spread(value, loads, groups) for value in (for_other(near_ref, sent_refs), handed(got_ref, height)))
    jump_ref[...] = own - got
    image = half_ref[...] + split_dot(own - got, placed_ref[1], NT)
    image_ref[...] = image
    send_far(image, far_ref, *pair_refs)


def products_of(left, right):
    both = lax.dot_general(split(left), split(right), NT, preferred_element_type=jnp.float32)
    both = both[: left.shape[0]] + both[left.shape[0] :]
    return both + pltpu.roll(both, right.shape[0], 1)


def with_scalars(top, products, lanes):
    lane = lax.broadcasted_iota(jnp.int32, top.shape, 1)
    for at, product in zip(lanes, products):
        top = jnp.where(lane == at, jnp.sum(product, axis=1, keepdims=True), top)
    return top


def middle_kernel(
    edge_ref, slots_ref, straight_ref, handed_ref, image_ref, basis_ref, terms_ref, near_ref, back_ref, stay_ref
):
    image = image_ref[...]
    send_near(image, edge_ref, near_ref, back_ref, stay_ref)
    coarse = terms_ref.shape[1] // 8
    loads = image.shape[0] - coarse
    basis = split_dot(straight_ref[...], slots_ref[0], NT) + split_dot(handed_ref[...], slots_ref[1], NT)
    basis_ref[...] = basis
    left = jnp.concatenate([basis[:loads], image[:loads], basis[loads:]])
    empty = jnp.zeros((2 * coarse, basis.shape[1]), jnp.float32)
    both = products_of(left, jnp.concatenate([basis[loads:], image[loads:], empty]))
    strip = lax.broadcasted_iota(jnp.int32, (loads, 8 * coarse), 1) // coarse
    top = jnp.where(strip < 2, both[:loads], 0.0)
    top = jnp.where(strip == 4, both[loads : 2 * loads], top)
    residual = basis[:loads]
    terms_ref[:loads] = with_scalars(top, (residual * residual, residual * image[:loads]), SCALAR_LANES[:2])
    strip = lax.broadcasted_iota(jnp.int32, (coarse, 8 * coarse), 1) // coarse
    terms_ref[loads:] = jnp.where(strip < 2, both[2 * loads :], 0.0)


def second_half_kernel(slots_ref, placed_ref, stay_ref, back_ref, *refs):
    *pair_refs, jump_ref, second_ref = refs
    sent_refs, got_refs = pair_refs[: len(pair_refs) // 2], pair_refs[len(pair_refs) // 2 :]
    jump = straight(stay_ref, sent_refs) - straight(back_ref, got_refs)
    jump_ref[...] = split_dot(jump, slots_ref[0], NT)
    second_ref[...] = split_dot(jump, placed_ref[0], NT)


def second_kernel(slots_ref, placed_ref, basis_ref, half_jump_ref, half_second_ref, early_ref, got_ref, near_ref, *refs):
    *sent_refs, jump_ref, terms_ref = refs
    coarse = terms_ref.shape[1] // 8
    loads = basis_ref.shape[0] - coarse
    jump = for_other(near_ref, sent_refs) - handed(got_ref, loads + coarse)
    second = half_second_ref[...] + split_dot(jump, placed_ref[1], NT)
    jump = half_jump_ref[...] + split_dot(jump, slots_ref[1], NT)
    jump_ref[...] = jump
    basis = basis_ref[...]
    left = jnp.concatenate([basis[:loads], jump[:loads], second[:loads], basis[loads:], jump[loads:]])
    empty = jnp.zeros((coarse, basis.shape[1]), jnp.float32)
    both = products_of(left, jnp.concatenate([basis[loads:], empty, jump[loads:], second[loads:]]))
    along, jumped, doubled = (both[at * loads : (at + 1) * loads] for at in range(3))
    base, far = both[3 * loads : 3 * loads + coarse], both[3 * loads + coarse :]
    strip = lax.broadcasted_iota(jnp.int32, (loads, 8 * coarse), 1) // coarse
    top = jnp.where(strip == 2, doubled, 0.0)
    top = jnp.where(strip == 3, along, top)
    top = jnp.where(strip == 5, pltpu.roll(doubled, coarse, 1), top)
    top = jnp.where(strip >= 6, jumped, top)
    residual, jump_loads, second_loads = basis[:loads], jump[:loads], second[:loads]
    products = (jump_loads * jump_loads, jump_loads * second_loads, residual * second_loads)
    terms_ref[:loads] = early_ref[:loads] + with_scalars(top, products, SCALAR_LANES[2:])
    strip = lax.broadcasted_iota(jnp.int32, (coarse, 8 * coarse), 1) // coarse
    base = jnp.where((strip == 2) | (strip == 3), base, 0.0)
    terms_ref[loads:] = early_ref[loads:] + jnp.where(strip < 4, base, far)


def sum_kernel(count, *refs):
    parts = [ref[...] for ref in reversed(refs[:count])]
    while len(parts) > 1:
        parts = [low + high for low, high in zip(parts[::2], parts[1::2])]
    for ref in refs[count:]:
        ref[...] = parts[0]


def eliminate(work, coarse):
    row = lax.broadcasted_iota(jnp.int32, work.shape, 0)
    for first in range(coarse):
        if first % 2 or first % GROUP >= MODES:
            continue
        second = first + 1
        left = jnp.broadcast_to(work[:, first : first + 1], work.shape)
        right = jnp.broadcast_to(work[:, second : second + 1], work.shape)
        upper, lower = work[first : first + 1], work[second : second + 1]
        pivot = 1.0 / left[first : first + 1]
        ratio = left[second : second + 1] * pivot
        corner = 1.0 / (right[second : second + 1] - ratio * right[first : first + 1])
        lower = (lower - ratio * upper) * corner
        upper = (upper - right[first : first + 1] * lower) * pivot
        work = work - left * upper - right * lower
        work = jnp.where(row == first, upper, jnp.where(row == second, lower, work))
    return work


def thin_dot(left, right):
    high, right_high = (value.astype(jnp.bfloat16).astype(jnp.float32) for value in (left, right))
    return jnp.dot(
        jnp.concatenate([high, left - high, high], axis=1).astype(jnp.bfloat16),
        jnp.concatenate([right_high, right_high, right - right_high], axis=0).astype(jnp.bfloat16),
        preferred_element_type=jnp.float32,
    )


def final_kernel(terms_ref, basis_ref, jump_ref, multipliers_ref, amplitudes_ref):
    coarse = terms_ref.shape[1] // 8
    loads = basis_ref.shape[0] - coarse
    groups = coarse // GROUP
    by_load = terms_ref[:loads].T
    used = lax.broadcasted_iota(jnp.int32, (coarse, loads), 0) % GROUP < MODES

    def strip(at):
        return by_load[at * coarse : (at + 1) * coarse]

    def block(at):
        return terms_ref[loads:, at * coarse : (at + 1) * coarse]

    def total(values):
        return jnp.sum(values, axis=0, keepdims=True)

    res_res, res_image, jump_jump, jump_second, res_second = (by_load[at : at + 1] for at in SCALAR_LANES)
    coarse_res, res_h = (jnp.where(used, strip(at), 0.0) for at in (0, 1))
    second_z, res_dz, image_g, second_g, jump_z, jump_dz = (strip(at) for at in range(2, 8))
    g_h, g_dz, z_z, z_dz = block(1), block(3), block(6), block(7)
    row = lax.broadcasted_iota(jnp.int32, (coarse, coarse), 0)
    unit = jnp.where(row == lax.broadcasted_iota(jnp.int32, (coarse, coarse), 1), 1.0, 0.0)
    empty = jnp.zeros((coarse, 5 * coarse - 2 * loads), jnp.float32)
    solved = eliminate(
        jnp.concatenate([terms_ref[loads:, : 2 * coarse], coarse_res, image_g, unit, empty], axis=1), coarse
    )
    inverse_h = solved[:, coarse : 2 * coarse]
    amounts = solved[:, 2 * coarse : 2 * coarse + loads]
    inverse_image = solved[:, 2 * coarse + loads : 2 * coarse + 2 * loads]
    inverse = solved[:, 2 * coarse + 2 * loads : 3 * coarse + 2 * loads]
    products = small_dot(jnp.concatenate([inverse_h, g_h, z_z, g_dz, z_dz], axis=0), amounts)
    inverse_h_amounts, h_amounts, z_amounts, g_dz_amounts, z_dz_amounts = (
        products[at * coarse : (at + 1) * coarse] for at in range(5)
    )
    shares = 2.0 * (inverse_image - inverse_h_amounts)
    both = jnp.concatenate([amounts, shares], axis=0).T
    basis_g, jump_z_rows = basis_ref[loads:], jump_ref[loads:]
    d = basis_ref[:loads] - thin_dot(both[:, :coarse], basis_g)
    u = jump_ref[:loads] - thin_dot(both, jnp.concatenate([jump_z_rows, basis_g], axis=0))
    products = small_dot(jnp.concatenate([g_h, z_z], axis=0), shares)
    image_d = image_g - h_amounts
    inner = res_res - total(amounts * coarse_res)
    curvature = 2.0 * (res_image - total(amounts * (res_h + image_d)))
    u_u = jump_jump - total(amounts * (2.0 * jump_z - z_amounts) + 2.0 * image_d * shares)
    second_u = second_g - g_dz_amounts - products[:coarse]
    jump_u = second_z - z_dz_amounts - 0.5 * products[coarse:]
    d_second = res_second - total(amounts * (res_dz + second_u) + shares * res_h)
    u_second = jump_second - total(amounts * (jump_dz + jump_u) + shares * (0.5 * jump_z + second_u))
    step = inner / curvature
    renewed = step * step * u_u - inner
    grown = 1.0 + renewed / inner
    curvature = grown * grown * curvature - grown * step * (2.0 * d_second + u_u) + 2.0 * step * step * u_second
    second_step = renewed / curvature
    on_d, on_u = step + second_step * grown, second_step * step
    amplitudes = amounts - on_d * shares + 2.0 * on_u * small_dot(inverse, second_u)
    amplitudes_ref[...] = jnp.concatenate(
        [amplitudes[label * GROUP : label * GROUP + MODES] for label in range(groups)], axis=0
    )
    weights = jnp.concatenate([on_d, on_u, jnp.zeros((6, loads), jnp.float32)], axis=0).T
    multipliers_ref[...] = weights[:, 0:1] * d - weights[:, 1:2] * u


def call(kernel, shapes, in_specs, name, scratch=(), flops=0):
    return pl.pallas_call(
        kernel,
        out_shape=[jax.ShapeDtypeStruct(*shape) for shape in shapes],
        in_specs=in_specs,
        out_specs=[VMEM] * len(shapes),
        scratch_shapes=scratch,
        compiler_params=pltpu.CompilerParams(vmem_limit_bytes=24 * 1024 * 1024),
        cost_estimate=pl.CostEstimate(flops=flops, bytes_accessed=2**20, transcendentals=0),
        name=name,
    )


def permute(values, offset, plane_offset=0):
    peers, planes = lax.axis_size("sub"), lax.axis_size("rep")
    offset = offset * planes + plane_offset
    return lax.ppermute(values, ("sub", "rep"), [(at, at ^ offset) for at in range(peers * planes)])


def to_chips(*pairs):
    return [permute(pair, 2 * (len(pairs) - at) + 1) for at, pair in enumerate(pairs)]


def to_core(near, *pairs):
    return permute(jnp.concatenate([near, *(pair[near.shape[0] :] for pair in pairs)], axis=0), 1)


def total(terms):
    chips = [(offset + 1, 0) for offset in reversed(range(2, lax.axis_size("sub"), 2))]
    chips = chips[-1:] + chips[:-1]
    planes = [(1, offset) for offset in reversed(range(1, lax.axis_size("rep")))]
    copies = [terms]
    for offsets, following in (([(1, 0)], len(chips)), (chips, len(planes)), (planes, 1)):
        parts = [permute(copy, *offset) for copy, offset in zip(copies, offsets)]
        kernel = functools.partial(sum_kernel, len(parts) + 1)
        copies = call(kernel, [(terms.shape, terms.dtype)] * following, [VMEM] * (len(parts) + 1), "sum")(
            *parts, copies[0]
        )
    return copies[0]


def fused_body(dual_ops, mode_traces, route, mode_block, local_gap):
    peers = lax.axis_size("sub")
    loads, rows = local_gap.shape
    modes = mode_traces.shape[1]
    subs = mode_block.shape[0]
    groups = subs // AGG_SUBS
    per_peer = rows // peers
    height = loads + GROUP * groups
    f32, i32 = jnp.float32, jnp.int32
    tall = ((height, rows), f32)
    wide = ((height, 8 * GROUP * groups), f32)

    def pairs(height):
        return [((2 * height, per_peer), f32)] * (peers // 2 - 1)

    def singles(height):
        return [((height, per_peer), f32)] * 3

    def held(value):
        return pltpu.with_memory_space_constraint(value, pltpu.HBM)

    inputs = [route, mode_block.reshape(1, subs), local_gap, mode_traces.transpose(1, 0, 2), dual_ops]
    short = loads + GROUP
    far, values, operator, route, *send = call(
        place_kernel,
        [
            ((rows, rows - 2 * per_peer), jnp.bfloat16),
            ((short, rows), f32),
            (dual_ops.shape, dual_ops.dtype),
            (route.shape, i32),
            *pairs(short),
        ],
        [HBM] * 5,
        "place",
        [pltpu.VMEM((1, subs), i32), pltpu.VMEM((modes, 1, rows), f32), pltpu.SemaphoreType.DMA((5,))],
    )(*(held(value) for value in inputs))
    got = to_chips(*send)
    halves = ((2, rows, rows // 2), dual_ops.dtype)
    edge, slots, placed, near, back, stay = call(
        ready_kernel,
        [((rows, 3 * per_peer), jnp.bfloat16), halves, halves, *singles(short)],
        [VMEM] * 4,
        "ready",
        flops=2 * rows * rows * rows,
    )(route, far, values, operator)
    got_near = to_core(near, *got)
    half = ((height, rows // 2), f32)
    straight_jump, half_image = call(
        first_half_kernel, [half, tall], [VMEM] * (3 + 2 * len(got)), "first_half", flops=2 * rows * rows * height
    )(placed, stay, back, *send, *got)
    handed_jump, image, *image_send = call(
        first_kernel, [half, tall, *pairs(height)], [VMEM] * (5 + len(send)), "first"
    )(far, placed, half_image, got_near, near, *send)
    got = to_chips(*image_send)
    basis, terms, near, back, stay = call(
        middle_kernel, [tall, wide, *singles(height)], [VMEM] * 5, "middle", flops=4 * rows * rows * height
    )(edge, slots, straight_jump, handed_jump, image)
    got_near = to_core(near, *got)
    half_jump, half_second = call(
        second_half_kernel, [tall, tall], [VMEM] * (4 + 2 * len(got)), "second_half", flops=4 * rows * rows * height
    )(slots, placed, stay, back, *image_send, *got)
    jump, terms = call(second_kernel, [tall, wide], [VMEM] * (8 + len(got)), "second")(
        slots, placed, basis, half_jump, half_second, terms, got_near, near, *image_send
    )
    multipliers, amplitudes = call(
        final_kernel, [((loads, rows), f32), ((MODES * groups, loads), f32)], [VMEM] * 3, "final"
    )(total(terms), basis, jump)
    return multipliers, amplitudes.T


def general_body(dual_ops, mode_traces, route, mode_block, local_gap):
    own_index = lax.axis_index("sub")
    plane_index = lax.axis_index("rep")
    peer_count = lax.axis_size("sub")
    plane_count = lax.axis_size("rep")
    operator = dual_ops[0]
    traces = mode_traces[0]
    slot_rows = route[0]
    rows_here = operator.shape[0]
    load_cases = local_gap.shape[0]
    per_peer = rows_here // peer_count
    blocks = mode_block[:, 0]
    block_count = blocks.shape[0] // AGG_SUBS
    coarse = block_count * MODES
    positions = jnp.arange(rows_here, dtype=jnp.int32)
    inverse = jnp.zeros((rows_here,), jnp.int32).at[slot_rows].set(positions)
    slot_peer = positions // per_peer
    within = positions % per_peer
    flip_index = jnp.where(
        slot_peer == own_index, slot_peer * per_peer + per_peer - 1 - within, positions
    )
    peer_ids = jnp.arange(peer_count, dtype=jnp.int32)
    peer_blocks = blocks[peer_ids * plane_count + plane_index]
    own_block = blocks[own_index * plane_count + plane_index]
    labels = jnp.arange(block_count, dtype=jnp.int32)
    peer_onehot = (peer_blocks[:, None] == labels[None, :]).astype(jnp.float32)
    own_onehot = (labels == own_block).astype(jnp.float32)
    trace_slots = traces[:, slot_rows]
    receive_index = flip_index[inverse]

    def to_peers(values):
        return values[:, slot_rows]

    def from_peers(values):
        return values[:, inverse]

    gap_peers = to_peers(local_gap)
    got_traces = lax.all_to_all(trace_slots, "sub", split_axis=1, concat_axis=1, tiled=True)
    got_gap = lax.all_to_all(gap_peers, "sub", split_axis=1, concat_axis=1, tiled=True)
    partner_traces = got_traces[:, flip_index]
    residual = local_gap - got_gap[:, receive_index]
    own_gram = jnp.dot(traces, traces.T, precision=HIGHEST)
    paired = (trace_slots[:, None, :] * partner_traces[None, :, :]).reshape(
        MODES, MODES, peer_count, per_peer
    )
    cross_terms = jnp.sum(paired, axis=3)
    cross_blocks = jnp.einsum("klq,qb->kbl", cross_terms, peer_onehot, precision=HIGHEST)
    own_blocks = own_gram[:, None, :] * own_onehot[None, :, None]
    row_term = 2.0 * (own_blocks - cross_blocks).reshape(MODES, coarse)
    gram_term = (own_onehot[:, None, None] * row_term[None]).reshape(coarse, coarse)

    def coarse_term(values):
        own_part = 2.0 * jnp.dot(values, traces.T, precision=HIGHEST)
        return (own_part[:, None, :] * own_onehot[None, :, None]).reshape(load_cases, coarse)

    def expand(amounts):
        grouped = amounts.reshape(load_cases, block_count, MODES)
        own_amounts = lax.dynamic_index_in_dim(grouped, own_block, 1, keepdims=False)
        own_part = jnp.dot(own_amounts, traces, precision=HIGHEST)
        peer_amounts = jnp.einsum("qb,rbk->rkq", peer_onehot, grouped, precision=HIGHEST)
        spread = jnp.repeat(peer_amounts, per_peer, axis=2)
        peer_part = jnp.sum(spread * partner_traces[None, :, :], axis=1)
        return own_part - from_peers(peer_part)

    squares = jnp.sum(residual * residual, axis=1)
    gram_matrix, coarse_res, norm_res = lax.psum(
        (gram_term, coarse_term(residual), squares), ("sub", "rep")
    )
    factor = jnp.linalg.cholesky(gram_matrix)

    def solve_coarse(right):
        return jax.scipy.linalg.cho_solve((factor, True), right.T).T

    amplitudes = solve_coarse(coarse_res)
    projected = residual - expand(amplitudes)
    inner_sum = norm_res - jnp.sum(amplitudes * coarse_res, axis=1)
    direction = projected
    multipliers = jnp.zeros_like(residual)
    for iteration in range(ITERS):
        product = lax.dot_general(
            direction.astype(jnp.bfloat16),
            operator,
            (((1,), (1,)), ((), ())),
            preferred_element_type=jnp.float32,
        )
        got_product = lax.all_to_all(
            to_peers(product), "sub", split_axis=1, concat_axis=1, tiled=True
        )
        image_jump = product - got_product[:, receive_index]
        coarse_jump, jump_squares, residual_cross, curvature = lax.psum(
            (
                coarse_term(image_jump),
                jnp.sum(image_jump * image_jump, axis=1),
                jnp.sum(residual * image_jump, axis=1),
                jnp.sum(direction * image_jump, axis=1),
            ),
            ("sub", "rep"),
        )
        step_size = inner_sum / curvature
        multipliers = multipliers + step_size[:, None] * direction
        residual = residual - step_size[:, None] * image_jump
        coarse_res = coarse_res - step_size[:, None] * coarse_jump
        norm_res = (
            norm_res - 2.0 * step_size * residual_cross + step_size * step_size * jump_squares
        )
        amplitudes = solve_coarse(coarse_res)
        if iteration + 1 < ITERS:
            projected = residual - expand(amplitudes)
            renewed = norm_res - jnp.sum(amplitudes * coarse_res, axis=1)
            direction = projected + (renewed / inner_sum)[:, None] * direction
            inner_sum = renewed
    return (multipliers, amplitudes)


def fits(mesh, dual_ops, mode_block, local_gap):
    peers, planes = mesh.shape["sub"], mesh.shape["rep"]
    powers = all(size & (size - 1) == 0 for size in (peers, planes))
    whole = dual_ops.shape[1] % (128 * peers) == 0 and local_gap.shape[0] % 16 == 0
    return powers and whole and 8 * GROUP * (mode_block.shape[0] // AGG_SUBS) == 128


def solution(mesh):
    placed = (
        P(("sub", "rep"), None, None),
        P(("sub", "rep"), None, None),
        P(("sub", "rep"), None),
        P(),
        P(None, ("sub", "rep")),
    )

    def run(dual_ops, mode_traces, route, mode_block, local_gap):
        body = fused_body if fits(mesh, dual_ops, mode_block, local_gap) else general_body
        return jax.shard_map(
            body, mesh=mesh, in_specs=placed, out_specs=(P(None, ("sub", "rep")), P()), check_vma=False
        )(dual_ops, mode_traces, route, mode_block, local_gap)

    return run
```

profile of v0, /device:TPU:0, one launch (start us, length us, event | category | flops | bytes accessed | tf_op | source)
XLA Modules:
  0.0 38.1 jit_solution(2908840104388230302)
XLA Ops:
  0.6 1.8 %place.1 = (bf16[1024,768]{1,0:T(8,128)(2,1)S(1)}, f32[40,1024]{1,0:T(8,128)S(1)}, bf16[1,1024,1024]{2,1,0:T(8,128)(2,1)S(1)}, s32[1,1024]{1,0:T(1,128)S(1)}, f3...) custom-call(s32[1,1024]{1,0:T(1,128)} %route_hbm.1, s32[1,32]{1,0:T(1,128)} %bitcast.4, ...), custom_call_target="tpu_custom_call" | custom-call | bytes 1048576 | tf_op jit(solution)/shard_map/place/pallas_call | solution.py:408
  2.4 3.4 %collective-permute-start = (f32[80,128]{1,0:T(8,128)S(1)}, f32[80,128]{1,0:T(8,128)S(1)}, u32[]{:S(2)}, u32[]{:S(2)}) collective-permute-start(f32[80,128]{1,0:T(8,128)S(1)} %get-tuple-element.48.refs_0_), channel_id=1, source_target_pairs={{0,28},{1,29},{2,30},{3,31},{4,24},{5,25},{6,26},{7,27},{8,20},{9,... | collective-permute-start | bytes 122888 | tf_op jit(solution)/shard_map/ppermute | solution.py:360
  5.8 0.8 %collective-permute-start.1 = (f32[80,128]{1,0:T(8,128)S(1)}, f32[80,128]{1,0:T(8,128)S(1)}, u32[]{:S(2)}, u32[]{:S(2)}) collective-permute-start(f32[80,128]{1,0:T(8,128)S(1)} %get-tuple-element.49.refs_1_), channel_id=1, source_target_pairs={{0,20},{1,21},{2,22},{3,23},{4,16},{5,17},{6,18},{7,19},{8,28},{9,... | collective-permute-start | bytes 122888 | tf_op jit(solution)/shard_map/ppermute | solution.py:360
  6.6 0.1 collective-permute-start.2
  6.7 3.0 %ready.1 = (bf16[1024,384]{1,0:T(8,128)(2,1)S(1)}, bf16[2,1024,512]{2,1,0:T(8,128)(2,1)S(1)}, bf16[2,1024,512]{2,1,0:T(8,128)(2,1)S(1)}, f32[40,128]{1,0:T(8,128...) custom-call(s32[1,1024]{1,0:T(1,128)S(1)} %get-tuple-element.39.route_ref, ...), custom_call_target="tpu_custom_call" | custom-call | flops 2147483648 | bytes 1048576 | tf_op jit(solution)/shard_map/ready/pallas_call | solution.py:423
  9.7 0.0 collective-permute-done.refs_3_
  9.7 0.0 collective-permute-done.1.refs_4_
  9.7 0.6 %collective-permute-done.2.refs_5_ = f32[80,128]{1,0:T(8,128)S(1)} collective-permute-done((f32[80,128]{1,0:T(8,128)S(1)}, f32[80,128]{1,0:T(8,128)S(1)}, u32[]{:S(2)}, u32[]{:S(2)}) %collective-permute-start.2) | collective-permute-done | bytes 40992 | tf_op jit(solution)/shard_map/ppermute | solution.py:360
  10.4 0.2 collective-permute-start.3
  10.6 0.4 %first_half.1 = (f32[48,512]{1,0:T(8,128)S(1)}, f32[48,1024]{1,0:T(8,128)S(1)}) custom-call(bf16[2,1024,512]{2,1,0:T(8,128)(2,1)S(1)} %get-tuple-element.44.placed_ref, f32[40,128]{1,0:T(8,128)S(1)} %get-tuple-element.46.stay_ref, f32[40,128]{1,0:T(8,128)S(1)} %get-tuple-element.47.back_ref, f32[80,128]{1,0:T(8,128)S(1)} %get-tuple-element.48.refs_0_, ...), custom_call_target="tpu_custom_call" | custom-call | flops 100663296 | bytes 1048576 | tf_op jit(solution)/shard_map/first_half/pallas_call | solution.py:432
  11.0 0.7 %collective-permute-done.3.got_ref = f32[160,128]{1,0:T(8,128)S(1)} collective-permute-done((f32[160,128]{1,0:T(8,128)S(1)}, f32[160,128]{1,0:T(8,128)S(1)}, u32[]{:S(2)}, u32[]{:S(2)}) %collective-permute-start.3) | collective-permute-done | bytes 81952 | tf_op jit(solution)/shard_map/ppermute | solution.py:360
  11.7 0.8 %first.1 = (f32[48,512]{1,0:T(8,128)S(1)}, f32[48,1024]{1,0:T(8,128)S(1)}, f32[96,128]{1,0:T(8,128)S(1)}, f32[96,128]{1,0:T(8,128)S(1)}, f32[96,128]{1,0:T(8,128)S(1)}) custom-call(bf16[1024,768]{1,0:T(8,128)(2,1)S(1)} %get-tuple-element.40.far_ref, bf16[2,1024,512]{2,1,0:T(8,128)(2,1)S(1)} %get-tuple-element.44.placed_ref, ...), custom_call_target="tpu_custom_call" | custom-call | bytes 1048576 | tf_op jit(solution)/shard_map/first/pallas_call | solution.py:435
  12.5 2.0 %collective-permute-start.4 = (f32[96,128]{1,0:T(8,128)S(1)}, f32[96,128]{1,0:T(8,128)S(1)}, u32[]{:S(2)}, u32[]{:S(2)}) collective-permute-start(f32[96,128]{1,0:T(8,128)S(1)} %get-tuple-element.59.refs_0_), channel_id=1, source_target_pairs={{0,28},{1,29},{2,30},{3,31},{4,24},{5,25},{6,26},{7,27},{8,20},{9,... | collective-permute-start | bytes 147464 | tf_op jit(solution)/shard_map/ppermute | solution.py:360
  14.5 0.3 collective-permute-start.5
  14.8 0.8 %collective-permute-start.6 = (f32[96,128]{1,0:T(8,128)S(1)}, f32[96,128]{1,0:T(8,128)S(1)}, u32[]{:S(2)}, u32[]{:S(2)}) collective-permute-start(f32[96,128]{1,0:T(8,128)S(1)} %get-tuple-element.61.refs_2_), channel_id=1, source_target_pairs={{0,12},{1,13},{2,14},{3,15},{4,8},{5,9},{6,10},{7,11},{8,4},{9,5},... | collective-permute-start | bytes 147464 | tf_op jit(solution)/shard_map/ppermute | solution.py:360
  15.5 1.2 %middle.1 = (f32[48,1024]{1,0:T(8,128)S(1)}, f32[48,128]{1,0:T(8,128)S(1)}, f32[48,128]{1,0:T(8,128)S(1)}, f32[48,128]{1,0:T(8,128)S(1)}, f32[48,128]{1,0:T(8,128)S(1)}) custom-call(bf16[1024,384]{1,0:T(8,128)(2,1)S(1)} %get-tuple-element.45.edge_ref, bf16[2,1024,512]{2,1,0:T(8,128)(2,1)S(1)} %get-tuple-element.43.slots_ref, ...), custom_call_target="tpu_custom_call" | custom-call | flops 201326592 | bytes 1048576 | tf_op jit(solution)/shard_map/middle/pallas_call | solution.py:439
  16.7 0.4 %collective-permute-done.4.refs_3_ = f32[96,128]{1,0:T(8,128)S(1)} collective-permute-done((f32[96,128]{1,0:T(8,128)S(1)}, f32[96,128]{1,0:T(8,128)S(1)}, u32[]{:S(2)}, u32[]{:S(2)}) %collective-permute-start.4) | collective-permute-done | bytes 49184 | tf_op jit(solution)/shard_map/ppermute | solution.py:360
  17.2 1.1 %collective-permute-done.5.refs_4_ = f32[96,128]{1,0:T(8,128)S(1)} collective-permute-done((f32[96,128]{1,0:T(8,128)S(1)}, f32[96,128]{1,0:T(8,128)S(1)}, u32[]{:S(2)}, u32[]{:S(2)}) %collective-permute-start.5) | collective-permute-done | bytes 49184 | tf_op jit(solution)/shard_map/ppermute | solution.py:360
  18.2 0.1 collective-permute-done.6.refs_5_
  18.3 0.4 %collective-permute-start.7 = (f32[192,128]{1,0:T(8,128)S(1)}, f32[192,128]{1,0:T(8,128)S(1)}, u32[]{:S(2)}, u32[]{:S(2)}) collective-permute-start(f32[192,128]{1,0:T(8,128)S(1)} %pad_maximum_fusion), channel_id=1, source_target_pairs={{0,4},{1,5},{2,6},{3,7},{4,0},{5,1},{6,2},{7,3},{8,12},{9,13},{10,... | collective-permute-start | bytes 294920 | tf_op jit(solution)/shard_map/ppermute | solution.py:360
  18.7 0.7 %second_half.1 = (f32[48,1024]{1,0:T(8,128)S(1)}, f32[48,1024]{1,0:T(8,128)S(1)}) custom-call(bf16[2,1024,512]{2,1,0:T(8,128)(2,1)S(1)} %get-tuple-element.43.slots_ref, bf16[2,1024,512]{2,1,0:T(8,128)(2,1)S(1)} %get-tuple-element.44.placed_ref, f32[48,128]{1,0:T(8,128)S(1)} %get-tuple-element.57.stay_ref, f32[48,128]{1,0:T(8,128)S(1)} %get-tuple-element.58.back_ref, ...), custom_call_target="tpu_custom_call" | custom-call | flops 201326592 | bytes 1048576 | tf_op jit(solution)/shard_map/second_half/pallas_call | solution.py:443
  19.5 0.2 collective-permute-done.7.got_ref
  19.7 1.2 %second.1 = (f32[48,1024]{1,0:T(8,128)S(1)}, f32[48,128]{1,0:T(8,128)S(1)}) custom-call(bf16[2,1024,512]{2,1,0:T(8,128)(2,1)S(1)} %get-tuple-element.43.slots_ref, bf16[2,1024,512]{2,1,0:T(8,128)(2,1)S(1)} %get-tuple-element.44.placed_ref, f32[48,1024]{1,0:T(8,128)S(1)} %get-tuple-element.56.basis_ref, f32[48,1024]{1,0:T(8,128)S(1)} %get-tuple-element.62.half_jump_ref, ...), custom_call_target="tpu_custom_call" | custom-call | bytes 1048576 | tf_op jit(solution)/shard_map/second/pallas_call | solution.py:446
  20.9 0.4 %collective-permute-start.8 = (f32[48,128]{1,0:T(8,128)S(1)}, f32[48,128]{1,0:T(8,128)S(1)}, u32[]{:S(2)}, u32[]{:S(2)}) collective-permute-start(f32[48,128]{1,0:T(8,128)S(1)} %get-tuple-element.66.refs_1_), channel_id=1, source_target_pairs={{0,4},{1,5},{2,6},{3,7},{4,0},{5,1},{6,2},{7,3},{8,12},{9,13},{10,... | collective-permute-start | bytes 73736 | tf_op jit(solution)/shard_map/ppermute | solution.py:360
  21.3 0.8 %collective-permute-done.8.refs_0_ = f32[48,128]{1,0:T(8,128)S(1)} collective-permute-done((f32[48,128]{1,0:T(8,128)S(1)}, f32[48,128]{1,0:T(8,128)S(1)}, u32[]{:S(2)}, u32[]{:S(2)}) %collective-permute-start.8) | collective-permute-done | bytes 24608 | tf_op jit(solution)/shard_map/ppermute | solution.py:360
  22.2 2.0 %collective-permute-start.10 = (f32[48,128]{1,0:T(8,128)S(1)}, f32[48,128]{1,0:T(8,128)S(1)}, u32[]{:S(2)}, u32[]{:S(2)}) collective-permute-start(f32[48,128]{1,0:T(8,128)S(1)} %get-tuple-element.68), channel_id=1, source_target_pairs={{0,28},{1,29},{2,30},{3,31},{4,24},{5,25},{6,26},{7,27},{8,20},{9,... | collective-permute-start | bytes 73736 | tf_op jit(solution)/shard_map/ppermute | solution.py:360
  24.2 0.5 %collective-permute-start.11 = (f32[48,128]{1,0:T(8,128)S(1)}, f32[48,128]{1,0:T(8,128)S(1)}, u32[]{:S(2)}, u32[]{:S(2)}) collective-permute-start(f32[48,128]{1,0:T(8,128)S(1)} %get-tuple-element.69), channel_id=1, source_target_pairs={{0,20},{1,21},{2,22},{3,23},{4,16},{5,17},{6,18},{7,19},{8,28},{9,... | collective-permute-start | bytes 73736 | tf_op jit(solution)/shard_map/ppermute | solution.py:360
  24.7 0.7 %collective-permute-start.9 = (f32[48,128]{1,0:T(8,128)S(1)}, f32[48,128]{1,0:T(8,128)S(1)}, u32[]{:S(2)}, u32[]{:S(2)}) collective-permute-start(f32[48,128]{1,0:T(8,128)S(1)} %get-tuple-element.67.refs_3_), channel_id=1, source_target_pairs={{0,12},{1,13},{2,14},{3,15},{4,8},{5,9},{6,10},{7,11},{8,4},{9,5},... | collective-permute-start | bytes 73736 | tf_op jit(solution)/shard_map/ppermute | solution.py:360
  25.4 1.0 %collective-permute-done.10.refs_1_ = f32[48,128]{1,0:T(8,128)S(1)} collective-permute-done((f32[48,128]{1,0:T(8,128)S(1)}, f32[48,128]{1,0:T(8,128)S(1)}, u32[]{:S(2)}, u32[]{:S(2)}) %collective-permute-start.10) | collective-permute-done | bytes 24608 | tf_op jit(solution)/shard_map/ppermute | solution.py:360
  26.4 1.0 %collective-permute-done.11.refs_2_ = f32[48,128]{1,0:T(8,128)S(1)} collective-permute-done((f32[48,128]{1,0:T(8,128)S(1)}, f32[48,128]{1,0:T(8,128)S(1)}, u32[]{:S(2)}, u32[]{:S(2)}) %collective-permute-start.11) | collective-permute-done | bytes 24608 | tf_op jit(solution)/shard_map/ppermute | solution.py:360
  27.4 0.5 %collective-permute-done.9.refs_0_ = f32[48,128]{1,0:T(8,128)S(1)} collective-permute-done((f32[48,128]{1,0:T(8,128)S(1)}, f32[48,128]{1,0:T(8,128)S(1)}, u32[]{:S(2)}, u32[]{:S(2)}) %collective-permute-start.9) | collective-permute-done | bytes 24608 | tf_op jit(solution)/shard_map/ppermute | solution.py:360
  27.9 3.3 %collective-permute-start.12 = (f32[48,128]{1,0:T(8,128)S(1)}, f32[48,128]{1,0:T(8,128)S(1)}, u32[]{:S(2)}, u32[]{:S(2)}) collective-permute-start(f32[48,128]{1,0:T(8,128)S(1)} %get-tuple-element.70.refs_3_), channel_id=1, source_target_pairs={{0,7},{1,6},{2,5},{3,4},{4,3},{5,2},{6,1},{7,0},{8,15},{9,14},{10,... | collective-permute-start | bytes 73736 | tf_op jit(solution)/shard_map/ppermute | solution.py:360
  31.3 0.0 collective-permute-start.13
  31.3 0.6 %collective-permute-start.14 = (f32[48,128]{1,0:T(8,128)S(1)}, f32[48,128]{1,0:T(8,128)S(1)}, u32[]{:S(2)}, u32[]{:S(2)}) collective-permute-start(f32[48,128]{1,0:T(8,128)S(1)} %get-tuple-element.72), channel_id=1, source_target_pairs={{0,5},{1,4},{2,7},{3,6},{4,1},{5,0},{6,3},{7,2},{8,13},{9,12},{10,... | collective-permute-start | bytes 73736 | tf_op jit(solution)/shard_map/ppermute | solution.py:360
  31.9 1.2 %collective-permute-done.12.refs_0_ = f32[48,128]{1,0:T(8,128)S(1)} collective-permute-done((f32[48,128]{1,0:T(8,128)S(1)}, f32[48,128]{1,0:T(8,128)S(1)}, u32[]{:S(2)}, u32[]{:S(2)}) %collective-permute-start.12) | collective-permute-done | bytes 24608 | tf_op jit(solution)/shard_map/ppermute | solution.py:360
  33.1 2.4 %collective-permute-done.13.refs_1_ = f32[48,128]{1,0:T(8,128)S(1)} collective-permute-done((f32[48,128]{1,0:T(8,128)S(1)}, f32[48,128]{1,0:T(8,128)S(1)}, u32[]{:S(2)}, u32[]{:S(2)}) %collective-permute-start.13) | collective-permute-done | bytes 24608 | tf_op jit(solution)/shard_map/ppermute | solution.py:360
  35.4 0.0 collective-permute-done.14.refs_2_
  35.5 2.6 %final.1 = (f32[32,1024]{1,0:T(8,128)}, f32[12,32]{1,0:T(8,128)}) custom-call(f32[48,128]{1,0:T(8,128)S(1)} %sum.5.terms_ref, f32[48,1024]{1,0:T(8,128)S(1)} %get-tuple-element.56.basis_ref, f32[48,1024]{1,0:T(8,128)S(1)} %get-tuple-element.73.jump_ref), custom_call_target="tpu_custom_call" | custom-call | bytes 1048576 | tf_op jit(solution)/shard_map/final/pallas_call | solution.py:449
  (11 shorter events, 0.1 us)
Async XLA Ops:
  2.4 7.3 %collective-permute-start = (f32[80,128]{1,0:T(8,128)S(1)}, f32[80,128]{1,0:T(8,128)S(1)}, u32[]{:S(2)}, u32[]{:S(2)}) collective-permute-start(f32[80,128]{1,0:T(8,128)S(1)} %get-tuple-element.48.refs_0_), channel_id=1, source_target_pairs={{0,28},{1,29},{2,30},{3,31},{4,24},{5,25},{6,26},{7,27},{8,20},{9,... | collective-permute-start | bytes 122888 | tf_op jit(solution)/shard_map/ppermute | solution.py:360
  5.8 3.9 %collective-permute-start.1 = (f32[80,128]{1,0:T(8,128)S(1)}, f32[80,128]{1,0:T(8,128)S(1)}, u32[]{:S(2)}, u32[]{:S(2)}) collective-permute-start(f32[80,128]{1,0:T(8,128)S(1)} %get-tuple-element.49.refs_1_), channel_id=1, source_target_pairs={{0,20},{1,21},{2,22},{3,23},{4,16},{5,17},{6,18},{7,19},{8,28},{9,... | collective-permute-start | bytes 122888 | tf_op jit(solution)/shard_map/ppermute | solution.py:360
  6.6 3.8 %collective-permute-start.2 = (f32[80,128]{1,0:T(8,128)S(1)}, f32[80,128]{1,0:T(8,128)S(1)}, u32[]{:S(2)}, u32[]{:S(2)}) collective-permute-start(f32[80,128]{1,0:T(8,128)S(1)} %get-tuple-element.50.refs_2_), channel_id=1, source_target_pairs={{0,12},{1,13},{2,14},{3,15},{4,8},{5,9},{6,10},{7,11},{8,4},{9,5},... | collective-permute-start | bytes 122888 | tf_op jit(solution)/shard_map/ppermute | solution.py:360
  10.4 1.3 %collective-permute-start.3 = (f32[160,128]{1,0:T(8,128)S(1)}, f32[160,128]{1,0:T(8,128)S(1)}, u32[]{:S(2)}, u32[]{:S(2)}) collective-permute-start(f32[160,128]{1,0:T(8,128)S(1)} %pad_maximum_fusion.1), channel_id=1, source_target_pairs={{0,4},{1,5},{2,6},{3,7},{4,0},{5,1},{6,2},{7,3},{8,12},{9,13},{10,... | collective-permute-start | bytes 245768 | tf_op jit(solution)/shard_map/ppermute | solution.py:360
  12.5 4.6 %collective-permute-start.4 = (f32[96,128]{1,0:T(8,128)S(1)}, f32[96,128]{1,0:T(8,128)S(1)}, u32[]{:S(2)}, u32[]{:S(2)}) collective-permute-start(f32[96,128]{1,0:T(8,128)S(1)} %get-tuple-element.59.refs_0_), channel_id=1, source_target_pairs={{0,28},{1,29},{2,30},{3,31},{4,24},{5,25},{6,26},{7,27},{8,20},{9,... | collective-permute-start | bytes 147464 | tf_op jit(solution)/shard_map/ppermute | solution.py:360
  14.5 3.7 %collective-permute-start.5 = (f32[96,128]{1,0:T(8,128)S(1)}, f32[96,128]{1,0:T(8,128)S(1)}, u32[]{:S(2)}, u32[]{:S(2)}) collective-permute-start(f32[96,128]{1,0:T(8,128)S(1)} %get-tuple-element.60.refs_1_), channel_id=1, source_target_pairs={{0,20},{1,21},{2,22},{3,23},{4,16},{5,17},{6,18},{7,19},{8,28},{9,... | collective-permute-start | bytes 147464 | tf_op jit(solution)/shard_map/ppermute | solution.py:360
  14.8 3.5 %collective-permute-start.6 = (f32[96,128]{1,0:T(8,128)S(1)}, f32[96,128]{1,0:T(8,128)S(1)}, u32[]{:S(2)}, u32[]{:S(2)}) collective-permute-start(f32[96,128]{1,0:T(8,128)S(1)} %get-tuple-element.61.refs_2_), channel_id=1, source_target_pairs={{0,12},{1,13},{2,14},{3,15},{4,8},{5,9},{6,10},{7,11},{8,4},{9,5},... | collective-permute-start | bytes 147464 | tf_op jit(solution)/shard_map/ppermute | solution.py:360
  18.3 1.4 %collective-permute-start.7 = (f32[192,128]{1,0:T(8,128)S(1)}, f32[192,128]{1,0:T(8,128)S(1)}, u32[]{:S(2)}, u32[]{:S(2)}) collective-permute-start(f32[192,128]{1,0:T(8,128)S(1)} %pad_maximum_fusion), channel_id=1, source_target_pairs={{0,4},{1,5},{2,6},{3,7},{4,0},{5,1},{6,2},{7,3},{8,12},{9,13},{10,... | collective-permute-start | bytes 294920 | tf_op jit(solution)/shard_map/ppermute | solution.py:360
  20.9 1.3 %collective-permute-start.8 = (f32[48,128]{1,0:T(8,128)S(1)}, f32[48,128]{1,0:T(8,128)S(1)}, u32[]{:S(2)}, u32[]{:S(2)}) collective-permute-start(f32[48,128]{1,0:T(8,128)S(1)} %get-tuple-element.66.refs_1_), channel_id=1, source_target_pairs={{0,4},{1,5},{2,6},{3,7},{4,0},{5,1},{6,2},{7,3},{8,12},{9,13},{10,... | collective-permute-start | bytes 73736 | tf_op jit(solution)/shard_map/ppermute | solution.py:360
  22.2 4.2 %collective-permute-start.10 = (f32[48,128]{1,0:T(8,128)S(1)}, f32[48,128]{1,0:T(8,128)S(1)}, u32[]{:S(2)}, u32[]{:S(2)}) collective-permute-start(f32[48,128]{1,0:T(8,128)S(1)} %get-tuple-element.68), channel_id=1, source_target_pairs={{0,28},{1,29},{2,30},{3,31},{4,24},{5,25},{6,26},{7,27},{8,20},{9,... | collective-permute-start | bytes 73736 | tf_op jit(solution)/shard_map/ppermute | solution.py:360
  24.2 3.3 %collective-permute-start.11 = (f32[48,128]{1,0:T(8,128)S(1)}, f32[48,128]{1,0:T(8,128)S(1)}, u32[]{:S(2)}, u32[]{:S(2)}) collective-permute-start(f32[48,128]{1,0:T(8,128)S(1)} %get-tuple-element.69), channel_id=1, source_target_pairs={{0,20},{1,21},{2,22},{3,23},{4,16},{5,17},{6,18},{7,19},{8,28},{9,... | collective-permute-start | bytes 73736 | tf_op jit(solution)/shard_map/ppermute | solution.py:360
  24.7 3.3 %collective-permute-start.9 = (f32[48,128]{1,0:T(8,128)S(1)}, f32[48,128]{1,0:T(8,128)S(1)}, u32[]{:S(2)}, u32[]{:S(2)}) collective-permute-start(f32[48,128]{1,0:T(8,128)S(1)} %get-tuple-element.67.refs_3_), channel_id=1, source_target_pairs={{0,12},{1,13},{2,14},{3,15},{4,8},{5,9},{6,10},{7,11},{8,4},{9,5},... | collective-permute-start | bytes 73736 | tf_op jit(solution)/shard_map/ppermute | solution.py:360
  27.9 5.1 %collective-permute-start.12 = (f32[48,128]{1,0:T(8,128)S(1)}, f32[48,128]{1,0:T(8,128)S(1)}, u32[]{:S(2)}, u32[]{:S(2)}) collective-permute-start(f32[48,128]{1,0:T(8,128)S(1)} %get-tuple-element.70.refs_3_), channel_id=1, source_target_pairs={{0,7},{1,6},{2,5},{3,4},{4,3},{5,2},{6,1},{7,0},{8,15},{9,14},{10,... | collective-permute-start | bytes 73736 | tf_op jit(solution)/shard_map/ppermute | solution.py:360
  31.3 4.2 %collective-permute-start.13 = (f32[48,128]{1,0:T(8,128)S(1)}, f32[48,128]{1,0:T(8,128)S(1)}, u32[]{:S(2)}, u32[]{:S(2)}) collective-permute-start(f32[48,128]{1,0:T(8,128)S(1)} %get-tuple-element.71), channel_id=1, source_target_pairs={{0,6},{1,7},{2,4},{3,5},{4,2},{5,3},{6,0},{7,1},{8,14},{9,15},{10,... | collective-permute-start | bytes 73736 | tf_op jit(solution)/shard_map/ppermute | solution.py:360
  31.3 4.2 %collective-permute-start.14 = (f32[48,128]{1,0:T(8,128)S(1)}, f32[48,128]{1,0:T(8,128)S(1)}, u32[]{:S(2)}, u32[]{:S(2)}) collective-permute-start(f32[48,128]{1,0:T(8,128)S(1)} %get-tuple-element.72), channel_id=1, source_target_pairs={{0,5},{1,4},{2,7},{3,6},{4,1},{5,0},{6,3},{7,2},{8,13},{9,12},{10,... | collective-permute-start | bytes 73736 | tf_op jit(solution)/shard_map/ppermute | solution.py:360
where the time goes:
time: 38.2 us; the launch traced here: 38.1 us
  starting transfers between devices  15.5 us (41%)
  Pallas kernels  11.7 us (31%)
  waiting for transfers between devices  10 us (26%)
  between operations  0.75 us (2%)
    ppermute x15, starting transfers between devices, permute(): lax.ppermute(values, ('sub', 'rep'), [(at, at ^ offset) for at in range(p...  15.5 us
    ppermute x15, waiting for transfers between devices, permute(): lax.ppermute(values, ('sub', 'rep'), [(at, at ^ offset) for at in range(p...  10 us
    pallas_call x1, Pallas kernels, fused_body(): call(ready_kernel, [((rows, 3 * per_peer), jnp.bfloat16), halves, halves,...  2.96 us
    pallas_call x1, Pallas kernels, fused_body(): call(final_kernel, [((loads, rows), f32), ((MODES * groups, loads), f32)]...  2.6 us
    pallas_call x1, Pallas kernels, fused_body(): call(place_kernel, [((rows, rows - 2 * per_peer), jnp.bfloat16), ((short,...  1.77 us
    pallas_call x1, Pallas kernels, fused_body(): call(second_kernel, [tall, wide], [VMEM] * (8 + len(got)), 'second')  1.22 us
    pallas_call x1, Pallas kernels, fused_body(): call(middle_kernel, [tall, wide, *singles(height)], [VMEM] * 5, 'middle',...  1.2 us
    pallas_call x1, Pallas kernels, fused_body(): call(first_kernel, [half, tall, *pairs(height)], [VMEM] * (5 + len(send))...  0.79 us
  transfers between devices with their start and end apart: 15, of which 12 were waited for; matrix products, arithmetic and copies ran while one was open for 0% of the time, Pallas kernels for 14%

commit v1 on v0

--- a/solution.py
+++ b/solution.py
@@ -38,11 +38,13 @@
 def send_far(values, far_ref, *pair_refs):
     height = values.shape[0]
     per_peer = pair_refs[0].shape[1]
-    slots = split_dot(values, far_ref[...], NN)
-    for at, ref in enumerate(reversed(pair_refs)):
-        start = 2 * at * per_peer
-        ref[:height] = slots[:, start + per_peer : start + 2 * per_peer]
-        ref[height:] = slots[:, start : start + per_peer]
+    values = split(values)
+    for at, ref in enumerate(pair_refs):
+        columns = far_ref[:, 2 * at * per_peer : (2 * at + 2) * per_peer]
+        slots = jnp.dot(values, columns, preferred_element_type=jnp.float32)
+        slots = slots[:height] + slots[height:]
+        ref[:height] = slots[:, :per_peer]
+        ref[height:] = slots[:, per_peer:]
 
 
 def send_near(values, edge_ref, near_ref, back_ref, stay_ref):
@@ -100,14 +102,18 @@
             )
         )
     ]
+
+    def build(at):
+        peer = own_index ^ (peers - 1 - at)
+        far_ref[:, at * per_peer : (at + 1) * per_peer] = one_hot(route_ref, peer, per_peer)
+
     for copy in copies:
         copy.start()
     own_index = lax.axis_index("sub")
     device = own_index * lax.axis_size("rep") + lax.axis_index("rep")
     copies[0].wait()
-    for offset in range(2, peers):
-        at = (offset - 2) * per_peer
-        far_ref[:, at : at + per_peer] = one_hot(route_ref, own_index ^ offset, per_peer)
+    for at in range(peers - 4):
+        build(at)
     copies[1].wait()
     copies[2].wait()
     blocks = block_ref[...]
@@ -120,6 +126,8 @@
     values_ref[loads + modes : loads + modes + 1] = label
     values_ref[loads + modes + 1 :] = jnp.zeros((GROUP - modes - 1, rows), jnp.float32)
     copies[3].wait()
+    for at in range(peers - 4, peers - 2):
+        build(at)
     send_far(values_ref[...], far_ref, *pair_refs)
     copies[4].wait()
 
@@ -139,9 +147,9 @@
     reversed_columns = jnp.dot(own_columns, reverse, preferred_element_type=jnp.float32).astype(jnp.bfloat16)
     edge_ref[...] = jnp.concatenate([near_columns, reversed_columns, own_columns], axis=1)
     for at in range(peers // 2 - 1):
-        start = (peers - 4 - 2 * at) * per_peer
-        slots_ref[0, :, at * per_peer : (at + 1) * per_peer] = far_ref[:, start + per_peer : start + 2 * per_peer]
-        slots_ref[1, :, (at + 1) * per_peer : (at + 2) * per_peer] = far_ref[:, start : start + per_peer]
+        start = 2 * at * per_peer
+        slots_ref[0, :, at * per_peer : (at + 1) * per_peer] = far_ref[:, start : start + per_peer]
+        slots_ref[1, :, (at + 1) * per_peer : (at + 2) * per_peer] = far_ref[:, start + per_peer : start + 2 * per_peer]
     slots_ref[0, :, (peers // 2 - 1) * per_peer :] = own_columns
     slots_ref[1, :, :per_peer] = near_columns
     send_near(values_ref[...], edge_ref, near_ref, back_ref, stay_ref)
@@ -253,20 +261,27 @@
 
 def eliminate(work, coarse):
     row = lax.broadcasted_iota(jnp.int32, work.shape, 0)
-    for first in range(coarse):
-        if first % 2 or first % GROUP >= MODES:
-            continue
-        second = first + 1
-        left = jnp.broadcast_to(work[:, first : first + 1], work.shape)
-        right = jnp.broadcast_to(work[:, second : second + 1], work.shape)
-        upper, lower = work[first : first + 1], work[second : second + 1]
-        pivot = 1.0 / left[first : first + 1]
-        ratio = left[second : second + 1] * pivot
-        corner = 1.0 / (right[second : second + 1] - ratio * right[first : first + 1])
-        lower = (lower - ratio * upper) * corner
-        upper = (upper - right[first : first + 1] * lower) * pivot
-        work = work - left * upper - right * lower
-        work = jnp.where(row == first, upper, jnp.where(row == second, lower, work))
+    for start in range(0, coarse, GROUP):
+        pivots = range(start, start + MODES)
+        columns = [jnp.broadcast_to(work[:, pivot : pivot + 1], work.shape) for pivot in pivots]
+        square = [[column[pivot : pivot + 1] for column in columns] for pivot in pivots]
+        rows = [work[pivot : pivot + 1] for pivot in pivots]
+        for at in range(MODES):
+            scale = 1.0 / square[at][at]
+            rows[at] = rows[at] * scale
+            square[at] = [value * scale for value in square[at]]
+            for other in range(MODES):
+                if other != at:
+                    factor = square[other][at]
+                    rows[other] = rows[other] - factor * rows[at]
+                    square[other] = [
+                        value if to <= at else value - factor * square[at][to]
+                        for to, value in enumerate(square[other])
+                    ]
+        for column, solved in zip(columns, rows):
+            work = work - column * solved
+        for pivot, solved in zip(pivots, rows):
+            work = jnp.where(row == pivot, solved, work)
     return work
 
 

time: 38.2 us -> 37.9 us (level)
  no operation moved by 1% of the time
where the time goes in v1:
time: 37.9 us; the launch traced here: 37.7 us
  starting transfers between devices  15.5 us (41%)
  Pallas kernels  11.4 us (30%)
  waiting for transfers between devices  10 us (26%)
  between operations  0.75 us (2%)
    ppermute x15, starting transfers between devices, permute(): lax.ppermute(values, ('sub', 'rep'), [(at, at ^ offset) for at in range(p...  15.5 us
    ppermute x15, waiting for transfers between devices, permute(): lax.ppermute(values, ('sub', 'rep'), [(at, at ^ offset) for at in range(p...  10 us
    pallas_call x1, Pallas kernels, fused_body(): call(ready_kernel, [((rows, 3 * per_peer), jnp.bfloat16), halves, halves,...  2.97 us
    pallas_call x1, Pallas kernels, fused_body(): call(final_kernel, [((loads, rows), f32), ((MODES * groups, loads), f32)]...  2.28 us
    pallas_call x1, Pallas kernels, fused_body(): call(place_kernel, [((rows, rows - 2 * per_peer), jnp.bfloat16), ((short,...  1.77 us
    pallas_call x1, Pallas kernels, fused_body(): call(second_kernel, [tall, wide], [VMEM] * (8 + len(got)), 'second')  1.23 us
    pallas_call x1, Pallas kernels, fused_body(): call(middle_kernel, [tall, wide, *singles(height)], [VMEM] * 5, 'middle',...  1.2 us
    pallas_call x1, Pallas kernels, fused_body(): call(first_kernel, [half, tall, *pairs(height)], [VMEM] * (5 + len(send))...  0.79 us
  transfers between devices with their start and end apart: 15, of which 12 were waited for; matrix products, arithmetic and copies ran while one was open for 0% of the time, Pallas kernels for 14%

profile of v1, /device:TPU:0, one launch (start us, length us, event | category | flops | bytes accessed | tf_op | source)
XLA Modules:
  0.0 37.7 jit_solution(15170500392580696258)
XLA Ops:
  0.6 1.8 %place.1 = (bf16[1024,768]{1,0:T(8,128)(2,1)S(1)}, f32[40,1024]{1,0:T(8,128)S(1)}, bf16[1,1024,1024]{2,1,0:T(8,128)(2,1)S(1)}, s32[1,1024]{1,0:T(1,128)S(1)}, f3...) custom-call(s32[1,1024]{1,0:T(1,128)} %route_hbm.1, s32[1,32]{1,0:T(1,128)} %bitcast.4, ...), custom_call_target="tpu_custom_call" | custom-call | bytes 1048576 | tf_op jit(solution)/shard_map/place/pallas_call | solution.py:423
  2.4 3.4 %collective-permute-start = (f32[80,128]{1,0:T(8,128)S(1)}, f32[80,128]{1,0:T(8,128)S(1)}, u32[]{:S(2)}, u32[]{:S(2)}) collective-permute-start(f32[80,128]{1,0:T(8,128)S(1)} %get-tuple-element.48.refs_0_), channel_id=1, source_target_pairs={{0,28},{1,29},{2,30},{3,31},{4,24},{5,25},{6,26},{7,27},{8,20},{9,... | collective-permute-start | bytes 122888 | tf_op jit(solution)/shard_map/ppermute | solution.py:375
  5.8 0.8 %collective-permute-start.1 = (f32[80,128]{1,0:T(8,128)S(1)}, f32[80,128]{1,0:T(8,128)S(1)}, u32[]{:S(2)}, u32[]{:S(2)}) collective-permute-start(f32[80,128]{1,0:T(8,128)S(1)} %get-tuple-element.49.refs_1_), channel_id=1, source_target_pairs={{0,20},{1,21},{2,22},{3,23},{4,16},{5,17},{6,18},{7,19},{8,28},{9,... | collective-permute-start | bytes 122888 | tf_op jit(solution)/shard_map/ppermute | solution.py:375
  6.6 0.1 collective-permute-start.2
  6.7 3.0 %ready.1 = (bf16[1024,384]{1,0:T(8,128)(2,1)S(1)}, bf16[2,1024,512]{2,1,0:T(8,128)(2,1)S(1)}, bf16[2,1024,512]{2,1,0:T(8,128)(2,1)S(1)}, f32[40,128]{1,0:T(8,128...) custom-call(s32[1,1024]{1,0:T(1,128)S(1)} %get-tuple-element.39.route_ref, ...), custom_call_target="tpu_custom_call" | custom-call | flops 2147483648 | bytes 1048576 | tf_op jit(solution)/shard_map/ready/pallas_call | solution.py:438
  9.7 0.0 collective-permute-done.refs_3_
  9.7 0.0 collective-permute-done.1.refs_4_
  9.7 0.6 %collective-permute-done.2.refs_5_ = f32[80,128]{1,0:T(8,128)S(1)} collective-permute-done((f32[80,128]{1,0:T(8,128)S(1)}, f32[80,128]{1,0:T(8,128)S(1)}, u32[]{:S(2)}, u32[]{:S(2)}) %collective-permute-start.2) | collective-permute-done | bytes 40992 | tf_op jit(solution)/shard_map/ppermute | solution.py:375
  10.4 0.2 collective-permute-start.3
  10.6 0.4 %first_half.1 = (f32[48,512]{1,0:T(8,128)S(1)}, f32[48,1024]{1,0:T(8,128)S(1)}) custom-call(bf16[2,1024,512]{2,1,0:T(8,128)(2,1)S(1)} %get-tuple-element.44.placed_ref, f32[40,128]{1,0:T(8,128)S(1)} %get-tuple-element.46.stay_ref, f32[40,128]{1,0:T(8,128)S(1)} %get-tuple-element.47.back_ref, f32[80,128]{1,0:T(8,128)S(1)} %get-tuple-element.48.refs_0_, ...), custom_call_target="tpu_custom_call" | custom-call | flops 100663296 | bytes 1048576 | tf_op jit(solution)/shard_map/first_half/pallas_call | solution.py:447
  11.0 0.7 %collective-permute-done.3.got_ref = f32[160,128]{1,0:T(8,128)S(1)} collective-permute-done((f32[160,128]{1,0:T(8,128)S(1)}, f32[160,128]{1,0:T(8,128)S(1)}, u32[]{:S(2)}, u32[]{:S(2)}) %collective-permute-start.3) | collective-permute-done | bytes 81952 | tf_op jit(solution)/shard_map/ppermute | solution.py:375
  11.7 0.8 %first.1 = (f32[48,512]{1,0:T(8,128)S(1)}, f32[48,1024]{1,0:T(8,128)S(1)}, f32[96,128]{1,0:T(8,128)S(1)}, f32[96,128]{1,0:T(8,128)S(1)}, f32[96,128]{1,0:T(8,128)S(1)}) custom-call(bf16[1024,768]{1,0:T(8,128)(2,1)S(1)} %get-tuple-element.40.far_ref, bf16[2,1024,512]{2,1,0:T(8,128)(2,1)S(1)} %get-tuple-element.44.placed_ref, ...), custom_call_target="tpu_custom_call" | custom-call | bytes 1048576 | tf_op jit(solution)/shard_map/first/pallas_call | solution.py:450
  12.5 2.0 %collective-permute-start.4 = (f32[96,128]{1,0:T(8,128)S(1)}, f32[96,128]{1,0:T(8,128)S(1)}, u32[]{:S(2)}, u32[]{:S(2)}) collective-permute-start(f32[96,128]{1,0:T(8,128)S(1)} %get-tuple-element.59.refs_0_), channel_id=1, source_target_pairs={{0,28},{1,29},{2,30},{3,31},{4,24},{5,25},{6,26},{7,27},{8,20},{9,... | collective-permute-start | bytes 147464 | tf_op jit(solution)/shard_map/ppermute | solution.py:375
  14.5 0.3 collective-permute-start.5
  14.8 0.8 %collective-permute-start.6 = (f32[96,128]{1,0:T(8,128)S(1)}, f32[96,128]{1,0:T(8,128)S(1)}, u32[]{:S(2)}, u32[]{:S(2)}) collective-permute-start(f32[96,128]{1,0:T(8,128)S(1)} %get-tuple-element.61.refs_2_), channel_id=1, source_target_pairs={{0,12},{1,13},{2,14},{3,15},{4,8},{5,9},{6,10},{7,11},{8,4},{9,5},... | collective-permute-start | bytes 147464 | tf_op jit(solution)/shard_map/ppermute | solution.py:375
  15.5 1.2 %middle.1 = (f32[48,1024]{1,0:T(8,128)S(1)}, f32[48,128]{1,0:T(8,128)S(1)}, f32[48,128]{1,0:T(8,128)S(1)}, f32[48,128]{1,0:T(8,128)S(1)}, f32[48,128]{1,0:T(8,128)S(1)}) custom-call(bf16[1024,384]{1,0:T(8,128)(2,1)S(1)} %get-tuple-element.45.edge_ref, bf16[2,1024,512]{2,1,0:T(8,128)(2,1)S(1)} %get-tuple-element.43.slots_ref, ...), custom_call_target="tpu_custom_call" | custom-call | flops 201326592 | bytes 1048576 | tf_op jit(solution)/shard_map/middle/pallas_call | solution.py:454
  16.7 0.4 %collective-permute-done.4.refs_3_ = f32[96,128]{1,0:T(8,128)S(1)} collective-permute-done((f32[96,128]{1,0:T(8,128)S(1)}, f32[96,128]{1,0:T(8,128)S(1)}, u32[]{:S(2)}, u32[]{:S(2)}) %collective-permute-start.4) | collective-permute-done | bytes 49184 | tf_op jit(solution)/shard_map/ppermute | solution.py:375
  17.2 1.0 %collective-permute-done.5.refs_4_ = f32[96,128]{1,0:T(8,128)S(1)} collective-permute-done((f32[96,128]{1,0:T(8,128)S(1)}, f32[96,128]{1,0:T(8,128)S(1)}, u32[]{:S(2)}, u32[]{:S(2)}) %collective-permute-start.5) | collective-permute-done | bytes 49184 | tf_op jit(solution)/shard_map/ppermute | solution.py:375
  18.2 0.1 collective-permute-done.6.refs_5_
  18.3 0.4 %collective-permute-start.7 = (f32[192,128]{1,0:T(8,128)S(1)}, f32[192,128]{1,0:T(8,128)S(1)}, u32[]{:S(2)}, u32[]{:S(2)}) collective-permute-start(f32[192,128]{1,0:T(8,128)S(1)} %pad_maximum_fusion), channel_id=1, source_target_pairs={{0,4},{1,5},{2,6},{3,7},{4,0},{5,1},{6,2},{7,3},{8,12},{9,13},{10,... | collective-permute-start | bytes 294920 | tf_op jit(solution)/shard_map/ppermute | solution.py:375
  18.7 0.7 %second_half.1 = (f32[48,1024]{1,0:T(8,128)S(1)}, f32[48,1024]{1,0:T(8,128)S(1)}) custom-call(bf16[2,1024,512]{2,1,0:T(8,128)(2,1)S(1)} %get-tuple-element.43.slots_ref, bf16[2,1024,512]{2,1,0:T(8,128)(2,1)S(1)} %get-tuple-element.44.placed_ref, f32[48,128]{1,0:T(8,128)S(1)} %get-tuple-element.57.stay_ref, f32[48,128]{1,0:T(8,128)S(1)} %get-tuple-element.58.back_ref, ...), custom_call_target="tpu_custom_call" | custom-call | flops 201326592 | bytes 1048576 | tf_op jit(solution)/shard_map/second_half/pallas_call | solution.py:458
  19.5 0.2 collective-permute-done.7.got_ref
  19.7 1.2 %second.1 = (f32[48,1024]{1,0:T(8,128)S(1)}, f32[48,128]{1,0:T(8,128)S(1)}) custom-call(bf16[2,1024,512]{2,1,0:T(8,128)(2,1)S(1)} %get-tuple-element.43.slots_ref, bf16[2,1024,512]{2,1,0:T(8,128)(2,1)S(1)} %get-tuple-element.44.placed_ref, f32[48,1024]{1,0:T(8,128)S(1)} %get-tuple-element.56.basis_ref, f32[48,1024]{1,0:T(8,128)S(1)} %get-tuple-element.62.half_jump_ref, ...), custom_call_target="tpu_custom_call" | custom-call | bytes 1048576 | tf_op jit(solution)/shard_map/second/pallas_call | solution.py:461
  20.9 0.4 %collective-permute-start.8 = (f32[48,128]{1,0:T(8,128)S(1)}, f32[48,128]{1,0:T(8,128)S(1)}, u32[]{:S(2)}, u32[]{:S(2)}) collective-permute-start(f32[48,128]{1,0:T(8,128)S(1)} %get-tuple-element.66.refs_1_), channel_id=1, source_target_pairs={{0,4},{1,5},{2,6},{3,7},{4,0},{5,1},{6,2},{7,3},{8,12},{9,13},{10,... | collective-permute-start | bytes 73736 | tf_op jit(solution)/shard_map/ppermute | solution.py:375
  21.3 0.8 %collective-permute-done.8.refs_0_ = f32[48,128]{1,0:T(8,128)S(1)} collective-permute-done((f32[48,128]{1,0:T(8,128)S(1)}, f32[48,128]{1,0:T(8,128)S(1)}, u32[]{:S(2)}, u32[]{:S(2)}) %collective-permute-start.8) | collective-permute-done | bytes 24608 | tf_op jit(solution)/shard_map/ppermute | solution.py:375
  22.2 2.0 %collective-permute-start.10 = (f32[48,128]{1,0:T(8,128)S(1)}, f32[48,128]{1,0:T(8,128)S(1)}, u32[]{:S(2)}, u32[]{:S(2)}) collective-permute-start(f32[48,128]{1,0:T(8,128)S(1)} %get-tuple-element.68), channel_id=1, source_target_pairs={{0,28},{1,29},{2,30},{3,31},{4,24},{5,25},{6,26},{7,27},{8,20},{9,... | collective-permute-start | bytes 73736 | tf_op jit(solution)/shard_map/ppermute | solution.py:375
  24.2 0.5 %collective-permute-start.11 = (f32[48,128]{1,0:T(8,128)S(1)}, f32[48,128]{1,0:T(8,128)S(1)}, u32[]{:S(2)}, u32[]{:S(2)}) collective-permute-start(f32[48,128]{1,0:T(8,128)S(1)} %get-tuple-element.69), channel_id=1, source_target_pairs={{0,20},{1,21},{2,22},{3,23},{4,16},{5,17},{6,18},{7,19},{8,28},{9,... | collective-permute-start | bytes 73736 | tf_op jit(solution)/shard_map/ppermute | solution.py:375
  24.7 0.7 %collective-permute-start.9 = (f32[48,128]{1,0:T(8,128)S(1)}, f32[48,128]{1,0:T(8,128)S(1)}, u32[]{:S(2)}, u32[]{:S(2)}) collective-permute-start(f32[48,128]{1,0:T(8,128)S(1)} %get-tuple-element.67.refs_3_), channel_id=1, source_target_pairs={{0,12},{1,13},{2,14},{3,15},{4,8},{5,9},{6,10},{7,11},{8,4},{9,5},... | collective-permute-start | bytes 73736 | tf_op jit(solution)/shard_map/ppermute | solution.py:375
  25.4 1.0 %collective-permute-done.10.refs_1_ = f32[48,128]{1,0:T(8,128)S(1)} collective-permute-done((f32[48,128]{1,0:T(8,128)S(1)}, f32[48,128]{1,0:T(8,128)S(1)}, u32[]{:S(2)}, u32[]{:S(2)}) %collective-permute-start.10) | collective-permute-done | bytes 24608 | tf_op jit(solution)/shard_map/ppermute | solution.py:375
  26.4 1.0 %collective-permute-done.11.refs_2_ = f32[48,128]{1,0:T(8,128)S(1)} collective-permute-done((f32[48,128]{1,0:T(8,128)S(1)}, f32[48,128]{1,0:T(8,128)S(1)}, u32[]{:S(2)}, u32[]{:S(2)}) %collective-permute-start.11) | collective-permute-done | bytes 24608 | tf_op jit(solution)/shard_map/ppermute | solution.py:375
  27.4 0.5 %collective-permute-done.9.refs_0_ = f32[48,128]{1,0:T(8,128)S(1)} collective-permute-done((f32[48,128]{1,0:T(8,128)S(1)}, f32[48,128]{1,0:T(8,128)S(1)}, u32[]{:S(2)}, u32[]{:S(2)}) %collective-permute-start.9) | collective-permute-done | bytes 24608 | tf_op jit(solution)/shard_map/ppermute | solution.py:375
  27.9 3.3 %collective-permute-start.12 = (f32[48,128]{1,0:T(8,128)S(1)}, f32[48,128]{1,0:T(8,128)S(1)}, u32[]{:S(2)}, u32[]{:S(2)}) collective-permute-start(f32[48,128]{1,0:T(8,128)S(1)} %get-tuple-element.70.refs_3_), channel_id=1, source_target_pairs={{0,7},{1,6},{2,5},{3,4},{4,3},{5,2},{6,1},{7,0},{8,15},{9,14},{10,... | collective-permute-start | bytes 73736 | tf_op jit(solution)/shard_map/ppermute | solution.py:375
  31.3 0.0 collective-permute-start.13
  31.3 0.6 %collective-permute-start.14 = (f32[48,128]{1,0:T(8,128)S(1)}, f32[48,128]{1,0:T(8,128)S(1)}, u32[]{:S(2)}, u32[]{:S(2)}) collective-permute-start(f32[48,128]{1,0:T(8,128)S(1)} %get-tuple-element.72), channel_id=1, source_target_pairs={{0,5},{1,4},{2,7},{3,6},{4,1},{5,0},{6,3},{7,2},{8,13},{9,12},{10,... | collective-permute-start | bytes 73736 | tf_op jit(solution)/shard_map/ppermute | solution.py:375
  31.9 1.2 %collective-permute-done.12.refs_0_ = f32[48,128]{1,0:T(8,128)S(1)} collective-permute-done((f32[48,128]{1,0:T(8,128)S(1)}, f32[48,128]{1,0:T(8,128)S(1)}, u32[]{:S(2)}, u32[]{:S(2)}) %collective-permute-start.12) | collective-permute-done | bytes 24608 | tf_op jit(solution)/shard_map/ppermute | solution.py:375
  33.1 2.4 %collective-permute-done.13.refs_1_ = f32[48,128]{1,0:T(8,128)S(1)} collective-permute-done((f32[48,128]{1,0:T(8,128)S(1)}, f32[48,128]{1,0:T(8,128)S(1)}, u32[]{:S(2)}, u32[]{:S(2)}) %collective-permute-start.13) | collective-permute-done | bytes 24608 | tf_op jit(solution)/shard_map/ppermute | solution.py:375
  35.4 0.0 collective-permute-done.14.refs_2_
  35.5 2.3 %final.1 = (f32[32,1024]{1,0:T(8,128)}, f32[12,32]{1,0:T(8,128)}) custom-call(f32[48,128]{1,0:T(8,128)S(1)} %sum.5.terms_ref, f32[48,1024]{1,0:T(8,128)S(1)} %get-tuple-element.56.basis_ref, f32[48,1024]{1,0:T(8,128)S(1)} %get-tuple-element.73.jump_ref), custom_call_target="tpu_custom_call" | custom-call | bytes 1048576 | tf_op jit(solution)/shard_map/final/pallas_call | solution.py:464
  (11 shorter events, 0.1 us)
Async XLA Ops:
  2.4 7.3 %collective-permute-start = (f32[80,128]{1,0:T(8,128)S(1)}, f32[80,128]{1,0:T(8,128)S(1)}, u32[]{:S(2)}, u32[]{:S(2)}) collective-permute-start(f32[80,128]{1,0:T(8,128)S(1)} %get-tuple-element.48.refs_0_), channel_id=1, source_target_pairs={{0,28},{1,29},{2,30},{3,31},{4,24},{5,25},{6,26},{7,27},{8,20},{9,... | collective-permute-start | bytes 122888 | tf_op jit(solution)/shard_map/ppermute | solution.py:375
  5.8 3.9 %collective-permute-start.1 = (f32[80,128]{1,0:T(8,128)S(1)}, f32[80,128]{1,0:T(8,128)S(1)}, u32[]{:S(2)}, u32[]{:S(2)}) collective-permute-start(f32[80,128]{1,0:T(8,128)S(1)} %get-tuple-element.49.refs_1_), channel_id=1, source_target_pairs={{0,20},{1,21},{2,22},{3,23},{4,16},{5,17},{6,18},{7,19},{8,28},{9,... | collective-permute-start | bytes 122888 | tf_op jit(solution)/shard_map/ppermute | solution.py:375
  6.6 3.8 %collective-permute-start.2 = (f32[80,128]{1,0:T(8,128)S(1)}, f32[80,128]{1,0:T(8,128)S(1)}, u32[]{:S(2)}, u32[]{:S(2)}) collective-permute-start(f32[80,128]{1,0:T(8,128)S(1)} %get-tuple-element.50.refs_2_), channel_id=1, source_target_pairs={{0,12},{1,13},{2,14},{3,15},{4,8},{5,9},{6,10},{7,11},{8,4},{9,5},... | collective-permute-start | bytes 122888 | tf_op jit(solution)/shard_map/ppermute | solution.py:375
  10.4 1.3 %collective-permute-start.3 = (f32[160,128]{1,0:T(8,128)S(1)}, f32[160,128]{1,0:T(8,128)S(1)}, u32[]{:S(2)}, u32[]{:S(2)}) collective-permute-start(f32[160,128]{1,0:T(8,128)S(1)} %pad_maximum_fusion.1), channel_id=1, source_target_pairs={{0,4},{1,5},{2,6},{3,7},{4,0},{5,1},{6,2},{7,3},{8,12},{9,13},{10,... | collective-permute-start | bytes 245768 | tf_op jit(solution)/shard_map/ppermute | solution.py:375
  12.5 4.6 %collective-permute-start.4 = (f32[96,128]{1,0:T(8,128)S(1)}, f32[96,128]{1,0:T(8,128)S(1)}, u32[]{:S(2)}, u32[]{:S(2)}) collective-permute-start(f32[96,128]{1,0:T(8,128)S(1)} %get-tuple-element.59.refs_0_), channel_id=1, source_target_pairs={{0,28},{1,29},{2,30},{3,31},{4,24},{5,25},{6,26},{7,27},{8,20},{9,... | collective-permute-start | bytes 147464 | tf_op jit(solution)/shard_map/ppermute | solution.py:375
  14.5 3.7 %collective-permute-start.5 = (f32[96,128]{1,0:T(8,128)S(1)}, f32[96,128]{1,0:T(8,128)S(1)}, u32[]{:S(2)}, u32[]{:S(2)}) collective-permute-start(f32[96,128]{1,0:T(8,128)S(1)} %get-tuple-element.60.refs_1_), channel_id=1, source_target_pairs={{0,20},{1,21},{2,22},{3,23},{4,16},{5,17},{6,18},{7,19},{8,28},{9,... | collective-permute-start | bytes 147464 | tf_op jit(solution)/shard_map/ppermute | solution.py:375
  14.8 3.5 %collective-permute-start.6 = (f32[96,128]{1,0:T(8,128)S(1)}, f32[96,128]{1,0:T(8,128)S(1)}, u32[]{:S(2)}, u32[]{:S(2)}) collective-permute-start(f32[96,128]{1,0:T(8,128)S(1)} %get-tuple-element.61.refs_2_), channel_id=1, source_target_pairs={{0,12},{1,13},{2,14},{3,15},{4,8},{5,9},{6,10},{7,11},{8,4},{9,5},... | collective-permute-start | bytes 147464 | tf_op jit(solution)/shard_map/ppermute | solution.py:375
  18.3 1.4 %collective-permute-start.7 = (f32[192,128]{1,0:T(8,128)S(1)}, f32[192,128]{1,0:T(8,128)S(1)}, u32[]{:S(2)}, u32[]{:S(2)}) collective-permute-start(f32[192,128]{1,0:T(8,128)S(1)} %pad_maximum_fusion), channel_id=1, source_target_pairs={{0,4},{1,5},{2,6},{3,7},{4,0},{5,1},{6,2},{7,3},{8,12},{9,13},{10,... | collective-permute-start | bytes 294920 | tf_op jit(solution)/shard_map/ppermute | solution.py:375
  20.9 1.3 %collective-permute-start.8 = (f32[48,128]{1,0:T(8,128)S(1)}, f32[48,128]{1,0:T(8,128)S(1)}, u32[]{:S(2)}, u32[]{:S(2)}) collective-permute-start(f32[48,128]{1,0:T(8,128)S(1)} %get-tuple-element.66.refs_1_), channel_id=1, source_target_pairs={{0,4},{1,5},{2,6},{3,7},{4,0},{5,1},{6,2},{7,3},{8,12},{9,13},{10,... | collective-permute-start | bytes 73736 | tf_op jit(solution)/shard_map/ppermute | solution.py:375
  22.2 4.2 %collective-permute-start.10 = (f32[48,128]{1,0:T(8,128)S(1)}, f32[48,128]{1,0:T(8,128)S(1)}, u32[]{:S(2)}, u32[]{:S(2)}) collective-permute-start(f32[48,128]{1,0:T(8,128)S(1)} %get-tuple-element.68), channel_id=1, source_target_pairs={{0,28},{1,29},{2,30},{3,31},{4,24},{5,25},{6,26},{7,27},{8,20},{9,... | collective-permute-start | bytes 73736 | tf_op jit(solution)/shard_map/ppermute | solution.py:375
  24.2 3.3 %collective-permute-start.11 = (f32[48,128]{1,0:T(8,128)S(1)}, f32[48,128]{1,0:T(8,128)S(1)}, u32[]{:S(2)}, u32[]{:S(2)}) collective-permute-start(f32[48,128]{1,0:T(8,128)S(1)} %get-tuple-element.69), channel_id=1, source_target_pairs={{0,20},{1,21},{2,22},{3,23},{4,16},{5,17},{6,18},{7,19},{8,28},{9,... | collective-permute-start | bytes 73736 | tf_op jit(solution)/shard_map/ppermute | solution.py:375
  24.7 3.3 %collective-permute-start.9 = (f32[48,128]{1,0:T(8,128)S(1)}, f32[48,128]{1,0:T(8,128)S(1)}, u32[]{:S(2)}, u32[]{:S(2)}) collective-permute-start(f32[48,128]{1,0:T(8,128)S(1)} %get-tuple-element.67.refs_3_), channel_id=1, source_target_pairs={{0,12},{1,13},{2,14},{3,15},{4,8},{5,9},{6,10},{7,11},{8,4},{9,5},... | collective-permute-start | bytes 73736 | tf_op jit(solution)/shard_map/ppermute | solution.py:375
  27.9 5.1 %collective-permute-start.12 = (f32[48,128]{1,0:T(8,128)S(1)}, f32[48,128]{1,0:T(8,128)S(1)}, u32[]{:S(2)}, u32[]{:S(2)}) collective-permute-start(f32[48,128]{1,0:T(8,128)S(1)} %get-tuple-element.70.refs_3_), channel_id=1, source_target_pairs={{0,7},{1,6},{2,5},{3,4},{4,3},{5,2},{6,1},{7,0},{8,15},{9,14},{10,... | collective-permute-start | bytes 73736 | tf_op jit(solution)/shard_map/ppermute | solution.py:375
  31.3 4.2 %collective-permute-start.13 = (f32[48,128]{1,0:T(8,128)S(1)}, f32[48,128]{1,0:T(8,128)S(1)}, u32[]{:S(2)}, u32[]{:S(2)}) collective-permute-start(f32[48,128]{1,0:T(8,128)S(1)} %get-tuple-element.71), channel_id=1, source_target_pairs={{0,6},{1,7},{2,4},{3,5},{4,2},{5,3},{6,0},{7,1},{8,14},{9,15},{10,... | collective-permute-start | bytes 73736 | tf_op jit(solution)/shard_map/ppermute | solution.py:375
  31.3 4.2 %collective-permute-start.14 = (f32[48,128]{1,0:T(8,128)S(1)}, f32[48,128]{1,0:T(8,128)S(1)}, u32[]{:S(2)}, u32[]{:S(2)}) collective-permute-start(f32[48,128]{1,0:T(8,128)S(1)} %get-tuple-element.72), channel_id=1, source_target_pairs={{0,5},{1,4},{2,7},{3,6},{4,1},{5,0},{6,3},{7,2},{8,13},{9,12},{10,... | collective-permute-start | bytes 73736 | tf_op jit(solution)/shard_map/ppermute | solution.py:375

commit v2 on v1

--- a/solution.py
+++ b/solution.py
@@ -12,6 +12,7 @@
 ITERS = 2
 GROUP = 8
 SCALAR_LANES = (MODES, MODES + 1, GROUP + MODES, GROUP + MODES + 1, 2 * GROUP + MODES)
+OPERATOR_PARTS = 8
 
 HIGHEST = lax.Precision.HIGHEST
 VMEM = pl.BlockSpec(memory_space=pltpu.VMEM)
@@ -29,10 +30,6 @@
     rows = values.shape[0]
     both = lax.dot_general(split(values), matrix, dims, preferred_element_type=jnp.float32)
     return both[:rows] + both[rows:]
-
-
-def small_dot(left, right):
-    return jnp.dot(left, right, precision=HIGHEST, preferred_element_type=jnp.float32)
 
 
 def send_far(values, far_ref, *pair_refs):
@@ -90,6 +87,8 @@
     loads, rows = gap_hbm.shape
     per_peer = pair_refs[0].shape[1]
     peers = rows // per_peer
+    height = rows // OPERATOR_PARTS
+    parts = [pl.ds(start, height) for start in range(0, rows, height)]
     copies = [
         pltpu.make_async_copy(source, target, sems.at[at])
         for at, (source, target) in enumerate(
@@ -98,7 +97,7 @@
                 (block_hbm, block_ref),
                 (traces_hbm, traces_ref),
                 (gap_hbm, values_ref.at[pl.ds(0, loads)]),
-                (operator_hbm, operator_ref),
+                *((operator_hbm.at[:, part], operator_ref.at[:, part]) for part in parts),
             )
         )
     ]
@@ -129,7 +128,8 @@
     for at in range(peers - 4, peers - 2):
         build(at)
     send_far(values_ref[...], far_ref, *pair_refs)
-    copies[4].wait()
+    for copy in copies[4:]:
+        copy.wait()
 
 
 def ready_kernel(
@@ -324,7 +324,7 @@
     amounts = solved[:, 2 * coarse : 2 * coarse + loads]
     inverse_image = solved[:, 2 * coarse + loads : 2 * coarse + 2 * loads]
     inverse = solved[:, 2 * coarse + 2 * loads : 3 * coarse + 2 * loads]
-    products = small_dot(jnp.concatenate([inverse_h, g_h, z_z, g_dz, z_dz], axis=0), amounts)
+    products = thin_dot(jnp.concatenate([inverse_h, g_h, z_z, g_dz, z_dz], axis=0), amounts)
     inverse_h_amounts, h_amounts, z_amounts, g_dz_amounts, z_dz_amounts = (
         products[at * coarse : (at + 1) * coarse] for at in range(5)
     )
@@ -333,7 +333,7 @@
     basis_g, jump_z_rows = basis_ref[loads:], jump_ref[loads:]
     d = basis_ref[:loads] - thin_dot(both[:, :coarse], basis_g)
     u = jump_ref[:loads] - thin_dot(both, jnp.concatenate([jump_z_rows, basis_g], axis=0))
-    products = small_dot(jnp.concatenate([g_h, z_z], axis=0), shares)
+    products = thin_dot(jnp.concatenate([g_h, z_z], axis=0), shares)
     image_d = image_g - h_amounts
     inner = res_res - total(amounts * coarse_res)
     curvature = 2.0 * (res_image - total(amounts * (res_h + image_d)))
@@ -348,7 +348,7 @@
     curvature = grown * grown * curvature - grown * step * (2.0 * d_second + u_u) + 2.0 * step * step * u_second
     second_step = renewed / curvature
     on_d, on_u = step + second_step * grown, second_step * step
-    amplitudes = amounts - on_d * shares + 2.0 * on_u * small_dot(inverse, second_u)
+    amplitudes = amounts - on_d * shares + 2.0 * on_u * thin_dot(inverse, second_u)
     amplitudes_ref[...] = jnp.concatenate(
         [amplitudes[label * GROUP : label * GROUP + MODES] for label in range(groups)], axis=0
     )
@@ -431,7 +431,7 @@
         ],
         [HBM] * 5,
         "place",
-        [pltpu.VMEM((1, subs), i32), pltpu.VMEM((modes, 1, rows), f32), pltpu.SemaphoreType.DMA((5,))],
+        [pltpu.VMEM((1, subs), i32), pltpu.VMEM((modes, 1, rows), f32), pltpu.SemaphoreType.DMA((4 + OPERATOR_PARTS,))],
     )(*(held(value) for value in inputs))
     got = to_chips(*send)
     halves = ((2, rows, rows // 2), dual_ops.dtype)

time: 37.9 us -> 37.9 us (level)
  no operation moved by 1% of the time
where the time goes in v2:
time: 37.9 us; the launch traced here: 37.7 us
  starting transfers between devices  15.6 us (41%)
  Pallas kernels  11.4 us (30%)
  waiting for transfers between devices  9.96 us (26%)
  between operations  0.75 us (2%)
    ppermute x15, starting transfers between devices, permute(): lax.ppermute(values, ('sub', 'rep'), [(at, at ^ offset) for at in range(p...  15.6 us
    ppermute x15, waiting for transfers between devices, permute(): lax.ppermute(values, ('sub', 'rep'), [(at, at ^ offset) for at in range(p...  9.96 us
    pallas_call x1, Pallas kernels, fused_body(): call(ready_kernel, [((rows, 3 * per_peer), jnp.bfloat16), halves, halves,...  2.97 us
    pallas_call x1, Pallas kernels, fused_body(): call(final_kernel, [((loads, rows), f32), ((MODES * groups, loads), f32)]...  2.29 us
    pallas_call x1, Pallas kernels, fused_body(): call(place_kernel, [((rows, rows - 2 * per_peer), jnp.bfloat16), ((short,...  1.72 us
    pallas_call x1, Pallas kernels, fused_body(): call(second_kernel, [tall, wide], [VMEM] * (8 + len(got)), 'second')  1.22 us
    pallas_call x1, Pallas kernels, fused_body(): call(middle_kernel, [tall, wide, *singles(height)], [VMEM] * 5, 'middle',...  1.2 us
    pallas_call x1, Pallas kernels, fused_body(): call(first_kernel, [half, tall, *pairs(height)], [VMEM] * (5 + len(send))...  0.79 us
  transfers between devices with their start and end apart: 15, of which 12 were waited for; matrix products, arithmetic and copies ran while one was open for 0% of the time, Pallas kernels for 14%

profile of v2, /device:TPU:0, one launch (start us, length us, event | category | flops | bytes accessed | tf_op | source)
XLA Modules:
  0.0 37.7 jit_solution(1066363802867877802)
XLA Ops:
  0.6 1.7 %place.1 = (bf16[1024,768]{1,0:T(8,128)(2,1)S(1)}, f32[40,1024]{1,0:T(8,128)S(1)}, bf16[1,1024,1024]{2,1,0:T(8,128)(2,1)S(1)}, s32[1,1024]{1,0:T(1,128)S(1)}, f3...) custom-call(s32[1,1024]{1,0:T(1,128)} %route_hbm.1, s32[1,32]{1,0:T(1,128)} %bitcast.4, ...), custom_call_target="tpu_custom_call" | custom-call | bytes 1048576 | tf_op jit(solution)/shard_map/place/pallas_call | solution.py:423
  2.4 3.4 %collective-permute-start = (f32[80,128]{1,0:T(8,128)S(1)}, f32[80,128]{1,0:T(8,128)S(1)}, u32[]{:S(2)}, u32[]{:S(2)}) collective-permute-start(f32[80,128]{1,0:T(8,128)S(1)} %get-tuple-element.48.refs_0_), channel_id=1, source_target_pairs={{0,28},{1,29},{2,30},{3,31},{4,24},{5,25},{6,26},{7,27},{8,20},{9,... | collective-permute-start | bytes 122888 | tf_op jit(solution)/shard_map/ppermute | solution.py:375
  5.8 0.8 %collective-permute-start.1 = (f32[80,128]{1,0:T(8,128)S(1)}, f32[80,128]{1,0:T(8,128)S(1)}, u32[]{:S(2)}, u32[]{:S(2)}) collective-permute-start(f32[80,128]{1,0:T(8,128)S(1)} %get-tuple-element.49.refs_1_), channel_id=1, source_target_pairs={{0,20},{1,21},{2,22},{3,23},{4,16},{5,17},{6,18},{7,19},{8,28},{9,... | collective-permute-start | bytes 122888 | tf_op jit(solution)/shard_map/ppermute | solution.py:375
  6.5 0.1 collective-permute-start.2
  6.7 3.0 %ready.1 = (bf16[1024,384]{1,0:T(8,128)(2,1)S(1)}, bf16[2,1024,512]{2,1,0:T(8,128)(2,1)S(1)}, bf16[2,1024,512]{2,1,0:T(8,128)(2,1)S(1)}, f32[40,128]{1,0:T(8,128...) custom-call(s32[1,1024]{1,0:T(1,128)S(1)} %get-tuple-element.39.route_ref, ...), custom_call_target="tpu_custom_call" | custom-call | flops 2147483648 | bytes 1048576 | tf_op jit(solution)/shard_map/ready/pallas_call | solution.py:438
  9.7 0.0 collective-permute-done.refs_3_
  9.7 0.0 collective-permute-done.1.refs_4_
  9.7 0.6 %collective-permute-done.2.refs_5_ = f32[80,128]{1,0:T(8,128)S(1)} collective-permute-done((f32[80,128]{1,0:T(8,128)S(1)}, f32[80,128]{1,0:T(8,128)S(1)}, u32[]{:S(2)}, u32[]{:S(2)}) %collective-permute-start.2) | collective-permute-done | bytes 40992 | tf_op jit(solution)/shard_map/ppermute | solution.py:375
  10.4 0.2 collective-permute-start.3
  10.5 0.4 %first_half.1 = (f32[48,512]{1,0:T(8,128)S(1)}, f32[48,1024]{1,0:T(8,128)S(1)}) custom-call(bf16[2,1024,512]{2,1,0:T(8,128)(2,1)S(1)} %get-tuple-element.44.placed_ref, f32[40,128]{1,0:T(8,128)S(1)} %get-tuple-element.46.stay_ref, f32[40,128]{1,0:T(8,128)S(1)} %get-tuple-element.47.back_ref, f32[80,128]{1,0:T(8,128)S(1)} %get-tuple-element.48.refs_0_, ...), custom_call_target="tpu_custom_call" | custom-call | flops 100663296 | bytes 1048576 | tf_op jit(solution)/shard_map/first_half/pallas_call | solution.py:447
  11.0 0.7 %collective-permute-done.3.got_ref = f32[160,128]{1,0:T(8,128)S(1)} collective-permute-done((f32[160,128]{1,0:T(8,128)S(1)}, f32[160,128]{1,0:T(8,128)S(1)}, u32[]{:S(2)}, u32[]{:S(2)}) %collective-permute-start.3) | collective-permute-done | bytes 81952 | tf_op jit(solution)/shard_map/ppermute | solution.py:375
  11.7 0.8 %first.1 = (f32[48,512]{1,0:T(8,128)S(1)}, f32[48,1024]{1,0:T(8,128)S(1)}, f32[96,128]{1,0:T(8,128)S(1)}, f32[96,128]{1,0:T(8,128)S(1)}, f32[96,128]{1,0:T(8,128)S(1)}) custom-call(bf16[1024,768]{1,0:T(8,128)(2,1)S(1)} %get-tuple-element.40.far_ref, bf16[2,1024,512]{2,1,0:T(8,128)(2,1)S(1)} %get-tuple-element.44.placed_ref, ...), custom_call_target="tpu_custom_call" | custom-call | bytes 1048576 | tf_op jit(solution)/shard_map/first/pallas_call | solution.py:450
  12.5 2.0 %collective-permute-start.4 = (f32[96,128]{1,0:T(8,128)S(1)}, f32[96,128]{1,0:T(8,128)S(1)}, u32[]{:S(2)}, u32[]{:S(2)}) collective-permute-start(f32[96,128]{1,0:T(8,128)S(1)} %get-tuple-element.59.refs_0_), channel_id=1, source_target_pairs={{0,28},{1,29},{2,30},{3,31},{4,24},{5,25},{6,26},{7,27},{8,20},{9,... | collective-permute-start | bytes 147464 | tf_op jit(solution)/shard_map/ppermute | solution.py:375
  14.5 0.3 collective-permute-start.5
  14.7 0.7 %collective-permute-start.6 = (f32[96,128]{1,0:T(8,128)S(1)}, f32[96,128]{1,0:T(8,128)S(1)}, u32[]{:S(2)}, u32[]{:S(2)}) collective-permute-start(f32[96,128]{1,0:T(8,128)S(1)} %get-tuple-element.61.refs_2_), channel_id=1, source_target_pairs={{0,12},{1,13},{2,14},{3,15},{4,8},{5,9},{6,10},{7,11},{8,4},{9,5},... | collective-permute-start | bytes 147464 | tf_op jit(solution)/shard_map/ppermute | solution.py:375
  15.5 1.2 %middle.1 = (f32[48,1024]{1,0:T(8,128)S(1)}, f32[48,128]{1,0:T(8,128)S(1)}, f32[48,128]{1,0:T(8,128)S(1)}, f32[48,128]{1,0:T(8,128)S(1)}, f32[48,128]{1,0:T(8,128)S(1)}) custom-call(bf16[1024,384]{1,0:T(8,128)(2,1)S(1)} %get-tuple-element.45.edge_ref, bf16[2,1024,512]{2,1,0:T(8,128)(2,1)S(1)} %get-tuple-element.43.slots_ref, ...), custom_call_target="tpu_custom_call" | custom-call | flops 201326592 | bytes 1048576 | tf_op jit(solution)/shard_map/middle/pallas_call | solution.py:454
  16.7 0.4 %collective-permute-done.4.refs_3_ = f32[96,128]{1,0:T(8,128)S(1)} collective-permute-done((f32[96,128]{1,0:T(8,128)S(1)}, f32[96,128]{1,0:T(8,128)S(1)}, u32[]{:S(2)}, u32[]{:S(2)}) %collective-permute-start.4) | collective-permute-done | bytes 49184 | tf_op jit(solution)/shard_map/ppermute | solution.py:375
  17.1 1.1 %collective-permute-done.5.refs_4_ = f32[96,128]{1,0:T(8,128)S(1)} collective-permute-done((f32[96,128]{1,0:T(8,128)S(1)}, f32[96,128]{1,0:T(8,128)S(1)}, u32[]{:S(2)}, u32[]{:S(2)}) %collective-permute-start.5) | collective-permute-done | bytes 49184 | tf_op jit(solution)/shard_map/ppermute | solution.py:375
  18.2 0.1 collective-permute-done.6.refs_5_
  18.3 0.4 %collective-permute-start.7 = (f32[192,128]{1,0:T(8,128)S(1)}, f32[192,128]{1,0:T(8,128)S(1)}, u32[]{:S(2)}, u32[]{:S(2)}) collective-permute-start(f32[192,128]{1,0:T(8,128)S(1)} %pad_maximum_fusion), channel_id=1, source_target_pairs={{0,4},{1,5},{2,6},{3,7},{4,0},{5,1},{6,2},{7,3},{8,12},{9,13},{10,... | collective-permute-start | bytes 294920 | tf_op jit(solution)/shard_map/ppermute | solution.py:375
  18.7 0.7 %second_half.1 = (f32[48,1024]{1,0:T(8,128)S(1)}, f32[48,1024]{1,0:T(8,128)S(1)}) custom-call(bf16[2,1024,512]{2,1,0:T(8,128)(2,1)S(1)} %get-tuple-element.43.slots_ref, bf16[2,1024,512]{2,1,0:T(8,128)(2,1)S(1)} %get-tuple-element.44.placed_ref, f32[48,128]{1,0:T(8,128)S(1)} %get-tuple-element.57.stay_ref, f32[48,128]{1,0:T(8,128)S(1)} %get-tuple-element.58.back_ref, ...), custom_call_target="tpu_custom_call" | custom-call | flops 201326592 | bytes 1048576 | tf_op jit(solution)/shard_map/second_half/pallas_call | solution.py:458
  19.4 0.2 collective-permute-done.7.got_ref
  19.6 1.2 %second.1 = (f32[48,1024]{1,0:T(8,128)S(1)}, f32[48,128]{1,0:T(8,128)S(1)}) custom-call(bf16[2,1024,512]{2,1,0:T(8,128)(2,1)S(1)} %get-tuple-element.43.slots_ref, bf16[2,1024,512]{2,1,0:T(8,128)(2,1)S(1)} %get-tuple-element.44.placed_ref, f32[48,1024]{1,0:T(8,128)S(1)} %get-tuple-element.56.basis_ref, f32[48,1024]{1,0:T(8,128)S(1)} %get-tuple-element.62.half_jump_ref, ...), custom_call_target="tpu_custom_call" | custom-call | bytes 1048576 | tf_op jit(solution)/shard_map/second/pallas_call | solution.py:461
  20.9 0.4 %collective-permute-start.8 = (f32[48,128]{1,0:T(8,128)S(1)}, f32[48,128]{1,0:T(8,128)S(1)}, u32[]{:S(2)}, u32[]{:S(2)}) collective-permute-start(f32[48,128]{1,0:T(8,128)S(1)} %get-tuple-element.66.refs_1_), channel_id=1, source_target_pairs={{0,4},{1,5},{2,6},{3,7},{4,0},{5,1},{6,2},{7,3},{8,12},{9,13},{10,... | collective-permute-start | bytes 73736 | tf_op jit(solution)/shard_map/ppermute | solution.py:375
  21.3 0.8 %collective-permute-done.8.refs_0_ = f32[48,128]{1,0:T(8,128)S(1)} collective-permute-done((f32[48,128]{1,0:T(8,128)S(1)}, f32[48,128]{1,0:T(8,128)S(1)}, u32[]{:S(2)}, u32[]{:S(2)}) %collective-permute-start.8) | collective-permute-done | bytes 24608 | tf_op jit(solution)/shard_map/ppermute | solution.py:375
  22.1 2.0 %collective-permute-start.10 = (f32[48,128]{1,0:T(8,128)S(1)}, f32[48,128]{1,0:T(8,128)S(1)}, u32[]{:S(2)}, u32[]{:S(2)}) collective-permute-start(f32[48,128]{1,0:T(8,128)S(1)} %get-tuple-element.68), channel_id=1, source_target_pairs={{0,28},{1,29},{2,30},{3,31},{4,24},{5,25},{6,26},{7,27},{8,20},{9,... | collective-permute-start | bytes 73736 | tf_op jit(solution)/shard_map/ppermute | solution.py:375
  24.1 0.4 %collective-permute-start.11 = (f32[48,128]{1,0:T(8,128)S(1)}, f32[48,128]{1,0:T(8,128)S(1)}, u32[]{:S(2)}, u32[]{:S(2)}) collective-permute-start(f32[48,128]{1,0:T(8,128)S(1)} %get-tuple-element.69), channel_id=1, source_target_pairs={{0,20},{1,21},{2,22},{3,23},{4,16},{5,17},{6,18},{7,19},{8,28},{9,... | collective-permute-start | bytes 73736 | tf_op jit(solution)/shard_map/ppermute | solution.py:375
  24.5 0.8 %collective-permute-start.9 = (f32[48,128]{1,0:T(8,128)S(1)}, f32[48,128]{1,0:T(8,128)S(1)}, u32[]{:S(2)}, u32[]{:S(2)}) collective-permute-start(f32[48,128]{1,0:T(8,128)S(1)} %get-tuple-element.67.refs_3_), channel_id=1, source_target_pairs={{0,12},{1,13},{2,14},{3,15},{4,8},{5,9},{6,10},{7,11},{8,4},{9,5},... | collective-permute-start | bytes 73736 | tf_op jit(solution)/shard_map/ppermute | solution.py:375
  25.4 1.0 %collective-permute-done.10.refs_1_ = f32[48,128]{1,0:T(8,128)S(1)} collective-permute-done((f32[48,128]{1,0:T(8,128)S(1)}, f32[48,128]{1,0:T(8,128)S(1)}, u32[]{:S(2)}, u32[]{:S(2)}) %collective-permute-start.10) | collective-permute-done | bytes 24608 | tf_op jit(solution)/shard_map/ppermute | solution.py:375
  26.3 1.1 %collective-permute-done.11.refs_2_ = f32[48,128]{1,0:T(8,128)S(1)} collective-permute-done((f32[48,128]{1,0:T(8,128)S(1)}, f32[48,128]{1,0:T(8,128)S(1)}, u32[]{:S(2)}, u32[]{:S(2)}) %collective-permute-start.11) | collective-permute-done | bytes 24608 | tf_op jit(solution)/shard_map/ppermute | solution.py:375
  27.4 0.4 %collective-permute-done.9.refs_0_ = f32[48,128]{1,0:T(8,128)S(1)} collective-permute-done((f32[48,128]{1,0:T(8,128)S(1)}, f32[48,128]{1,0:T(8,128)S(1)}, u32[]{:S(2)}, u32[]{:S(2)}) %collective-permute-start.9) | collective-permute-done | bytes 24608 | tf_op jit(solution)/shard_map/ppermute | solution.py:375
  27.8 3.4 %collective-permute-start.12 = (f32[48,128]{1,0:T(8,128)S(1)}, f32[48,128]{1,0:T(8,128)S(1)}, u32[]{:S(2)}, u32[]{:S(2)}) collective-permute-start(f32[48,128]{1,0:T(8,128)S(1)} %get-tuple-element.70.refs_3_), channel_id=1, source_target_pairs={{0,7},{1,6},{2,5},{3,4},{4,3},{5,2},{6,1},{7,0},{8,15},{9,14},{10,... | collective-permute-start | bytes 73736 | tf_op jit(solution)/shard_map/ppermute | solution.py:375
  31.2 0.0 collective-permute-start.13
  31.3 0.6 %collective-permute-start.14 = (f32[48,128]{1,0:T(8,128)S(1)}, f32[48,128]{1,0:T(8,128)S(1)}, u32[]{:S(2)}, u32[]{:S(2)}) collective-permute-start(f32[48,128]{1,0:T(8,128)S(1)} %get-tuple-element.72), channel_id=1, source_target_pairs={{0,5},{1,4},{2,7},{3,6},{4,1},{5,0},{6,3},{7,2},{8,13},{9,12},{10,... | collective-permute-start | bytes 73736 | tf_op jit(solution)/shard_map/ppermute | solution.py:375
  31.8 1.1 %collective-permute-done.12.refs_0_ = f32[48,128]{1,0:T(8,128)S(1)} collective-permute-done((f32[48,128]{1,0:T(8,128)S(1)}, f32[48,128]{1,0:T(8,128)S(1)}, u32[]{:S(2)}, u32[]{:S(2)}) %collective-permute-start.12) | collective-permute-done | bytes 24608 | tf_op jit(solution)/shard_map/ppermute | solution.py:375
  32.9 2.5 %collective-permute-done.13.refs_1_ = f32[48,128]{1,0:T(8,128)S(1)} collective-permute-done((f32[48,128]{1,0:T(8,128)S(1)}, f32[48,128]{1,0:T(8,128)S(1)}, u32[]{:S(2)}, u32[]{:S(2)}) %collective-permute-start.13) | collective-permute-done | bytes 24608 | tf_op jit(solution)/shard_map/ppermute | solution.py:375
  35.4 0.0 collective-permute-done.14.refs_2_
  35.4 2.3 %final.1 = (f32[32,1024]{1,0:T(8,128)}, f32[12,32]{1,0:T(8,128)}) custom-call(f32[48,128]{1,0:T(8,128)S(1)} %sum.5.terms_ref, f32[48,1024]{1,0:T(8,128)S(1)} %get-tuple-element.56.basis_ref, f32[48,1024]{1,0:T(8,128)S(1)} %get-tuple-element.73.jump_ref), custom_call_target="tpu_custom_call" | custom-call | bytes 1048576 | tf_op jit(solution)/shard_map/final/pallas_call | solution.py:464
  (11 shorter events, 0.1 us)
Async XLA Ops:
  2.4 7.3 %collective-permute-start = (f32[80,128]{1,0:T(8,128)S(1)}, f32[80,128]{1,0:T(8,128)S(1)}, u32[]{:S(2)}, u32[]{:S(2)}) collective-permute-start(f32[80,128]{1,0:T(8,128)S(1)} %get-tuple-element.48.refs_0_), channel_id=1, source_target_pairs={{0,28},{1,29},{2,30},{3,31},{4,24},{5,25},{6,26},{7,27},{8,20},{9,... | collective-permute-start | bytes 122888 | tf_op jit(solution)/shard_map/ppermute | solution.py:375
  5.8 3.9 %collective-permute-start.1 = (f32[80,128]{1,0:T(8,128)S(1)}, f32[80,128]{1,0:T(8,128)S(1)}, u32[]{:S(2)}, u32[]{:S(2)}) collective-permute-start(f32[80,128]{1,0:T(8,128)S(1)} %get-tuple-element.49.refs_1_), channel_id=1, source_target_pairs={{0,20},{1,21},{2,22},{3,23},{4,16},{5,17},{6,18},{7,19},{8,28},{9,... | collective-permute-start | bytes 122888 | tf_op jit(solution)/shard_map/ppermute | solution.py:375
  6.5 3.8 %collective-permute-start.2 = (f32[80,128]{1,0:T(8,128)S(1)}, f32[80,128]{1,0:T(8,128)S(1)}, u32[]{:S(2)}, u32[]{:S(2)}) collective-permute-start(f32[80,128]{1,0:T(8,128)S(1)} %get-tuple-element.50.refs_2_), channel_id=1, source_target_pairs={{0,12},{1,13},{2,14},{3,15},{4,8},{5,9},{6,10},{7,11},{8,4},{9,5},... | collective-permute-start | bytes 122888 | tf_op jit(solution)/shard_map/ppermute | solution.py:375
  10.4 1.3 %collective-permute-start.3 = (f32[160,128]{1,0:T(8,128)S(1)}, f32[160,128]{1,0:T(8,128)S(1)}, u32[]{:S(2)}, u32[]{:S(2)}) collective-permute-start(f32[160,128]{1,0:T(8,128)S(1)} %pad_maximum_fusion.1), channel_id=1, source_target_pairs={{0,4},{1,5},{2,6},{3,7},{4,0},{5,1},{6,2},{7,3},{8,12},{9,13},{10,... | collective-permute-start | bytes 245768 | tf_op jit(solution)/shard_map/ppermute | solution.py:375
  12.5 4.6 %collective-permute-start.4 = (f32[96,128]{1,0:T(8,128)S(1)}, f32[96,128]{1,0:T(8,128)S(1)}, u32[]{:S(2)}, u32[]{:S(2)}) collective-permute-start(f32[96,128]{1,0:T(8,128)S(1)} %get-tuple-element.59.refs_0_), channel_id=1, source_target_pairs={{0,28},{1,29},{2,30},{3,31},{4,24},{5,25},{6,26},{7,27},{8,20},{9,... | collective-permute-start | bytes 147464 | tf_op jit(solution)/shard_map/ppermute | solution.py:375
  14.5 3.7 %collective-permute-start.5 = (f32[96,128]{1,0:T(8,128)S(1)}, f32[96,128]{1,0:T(8,128)S(1)}, u32[]{:S(2)}, u32[]{:S(2)}) collective-permute-start(f32[96,128]{1,0:T(8,128)S(1)} %get-tuple-element.60.refs_1_), channel_id=1, source_target_pairs={{0,20},{1,21},{2,22},{3,23},{4,16},{5,17},{6,18},{7,19},{8,28},{9,... | collective-permute-start | bytes 147464 | tf_op jit(solution)/shard_map/ppermute | solution.py:375
  14.7 3.5 %collective-permute-start.6 = (f32[96,128]{1,0:T(8,128)S(1)}, f32[96,128]{1,0:T(8,128)S(1)}, u32[]{:S(2)}, u32[]{:S(2)}) collective-permute-start(f32[96,128]{1,0:T(8,128)S(1)} %get-tuple-element.61.refs_2_), channel_id=1, source_target_pairs={{0,12},{1,13},{2,14},{3,15},{4,8},{5,9},{6,10},{7,11},{8,4},{9,5},... | collective-permute-start | bytes 147464 | tf_op jit(solution)/shard_map/ppermute | solution.py:375
  18.3 1.4 %collective-permute-start.7 = (f32[192,128]{1,0:T(8,128)S(1)}, f32[192,128]{1,0:T(8,128)S(1)}, u32[]{:S(2)}, u32[]{:S(2)}) collective-permute-start(f32[192,128]{1,0:T(8,128)S(1)} %pad_maximum_fusion), channel_id=1, source_target_pairs={{0,4},{1,5},{2,6},{3,7},{4,0},{5,1},{6,2},{7,3},{8,12},{9,13},{10,... | collective-permute-start | bytes 294920 | tf_op jit(solution)/shard_map/ppermute | solution.py:375
  20.9 1.3 %collective-permute-start.8 = (f32[48,128]{1,0:T(8,128)S(1)}, f32[48,128]{1,0:T(8,128)S(1)}, u32[]{:S(2)}, u32[]{:S(2)}) collective-permute-start(f32[48,128]{1,0:T(8,128)S(1)} %get-tuple-element.66.refs_1_), channel_id=1, source_target_pairs={{0,4},{1,5},{2,6},{3,7},{4,0},{5,1},{6,2},{7,3},{8,12},{9,13},{10,... | collective-permute-start | bytes 73736 | tf_op jit(solution)/shard_map/ppermute | solution.py:375
  22.1 4.2 %collective-permute-start.10 = (f32[48,128]{1,0:T(8,128)S(1)}, f32[48,128]{1,0:T(8,128)S(1)}, u32[]{:S(2)}, u32[]{:S(2)}) collective-permute-start(f32[48,128]{1,0:T(8,128)S(1)} %get-tuple-element.68), channel_id=1, source_target_pairs={{0,28},{1,29},{2,30},{3,31},{4,24},{5,25},{6,26},{7,27},{8,20},{9,... | collective-permute-start | bytes 73736 | tf_op jit(solution)/shard_map/ppermute | solution.py:375
  24.1 3.3 %collective-permute-start.11 = (f32[48,128]{1,0:T(8,128)S(1)}, f32[48,128]{1,0:T(8,128)S(1)}, u32[]{:S(2)}, u32[]{:S(2)}) collective-permute-start(f32[48,128]{1,0:T(8,128)S(1)} %get-tuple-element.69), channel_id=1, source_target_pairs={{0,20},{1,21},{2,22},{3,23},{4,16},{5,17},{6,18},{7,19},{8,28},{9,... | collective-permute-start | bytes 73736 | tf_op jit(solution)/shard_map/ppermute | solution.py:375
  24.5 3.3 %collective-permute-start.9 = (f32[48,128]{1,0:T(8,128)S(1)}, f32[48,128]{1,0:T(8,128)S(1)}, u32[]{:S(2)}, u32[]{:S(2)}) collective-permute-start(f32[48,128]{1,0:T(8,128)S(1)} %get-tuple-element.67.refs_3_), channel_id=1, source_target_pairs={{0,12},{1,13},{2,14},{3,15},{4,8},{5,9},{6,10},{7,11},{8,4},{9,5},... | collective-permute-start | bytes 73736 | tf_op jit(solution)/shard_map/ppermute | solution.py:375
  27.8 5.1 %collective-permute-start.12 = (f32[48,128]{1,0:T(8,128)S(1)}, f32[48,128]{1,0:T(8,128)S(1)}, u32[]{:S(2)}, u32[]{:S(2)}) collective-permute-start(f32[48,128]{1,0:T(8,128)S(1)} %get-tuple-element.70.refs_3_), channel_id=1, source_target_pairs={{0,7},{1,6},{2,5},{3,4},{4,3},{5,2},{6,1},{7,0},{8,15},{9,14},{10,... | collective-permute-start | bytes 73736 | tf_op jit(solution)/shard_map/ppermute | solution.py:375
  31.2 4.2 %collective-permute-start.13 = (f32[48,128]{1,0:T(8,128)S(1)}, f32[48,128]{1,0:T(8,128)S(1)}, u32[]{:S(2)}, u32[]{:S(2)}) collective-permute-start(f32[48,128]{1,0:T(8,128)S(1)} %get-tuple-element.71), channel_id=1, source_target_pairs={{0,6},{1,7},{2,4},{3,5},{4,2},{5,3},{6,0},{7,1},{8,14},{9,15},{10,... | collective-permute-start | bytes 73736 | tf_op jit(solution)/shard_map/ppermute | solution.py:375
  31.3 4.2 %collective-permute-start.14 = (f32[48,128]{1,0:T(8,128)S(1)}, f32[48,128]{1,0:T(8,128)S(1)}, u32[]{:S(2)}, u32[]{:S(2)}) collective-permute-start(f32[48,128]{1,0:T(8,128)S(1)} %get-tuple-element.72), channel_id=1, source_target_pairs={{0,5},{1,4},{2,7},{3,6},{4,1},{5,0},{6,3},{7,2},{8,13},{9,12},{10,... | collective-permute-start | bytes 73736 | tf_op jit(solution)/shard_map/ppermute | solution.py:375

commit v3 on v2

--- a/solution.py
+++ b/solution.py
@@ -13,6 +13,8 @@
 GROUP = 8
 SCALAR_LANES = (MODES, MODES + 1, GROUP + MODES, GROUP + MODES + 1, 2 * GROUP + MODES)
 OPERATOR_PARTS = 8
+FINAL_PARTS = 4
+DIGIT = 32
 
 HIGHEST = lax.Precision.HIGHEST
 VMEM = pl.BlockSpec(memory_space=pltpu.VMEM)
@@ -30,6 +32,10 @@
     rows = values.shape[0]
     both = lax.dot_general(split(values), matrix, dims, preferred_element_type=jnp.float32)
     return both[:rows] + both[rows:]
+
+
+def small_dot(left, right):
+    return jnp.dot(left, right, precision=HIGHEST, preferred_element_type=jnp.float32)
 
 
 def send_far(values, far_ref, *pair_refs):
@@ -75,8 +81,17 @@
 
 def one_hot(route_ref, peer, per_peer):
     start = pl.multiple_of(peer * per_peer, per_peer)
-    row_ids = lax.broadcasted_iota(jnp.int32, (route_ref.shape[1], per_peer), 0)
-    return jnp.where(row_ids == route_ref[:, pl.ds(start, per_peer)], 1.0, 0.0).astype(jnp.bfloat16)
+    route = route_ref[:, pl.ds(start, per_peer)]
+    shape = (DIGIT, per_peer)
+    low, high = (
+        jnp.broadcast_to(digit.astype(jnp.float32), shape).astype(jnp.bfloat16)
+        for digit in (route % DIGIT, route // DIGIT)
+    )
+    row = lax.broadcasted_iota(jnp.int32, shape, 0).astype(jnp.float32).astype(jnp.bfloat16)
+    zero = jnp.zeros(shape, jnp.bfloat16)
+    match = jnp.where(low == row, jnp.ones(shape, jnp.bfloat16), zero)
+    pieces = [jnp.where(high == piece, match, zero) for piece in range(route_ref.shape[1] // DIGIT)]
+    return jnp.concatenate(pieces, axis=0)
 
 
 def place_kernel(
@@ -294,7 +309,9 @@
     )
 
 
-def final_kernel(terms_ref, basis_ref, jump_ref, multipliers_ref, amplitudes_ref):
+def final_kernel(
+    terms_ref, basis_ref, jump_ref, multipliers_hbm, amplitudes_hbm, multipliers_ref, amplitudes_ref, sems
+):
     coarse = terms_ref.shape[1] // 8
     loads = basis_ref.shape[0] - coarse
     groups = coarse // GROUP
@@ -324,7 +341,7 @@
     amounts = solved[:, 2 * coarse : 2 * coarse + loads]
     inverse_image = solved[:, 2 * coarse + loads : 2 * coarse + 2 * loads]
     inverse = solved[:, 2 * coarse + 2 * loads : 3 * coarse + 2 * loads]
-    products = thin_dot(jnp.concatenate([inverse_h, g_h, z_z, g_dz, z_dz], axis=0), amounts)
+    products = small_dot(jnp.concatenate([inverse_h, g_h, z_z, g_dz, z_dz], axis=0), amounts)
     inverse_h_amounts, h_amounts, z_amounts, g_dz_amounts, z_dz_amounts = (
         products[at * coarse : (at + 1) * coarse] for at in range(5)
     )
@@ -333,7 +350,7 @@
     basis_g, jump_z_rows = basis_ref[loads:], jump_ref[loads:]
     d = basis_ref[:loads] - thin_dot(both[:, :coarse], basis_g)
     u = jump_ref[:loads] - thin_dot(both, jnp.concatenate([jump_z_rows, basis_g], axis=0))
-    products = thin_dot(jnp.concatenate([g_h, z_z], axis=0), shares)
+    products = small_dot(jnp.concatenate([g_h, z_z], axis=0), shares)
     image_d = image_g - h_amounts
     inner = res_res - total(amounts * coarse_res)
     curvature = 2.0 * (res_image - total(amounts * (res_h + image_d)))
@@ -348,20 +365,30 @@
     curvature = grown * grown * curvature - grown * step * (2.0 * d_second + u_u) + 2.0 * step * step * u_second
     second_step = renewed / curvature
     on_d, on_u = step + second_step * grown, second_step * step
-    amplitudes = amounts - on_d * shares + 2.0 * on_u * thin_dot(inverse, second_u)
+    amplitudes = amounts - on_d * shares + 2.0 * on_u * small_dot(inverse, second_u)
     amplitudes_ref[...] = jnp.concatenate(
         [amplitudes[label * GROUP : label * GROUP + MODES] for label in range(groups)], axis=0
     )
+    copies = [pltpu.make_async_copy(amplitudes_ref, amplitudes_hbm, sems.at[0])]
+    copies[0].start()
     weights = jnp.concatenate([on_d, on_u, jnp.zeros((6, loads), jnp.float32)], axis=0).T
-    multipliers_ref[...] = weights[:, 0:1] * d - weights[:, 1:2] * u
-
-
-def call(kernel, shapes, in_specs, name, scratch=(), flops=0):
+    height = loads // FINAL_PARTS
+    for part in range(FINAL_PARTS):
+        rows = pl.ds(part * height, height)
+        here = slice(part * height, (part + 1) * height)
+        multipliers_ref[rows] = weights[here, 0:1] * d[here] - weights[here, 1:2] * u[here]
+        copies.append(pltpu.make_async_copy(multipliers_ref.at[rows], multipliers_hbm.at[rows], sems.at[part + 1]))
+        copies[-1].start()
+    for copy in copies:
+        copy.wait()
+
+
+def call(kernel, shapes, in_specs, name, scratch=(), flops=0, out_spec=VMEM):
     return pl.pallas_call(
         kernel,
         out_shape=[jax.ShapeDtypeStruct(*shape) for shape in shapes],
         in_specs=in_specs,
-        out_specs=[VMEM] * len(shapes),
+        out_specs=[out_spec] * len(shapes),
         scratch_shapes=scratch,
         compiler_params=pltpu.CompilerParams(vmem_limit_bytes=24 * 1024 * 1024),
         cost_estimate=pl.CostEstimate(flops=flops, bytes_accessed=2**20, transcendentals=0),
@@ -461,8 +488,14 @@
     jump, terms = call(second_kernel, [tall, wide], [VMEM] * (8 + len(got)), "second")(
         slots, placed, basis, half_jump, half_second, terms, got_near, near, *image_send
     )
+    outputs = [((loads, rows), f32), ((MODES * groups, loads), f32)]
     multipliers, amplitudes = call(
-        final_kernel, [((loads, rows), f32), ((MODES * groups, loads), f32)], [VMEM] * 3, "final"
+        final_kernel,
+        outputs,
+        [VMEM] * 3,
+        "final",
+        [*(pltpu.VMEM(*output) for output in outputs), pltpu.SemaphoreType.DMA((FINAL_PARTS + 1,))],
+        out_spec=HBM,
     )(total(terms), basis, jump)
     return multipliers, amplitudes.T
 

time: 37.9 us -> 37.9 us (level)
  waiting for transfers between devices: 9.96 us -> 10.4 us
  starting transfers between devices: 15.6 us -> 15.2 us
    ppermute x15, waiting for transfers between devices: 9.96 us -> 10.4 us  [permute(): lax.ppermute(values, ('sub', 'rep'), [(at, at ^ offset) for at in range(p...]
  transfers between devices with their start and end apart: 15 -> 15, of which waited for: 12 -> 11; matrix products, arithmetic and copies ran while one was open for 0% -> 0% of each run, Pallas kernels for 14% -> 14%
where the time goes in v3:
time: 37.9 us; the launch traced here: 37.7 us
  starting transfers between devices  15.2 us (40%)
  Pallas kernels  11.3 us (30%)
  waiting for transfers between devices  10.4 us (27%)
  between operations  0.76 us (2%)
    ppermute x15, starting transfers between devices, permute(): lax.ppermute(values, ('sub', 'rep'), [(at, at ^ offset) for at in range(p...  15.2 us
    ppermute x15, waiting for transfers between devices, permute(): lax.ppermute(values, ('sub', 'rep'), [(at, at ^ offset) for at in range(p...  10.4 us
    pallas_call x1, Pallas kernels, fused_body(): call(ready_kernel, [((rows, 3 * per_peer), jnp.bfloat16), halves, halves,...  2.88 us
    pallas_call x1, Pallas kernels, fused_body(): call(final_kernel, outputs, [VMEM] * 3, 'final', [*(pltpu.VMEM(*output) f...  2.31 us
    pallas_call x1, Pallas kernels, fused_body(): call(place_kernel, [((rows, rows - 2 * per_peer), jnp.bfloat16), ((short,...  1.72 us
    pallas_call x1, Pallas kernels, fused_body(): call(second_kernel, [tall, wide], [VMEM] * (8 + len(got)), 'second')  1.22 us
    pallas_call x1, Pallas kernels, fused_body(): call(middle_kernel, [tall, wide, *singles(height)], [VMEM] * 5, 'middle',...  1.2 us
    pallas_call x1, Pallas kernels, fused_body(): call(first_kernel, [half, tall, *pairs(height)], [VMEM] * (5 + len(send))...  0.79 us
  transfers between devices with their start and end apart: 15, of which 11 were waited for; matrix products, arithmetic and copies ran while one was open for 0% of the time, Pallas kernels for 14%

profile of v3, /device:TPU:0, one launch (start us, length us, event | category | flops | bytes accessed | tf_op | source)
XLA Modules:
  0.0 37.7 jit_solution(4747923047263571672)
XLA Ops:
  0.6 1.7 %place.1 = (bf16[1024,768]{1,0:T(8,128)(2,1)S(1)}, f32[40,1024]{1,0:T(8,128)S(1)}, bf16[1,1024,1024]{2,1,0:T(8,128)(2,1)S(1)}, s32[1,1024]{1,0:T(1,128)S(1)}, f3...) custom-call(s32[1,1024]{1,0:T(1,128)} %route_hbm.1, s32[1,32]{1,0:T(1,128)} %bitcast.4, ...), custom_call_target="tpu_custom_call" | custom-call | bytes 1048576 | tf_op jit(solution)/shard_map/place/pallas_call | solution.py:450
  2.4 3.4 %collective-permute-start = (f32[80,128]{1,0:T(8,128)S(1)}, f32[80,128]{1,0:T(8,128)S(1)}, u32[]{:S(2)}, u32[]{:S(2)}) collective-permute-start(f32[80,128]{1,0:T(8,128)S(1)} %get-tuple-element.48.refs_0_), channel_id=1, source_target_pairs={{0,28},{1,29},{2,30},{3,31},{4,24},{5,25},{6,26},{7,27},{8,20},{9,... | collective-permute-start | bytes 122888 | tf_op jit(solution)/shard_map/ppermute | solution.py:402
  5.8 0.8 %collective-permute-start.1 = (f32[80,128]{1,0:T(8,128)S(1)}, f32[80,128]{1,0:T(8,128)S(1)}, u32[]{:S(2)}, u32[]{:S(2)}) collective-permute-start(f32[80,128]{1,0:T(8,128)S(1)} %get-tuple-element.49.refs_1_), channel_id=1, source_target_pairs={{0,20},{1,21},{2,22},{3,23},{4,16},{5,17},{6,18},{7,19},{8,28},{9,... | collective-permute-start | bytes 122888 | tf_op jit(solution)/shard_map/ppermute | solution.py:402
  6.5 0.1 collective-permute-start.2
  6.7 2.9 %ready.1 = (bf16[1024,384]{1,0:T(8,128)(2,1)S(1)}, bf16[2,1024,512]{2,1,0:T(8,128)(2,1)S(1)}, bf16[2,1024,512]{2,1,0:T(8,128)(2,1)S(1)}, f32[40,128]{1,0:T(8,128...) custom-call(s32[1,1024]{1,0:T(1,128)S(1)} %get-tuple-element.39.route_ref, ...), custom_call_target="tpu_custom_call" | custom-call | flops 2147483648 | bytes 1048576 | tf_op jit(solution)/shard_map/ready/pallas_call | solution.py:465
  9.6 0.0 collective-permute-done.refs_3_
  9.6 0.0 collective-permute-done.1.refs_4_
  9.6 0.7 %collective-permute-done.2.refs_5_ = f32[80,128]{1,0:T(8,128)S(1)} collective-permute-done((f32[80,128]{1,0:T(8,128)S(1)}, f32[80,128]{1,0:T(8,128)S(1)}, u32[]{:S(2)}, u32[]{:S(2)}) %collective-permute-start.2) | collective-permute-done | bytes 40992 | tf_op jit(solution)/shard_map/ppermute | solution.py:402
  10.4 0.2 collective-permute-start.3
  10.5 0.4 %first_half.1 = (f32[48,512]{1,0:T(8,128)S(1)}, f32[48,1024]{1,0:T(8,128)S(1)}) custom-call(bf16[2,1024,512]{2,1,0:T(8,128)(2,1)S(1)} %get-tuple-element.44.placed_ref, f32[40,128]{1,0:T(8,128)S(1)} %get-tuple-element.46.stay_ref, f32[40,128]{1,0:T(8,128)S(1)} %get-tuple-element.47.back_ref, f32[80,128]{1,0:T(8,128)S(1)} %get-tuple-element.48.refs_0_, ...), custom_call_target="tpu_custom_call" | custom-call | flops 100663296 | bytes 1048576 | tf_op jit(solution)/shard_map/first_half/pallas_call | solution.py:474
  11.0 0.7 %collective-permute-done.3.got_ref = f32[160,128]{1,0:T(8,128)S(1)} collective-permute-done((f32[160,128]{1,0:T(8,128)S(1)}, f32[160,128]{1,0:T(8,128)S(1)}, u32[]{:S(2)}, u32[]{:S(2)}) %collective-permute-start.3) | collective-permute-done | bytes 81952 | tf_op jit(solution)/shard_map/ppermute | solution.py:402
  11.7 0.8 %first.1 = (f32[48,512]{1,0:T(8,128)S(1)}, f32[48,1024]{1,0:T(8,128)S(1)}, f32[96,128]{1,0:T(8,128)S(1)}, f32[96,128]{1,0:T(8,128)S(1)}, f32[96,128]{1,0:T(8,128)S(1)}) custom-call(bf16[1024,768]{1,0:T(8,128)(2,1)S(1)} %get-tuple-element.40.far_ref, bf16[2,1024,512]{2,1,0:T(8,128)(2,1)S(1)} %get-tuple-element.44.placed_ref, ...), custom_call_target="tpu_custom_call" | custom-call | bytes 1048576 | tf_op jit(solution)/shard_map/first/pallas_call | solution.py:477
  12.5 1.9 %collective-permute-start.4 = (f32[96,128]{1,0:T(8,128)S(1)}, f32[96,128]{1,0:T(8,128)S(1)}, u32[]{:S(2)}, u32[]{:S(2)}) collective-permute-start(f32[96,128]{1,0:T(8,128)S(1)} %get-tuple-element.59.refs_0_), channel_id=1, source_target_pairs={{0,28},{1,29},{2,30},{3,31},{4,24},{5,25},{6,26},{7,27},{8,20},{9,... | collective-permute-start | bytes 147464 | tf_op jit(solution)/shard_map/ppermute | solution.py:402
  14.4 0.3 collective-permute-start.5
  14.6 0.8 %collective-permute-start.6 = (f32[96,128]{1,0:T(8,128)S(1)}, f32[96,128]{1,0:T(8,128)S(1)}, u32[]{:S(2)}, u32[]{:S(2)}) collective-permute-start(f32[96,128]{1,0:T(8,128)S(1)} %get-tuple-element.61.refs_2_), channel_id=1, source_target_pairs={{0,12},{1,13},{2,14},{3,15},{4,8},{5,9},{6,10},{7,11},{8,4},{9,5},... | collective-permute-start | bytes 147464 | tf_op jit(solution)/shard_map/ppermute | solution.py:402
  15.5 1.2 %middle.1 = (f32[48,1024]{1,0:T(8,128)S(1)}, f32[48,128]{1,0:T(8,128)S(1)}, f32[48,128]{1,0:T(8,128)S(1)}, f32[48,128]{1,0:T(8,128)S(1)}, f32[48,128]{1,0:T(8,128)S(1)}) custom-call(bf16[1024,384]{1,0:T(8,128)(2,1)S(1)} %get-tuple-element.45.edge_ref, bf16[2,1024,512]{2,1,0:T(8,128)(2,1)S(1)} %get-tuple-element.43.slots_ref, ...), custom_call_target="tpu_custom_call" | custom-call | flops 201326592 | bytes 1048576 | tf_op jit(solution)/shard_map/middle/pallas_call | solution.py:481
  16.7 0.4 %collective-permute-done.4.refs_3_ = f32[96,128]{1,0:T(8,128)S(1)} collective-permute-done((f32[96,128]{1,0:T(8,128)S(1)}, f32[96,128]{1,0:T(8,128)S(1)}, u32[]{:S(2)}, u32[]{:S(2)}) %collective-permute-start.4) | collective-permute-done | bytes 49184 | tf_op jit(solution)/shard_map/ppermute | solution.py:402
  17.1 1.1 %collective-permute-done.5.refs_4_ = f32[96,128]{1,0:T(8,128)S(1)} collective-permute-done((f32[96,128]{1,0:T(8,128)S(1)}, f32[96,128]{1,0:T(8,128)S(1)}, u32[]{:S(2)}, u32[]{:S(2)}) %collective-permute-start.5) | collective-permute-done | bytes 49184 | tf_op jit(solution)/shard_map/ppermute | solution.py:402
  18.3 0.0 collective-permute-done.6.refs_5_
  18.3 0.3 collective-permute-start.7
  18.6 0.7 %second_half.1 = (f32[48,1024]{1,0:T(8,128)S(1)}, f32[48,1024]{1,0:T(8,128)S(1)}) custom-call(bf16[2,1024,512]{2,1,0:T(8,128)(2,1)S(1)} %get-tuple-element.43.slots_ref, bf16[2,1024,512]{2,1,0:T(8,128)(2,1)S(1)} %get-tuple-element.44.placed_ref, f32[48,128]{1,0:T(8,128)S(1)} %get-tuple-element.57.stay_ref, f32[48,128]{1,0:T(8,128)S(1)} %get-tuple-element.58.back_ref, ...), custom_call_target="tpu_custom_call" | custom-call | flops 201326592 | bytes 1048576 | tf_op jit(solution)/shard_map/second_half/pallas_call | solution.py:485
  19.3 0.3 collective-permute-done.7.got_ref
  19.6 1.2 %second.1 = (f32[48,1024]{1,0:T(8,128)S(1)}, f32[48,128]{1,0:T(8,128)S(1)}) custom-call(bf16[2,1024,512]{2,1,0:T(8,128)(2,1)S(1)} %get-tuple-element.43.slots_ref, bf16[2,1024,512]{2,1,0:T(8,128)(2,1)S(1)} %get-tuple-element.44.placed_ref, f32[48,1024]{1,0:T(8,128)S(1)} %get-tuple-element.56.basis_ref, f32[48,1024]{1,0:T(8,128)S(1)} %get-tuple-element.62.half_jump_ref, ...), custom_call_target="tpu_custom_call" | custom-call | bytes 1048576 | tf_op jit(solution)/shard_map/second/pallas_call | solution.py:488
  20.9 0.3 collective-permute-start.8
  21.2 1.0 %collective-permute-done.8.refs_0_ = f32[48,128]{1,0:T(8,128)S(1)} collective-permute-done((f32[48,128]{1,0:T(8,128)S(1)}, f32[48,128]{1,0:T(8,128)S(1)}, u32[]{:S(2)}, u32[]{:S(2)}) %collective-permute-start.8) | collective-permute-done | bytes 24608 | tf_op jit(solution)/shard_map/ppermute | solution.py:402
  22.1 2.0 %collective-permute-start.10 = (f32[48,128]{1,0:T(8,128)S(1)}, f32[48,128]{1,0:T(8,128)S(1)}, u32[]{:S(2)}, u32[]{:S(2)}) collective-permute-start(f32[48,128]{1,0:T(8,128)S(1)} %get-tuple-element.68), channel_id=1, source_target_pairs={{0,28},{1,29},{2,30},{3,31},{4,24},{5,25},{6,26},{7,27},{8,20},{9,... | collective-permute-start | bytes 73736 | tf_op jit(solution)/shard_map/ppermute | solution.py:402
  24.1 0.4 %collective-permute-start.11 = (f32[48,128]{1,0:T(8,128)S(1)}, f32[48,128]{1,0:T(8,128)S(1)}, u32[]{:S(2)}, u32[]{:S(2)}) collective-permute-start(f32[48,128]{1,0:T(8,128)S(1)} %get-tuple-element.69), channel_id=1, source_target_pairs={{0,20},{1,21},{2,22},{3,23},{4,16},{5,17},{6,18},{7,19},{8,28},{9,... | collective-permute-start | bytes 73736 | tf_op jit(solution)/shard_map/ppermute | solution.py:402
  24.5 0.7 %collective-permute-start.9 = (f32[48,128]{1,0:T(8,128)S(1)}, f32[48,128]{1,0:T(8,128)S(1)}, u32[]{:S(2)}, u32[]{:S(2)}) collective-permute-start(f32[48,128]{1,0:T(8,128)S(1)} %get-tuple-element.67.refs_3_), channel_id=1, source_target_pairs={{0,12},{1,13},{2,14},{3,15},{4,8},{5,9},{6,10},{7,11},{8,4},{9,5},... | collective-permute-start | bytes 73736 | tf_op jit(solution)/shard_map/ppermute | solution.py:402
  25.3 1.1 %collective-permute-done.10.refs_1_ = f32[48,128]{1,0:T(8,128)S(1)} collective-permute-done((f32[48,128]{1,0:T(8,128)S(1)}, f32[48,128]{1,0:T(8,128)S(1)}, u32[]{:S(2)}, u32[]{:S(2)}) %collective-permute-start.10) | collective-permute-done | bytes 24608 | tf_op jit(solution)/shard_map/ppermute | solution.py:402
  26.4 1.0 %collective-permute-done.11.refs_2_ = f32[48,128]{1,0:T(8,128)S(1)} collective-permute-done((f32[48,128]{1,0:T(8,128)S(1)}, f32[48,128]{1,0:T(8,128)S(1)}, u32[]{:S(2)}, u32[]{:S(2)}) %collective-permute-start.11) | collective-permute-done | bytes 24608 | tf_op jit(solution)/shard_map/ppermute | solution.py:402
  27.4 0.4 %collective-permute-done.9.refs_0_ = f32[48,128]{1,0:T(8,128)S(1)} collective-permute-done((f32[48,128]{1,0:T(8,128)S(1)}, f32[48,128]{1,0:T(8,128)S(1)}, u32[]{:S(2)}, u32[]{:S(2)}) %collective-permute-start.9) | collective-permute-done | bytes 24608 | tf_op jit(solution)/shard_map/ppermute | solution.py:402
  27.8 3.4 %collective-permute-start.12 = (f32[48,128]{1,0:T(8,128)S(1)}, f32[48,128]{1,0:T(8,128)S(1)}, u32[]{:S(2)}, u32[]{:S(2)}) collective-permute-start(f32[48,128]{1,0:T(8,128)S(1)} %get-tuple-element.70.refs_3_), channel_id=1, source_target_pairs={{0,7},{1,6},{2,5},{3,4},{4,3},{5,2},{6,1},{7,0},{8,15},{9,14},{10,... | collective-permute-start | bytes 73736 | tf_op jit(solution)/shard_map/ppermute | solution.py:402
  31.2 0.0 collective-permute-start.13
  31.3 0.6 %collective-permute-start.14 = (f32[48,128]{1,0:T(8,128)S(1)}, f32[48,128]{1,0:T(8,128)S(1)}, u32[]{:S(2)}, u32[]{:S(2)}) collective-permute-start(f32[48,128]{1,0:T(8,128)S(1)} %get-tuple-element.72), channel_id=1, source_target_pairs={{0,5},{1,4},{2,7},{3,6},{4,1},{5,0},{6,3},{7,2},{8,13},{9,12},{10,... | collective-permute-start | bytes 73736 | tf_op jit(solution)/shard_map/ppermute | solution.py:402
  31.8 1.1 %collective-permute-done.12.refs_0_ = f32[48,128]{1,0:T(8,128)S(1)} collective-permute-done((f32[48,128]{1,0:T(8,128)S(1)}, f32[48,128]{1,0:T(8,128)S(1)}, u32[]{:S(2)}, u32[]{:S(2)}) %collective-permute-start.12) | collective-permute-done | bytes 24608 | tf_op jit(solution)/shard_map/ppermute | solution.py:402
  32.9 2.5 %collective-permute-done.13.refs_1_ = f32[48,128]{1,0:T(8,128)S(1)} collective-permute-done((f32[48,128]{1,0:T(8,128)S(1)}, f32[48,128]{1,0:T(8,128)S(1)}, u32[]{:S(2)}, u32[]{:S(2)}) %collective-permute-start.13) | collective-permute-done | bytes 24608 | tf_op jit(solution)/shard_map/ppermute | solution.py:402
  35.4 0.0 collective-permute-done.14.refs_2_
  35.4 2.3 %final.1 = (f32[32,1024]{1,0:T(8,128)}, f32[12,32]{1,0:T(8,128)}) custom-call(f32[48,128]{1,0:T(8,128)S(1)} %sum.5.terms_ref, f32[48,1024]{1,0:T(8,128)S(1)} %get-tuple-element.56.basis_ref, f32[48,1024]{1,0:T(8,128)S(1)} %get-tuple-element.73.jump_ref), custom_call_target="tpu_custom_call" | custom-call | bytes 1048576 | tf_op jit(solution)/shard_map/final/pallas_call | solution.py:492
  (11 shorter events, 0.1 us)
Async XLA Ops:
  2.4 7.2 %collective-permute-start = (f32[80,128]{1,0:T(8,128)S(1)}, f32[80,128]{1,0:T(8,128)S(1)}, u32[]{:S(2)}, u32[]{:S(2)}) collective-permute-start(f32[80,128]{1,0:T(8,128)S(1)} %get-tuple-element.48.refs_0_), channel_id=1, source_target_pairs={{0,28},{1,29},{2,30},{3,31},{4,24},{5,25},{6,26},{7,27},{8,20},{9,... | collective-permute-start | bytes 122888 | tf_op jit(solution)/shard_map/ppermute | solution.py:402
  5.8 3.8 %collective-permute-start.1 = (f32[80,128]{1,0:T(8,128)S(1)}, f32[80,128]{1,0:T(8,128)S(1)}, u32[]{:S(2)}, u32[]{:S(2)}) collective-permute-start(f32[80,128]{1,0:T(8,128)S(1)} %get-tuple-element.49.refs_1_), channel_id=1, source_target_pairs={{0,20},{1,21},{2,22},{3,23},{4,16},{5,17},{6,18},{7,19},{8,28},{9,... | collective-permute-start | bytes 122888 | tf_op jit(solution)/shard_map/ppermute | solution.py:402
  6.5 3.8 %collective-permute-start.2 = (f32[80,128]{1,0:T(8,128)S(1)}, f32[80,128]{1,0:T(8,128)S(1)}, u32[]{:S(2)}, u32[]{:S(2)}) collective-permute-start(f32[80,128]{1,0:T(8,128)S(1)} %get-tuple-element.50.refs_2_), channel_id=1, source_target_pairs={{0,12},{1,13},{2,14},{3,15},{4,8},{5,9},{6,10},{7,11},{8,4},{9,5},... | collective-permute-start | bytes 122888 | tf_op jit(solution)/shard_map/ppermute | solution.py:402
  10.4 1.3 %collective-permute-start.3 = (f32[160,128]{1,0:T(8,128)S(1)}, f32[160,128]{1,0:T(8,128)S(1)}, u32[]{:S(2)}, u32[]{:S(2)}) collective-permute-start(f32[160,128]{1,0:T(8,128)S(1)} %pad_maximum_fusion.1), channel_id=1, source_target_pairs={{0,4},{1,5},{2,6},{3,7},{4,0},{5,1},{6,2},{7,3},{8,12},{9,13},{10,... | collective-permute-start | bytes 245768 | tf_op jit(solution)/shard_map/ppermute | solution.py:402
  12.5 4.6 %collective-permute-start.4 = (f32[96,128]{1,0:T(8,128)S(1)}, f32[96,128]{1,0:T(8,128)S(1)}, u32[]{:S(2)}, u32[]{:S(2)}) collective-permute-start(f32[96,128]{1,0:T(8,128)S(1)} %get-tuple-element.59.refs_0_), channel_id=1, source_target_pairs={{0,28},{1,29},{2,30},{3,31},{4,24},{5,25},{6,26},{7,27},{8,20},{9,... | collective-permute-start | bytes 147464 | tf_op jit(solution)/shard_map/ppermute | solution.py:402
  14.4 3.9 %collective-permute-start.5 = (f32[96,128]{1,0:T(8,128)S(1)}, f32[96,128]{1,0:T(8,128)S(1)}, u32[]{:S(2)}, u32[]{:S(2)}) collective-permute-start(f32[96,128]{1,0:T(8,128)S(1)} %get-tuple-element.60.refs_1_), channel_id=1, source_target_pairs={{0,20},{1,21},{2,22},{3,23},{4,16},{5,17},{6,18},{7,19},{8,28},{9,... | collective-permute-start | bytes 147464 | tf_op jit(solution)/shard_map/ppermute | solution.py:402
  14.6 3.6 %collective-permute-start.6 = (f32[96,128]{1,0:T(8,128)S(1)}, f32[96,128]{1,0:T(8,128)S(1)}, u32[]{:S(2)}, u32[]{:S(2)}) collective-permute-start(f32[96,128]{1,0:T(8,128)S(1)} %get-tuple-element.61.refs_2_), channel_id=1, source_target_pairs={{0,12},{1,13},{2,14},{3,15},{4,8},{5,9},{6,10},{7,11},{8,4},{9,5},... | collective-permute-start | bytes 147464 | tf_op jit(solution)/shard_map/ppermute | solution.py:402
  18.3 1.4 %collective-permute-start.7 = (f32[192,128]{1,0:T(8,128)S(1)}, f32[192,128]{1,0:T(8,128)S(1)}, u32[]{:S(2)}, u32[]{:S(2)}) collective-permute-start(f32[192,128]{1,0:T(8,128)S(1)} %pad_maximum_fusion), channel_id=1, source_target_pairs={{0,4},{1,5},{2,6},{3,7},{4,0},{5,1},{6,2},{7,3},{8,12},{9,13},{10,... | collective-permute-start | bytes 294920 | tf_op jit(solution)/shard_map/ppermute | solution.py:402
  20.9 1.3 %collective-permute-start.8 = (f32[48,128]{1,0:T(8,128)S(1)}, f32[48,128]{1,0:T(8,128)S(1)}, u32[]{:S(2)}, u32[]{:S(2)}) collective-permute-start(f32[48,128]{1,0:T(8,128)S(1)} %get-tuple-element.66.refs_1_), channel_id=1, source_target_pairs={{0,4},{1,5},{2,6},{3,7},{4,0},{5,1},{6,2},{7,3},{8,12},{9,13},{10,... | collective-permute-start | bytes 73736 | tf_op jit(solution)/shard_map/ppermute | solution.py:402
  22.1 4.2 %collective-permute-start.10 = (f32[48,128]{1,0:T(8,128)S(1)}, f32[48,128]{1,0:T(8,128)S(1)}, u32[]{:S(2)}, u32[]{:S(2)}) collective-permute-start(f32[48,128]{1,0:T(8,128)S(1)} %get-tuple-element.68), channel_id=1, source_target_pairs={{0,28},{1,29},{2,30},{3,31},{4,24},{5,25},{6,26},{7,27},{8,20},{9,... | collective-permute-start | bytes 73736 | tf_op jit(solution)/shard_map/ppermute | solution.py:402
  24.1 3.3 %collective-permute-start.11 = (f32[48,128]{1,0:T(8,128)S(1)}, f32[48,128]{1,0:T(8,128)S(1)}, u32[]{:S(2)}, u32[]{:S(2)}) collective-permute-start(f32[48,128]{1,0:T(8,128)S(1)} %get-tuple-element.69), channel_id=1, source_target_pairs={{0,20},{1,21},{2,22},{3,23},{4,16},{5,17},{6,18},{7,19},{8,28},{9,... | collective-permute-start | bytes 73736 | tf_op jit(solution)/shard_map/ppermute | solution.py:402
  24.5 3.3 %collective-permute-start.9 = (f32[48,128]{1,0:T(8,128)S(1)}, f32[48,128]{1,0:T(8,128)S(1)}, u32[]{:S(2)}, u32[]{:S(2)}) collective-permute-start(f32[48,128]{1,0:T(8,128)S(1)} %get-tuple-element.67.refs_3_), channel_id=1, source_target_pairs={{0,12},{1,13},{2,14},{3,15},{4,8},{5,9},{6,10},{7,11},{8,4},{9,5},... | collective-permute-start | bytes 73736 | tf_op jit(solution)/shard_map/ppermute | solution.py:402
  27.8 5.1 %collective-permute-start.12 = (f32[48,128]{1,0:T(8,128)S(1)}, f32[48,128]{1,0:T(8,128)S(1)}, u32[]{:S(2)}, u32[]{:S(2)}) collective-permute-start(f32[48,128]{1,0:T(8,128)S(1)} %get-tuple-element.70.refs_3_), channel_id=1, source_target_pairs={{0,7},{1,6},{2,5},{3,4},{4,3},{5,2},{6,1},{7,0},{8,15},{9,14},{10,... | collective-permute-start | bytes 73736 | tf_op jit(solution)/shard_map/ppermute | solution.py:402
  31.2 4.2 %collective-permute-start.13 = (f32[48,128]{1,0:T(8,128)S(1)}, f32[48,128]{1,0:T(8,128)S(1)}, u32[]{:S(2)}, u32[]{:S(2)}) collective-permute-start(f32[48,128]{1,0:T(8,128)S(1)} %get-tuple-element.71), channel_id=1, source_target_pairs={{0,6},{1,7},{2,4},{3,5},{4,2},{5,3},{6,0},{7,1},{8,14},{9,15},{10,... | collective-permute-start | bytes 73736 | tf_op jit(solution)/shard_map/ppermute | solution.py:402
  31.3 4.2 %collective-permute-start.14 = (f32[48,128]{1,0:T(8,128)S(1)}, f32[48,128]{1,0:T(8,128)S(1)}, u32[]{:S(2)}, u32[]{:S(2)}) collective-permute-start(f32[48,128]{1,0:T(8,128)S(1)} %get-tuple-element.72), channel_id=1, source_target_pairs={{0,5},{1,4},{2,7},{3,6},{4,1},{5,0},{6,3},{7,2},{8,13},{9,12},{10,... | collective-permute-start | bytes 73736 | tf_op jit(solution)/shard_map/ppermute | solution.py:402

commit v4 on v3

--- a/solution.py
+++ b/solution.py
@@ -104,6 +104,7 @@
     peers = rows // per_peer
     height = rows // OPERATOR_PARTS
     parts = [pl.ds(start, height) for start in range(0, rows, height)]
+    gap_parts = [pl.ds(start, GROUP) for start in range(0, loads, GROUP)]
     copies = [
         pltpu.make_async_copy(source, target, sems.at[at])
         for at, (source, target) in enumerate(
@@ -111,7 +112,7 @@
                 (route_hbm, route_ref),
                 (block_hbm, block_ref),
                 (traces_hbm, traces_ref),
-                (gap_hbm, values_ref.at[pl.ds(0, loads)]),
+                *((gap_hbm.at[part], values_ref.at[part]) for part in gap_parts),
                 *((operator_hbm.at[:, part], operator_ref.at[:, part]) for part in parts),
             )
         )
@@ -139,11 +140,12 @@
         values_ref[loads + mode : loads + mode + 1] = traces_ref[mode]
     values_ref[loads + modes : loads + modes + 1] = label
     values_ref[loads + modes + 1 :] = jnp.zeros((GROUP - modes - 1, rows), jnp.float32)
-    copies[3].wait()
+    for copy in copies[3 : 3 + len(gap_parts)]:
+        copy.wait()
     for at in range(peers - 4, peers - 2):
         build(at)
     send_far(values_ref[...], far_ref, *pair_refs)
-    for copy in copies[4:]:
+    for copy in copies[3 + len(gap_parts) :]:
         copy.wait()
 
 
@@ -274,6 +276,13 @@
         ref[...] = parts[0]
 
 
+def inverse_of(value):
+    guess = pl.reciprocal(value, approx=True)
+    for _ in range(2):
+        guess = guess * (2.0 - value * guess)
+    return guess
+
+
 def eliminate(work, coarse):
     row = lax.broadcasted_iota(jnp.int32, work.shape, 0)
     for start in range(0, coarse, GROUP):
@@ -282,7 +291,7 @@
         square = [[column[pivot : pivot + 1] for column in columns] for pivot in pivots]
         rows = [work[pivot : pivot + 1] for pivot in pivots]
         for at in range(MODES):
-            scale = 1.0 / square[at][at]
+            scale = inverse_of(square[at][at])
             rows[at] = rows[at] * scale
             square[at] = [value * scale for value in square[at]]
             for other in range(MODES):
@@ -359,11 +368,11 @@
     jump_u = second_z - z_dz_amounts - 0.5 * products[coarse:]
     d_second = res_second - total(amounts * (res_dz + second_u) + shares * res_h)
     u_second = jump_second - total(amounts * (jump_dz + jump_u) + shares * (0.5 * jump_z + second_u))
-    step = inner / curvature
+    step = inner * inverse_of(curvature)
     renewed = step * step * u_u - inner
-    grown = 1.0 + renewed / inner
+    grown = 1.0 + renewed * inverse_of(inner)
     curvature = grown * grown * curvature - grown * step * (2.0 * d_second + u_u) + 2.0 * step * step * u_second
-    second_step = renewed / curvature
+    second_step = renewed * inverse_of(curvature)
     on_d, on_u = step + second_step * grown, second_step * step
     amplitudes = amounts - on_d * shares + 2.0 * on_u * small_dot(inverse, second_u)
     amplitudes_ref[...] = jnp.concatenate(
@@ -414,6 +423,7 @@
     chips = [(offset + 1, 0) for offset in reversed(range(2, lax.axis_size("sub"), 2))]
     chips = chips[-1:] + chips[:-1]
     planes = [(1, offset) for offset in reversed(range(1, lax.axis_size("rep")))]
+    planes[:2] = planes[1::-1]
     copies = [terms]
     for offsets, following in (([(1, 0)], len(chips)), (chips, len(planes)), (planes, 1)):
         parts = [permute(copy, *offset) for copy, offset in zip(copies, offsets)]
@@ -458,7 +468,7 @@
         ],
         [HBM] * 5,
         "place",
-        [pltpu.VMEM((1, subs), i32), pltpu.VMEM((modes, 1, rows), f32), pltpu.SemaphoreType.DMA((4 + OPERATOR_PARTS,))],
+        [pltpu.VMEM((1, subs), i32), pltpu.VMEM((modes, 1, rows), f32), pltpu.SemaphoreType.DMA((3 + loads // GROUP + OPERATOR_PARTS,))],
     )(*(held(value) for value in inputs))
     got = to_chips(*send)
     halves = ((2, rows, rows // 2), dual_ops.dtype)

time: 37.9 us -> 38 us (level)
  no operation moved by 1% of the time
where the time goes in v4:
time: 38 us; the launch traced here: 37.8 us
  starting transfers between devices  15.2 us (40%)
  Pallas kernels  11.4 us (30%)
  waiting for transfers between devices  10.5 us (28%)
  between operations  0.76 us (2%)
    ppermute x15, starting transfers between devices, permute(): lax.ppermute(values, ('sub', 'rep'), [(at, at ^ offset) for at in range(p...  15.2 us
    ppermute x15, waiting for transfers between devices, permute(): lax.ppermute(values, ('sub', 'rep'), [(at, at ^ offset) for at in range(p...  10.5 us
    pallas_call x1, Pallas kernels, fused_body(): call(ready_kernel, [((rows, 3 * per_peer), jnp.bfloat16), halves, halves,...  2.88 us
    pallas_call x1, Pallas kernels, fused_body(): call(final_kernel, outputs, [VMEM] * 3, 'final', [*(pltpu.VMEM(*output) f...  2.36 us
    pallas_call x1, Pallas kernels, fused_body(): call(place_kernel, [((rows, rows - 2 * per_peer), jnp.bfloat16), ((short,...  1.76 us
    pallas_call x1, Pallas kernels, fused_body(): call(second_kernel, [tall, wide], [VMEM] * (8 + len(got)), 'second')  1.22 us
    pallas_call x1, Pallas kernels, fused_body(): call(middle_kernel, [tall, wide, *singles(height)], [VMEM] * 5, 'middle',...  1.2 us
    pallas_call x1, Pallas kernels, fused_body(): call(first_kernel, [half, tall, *pairs(height)], [VMEM] * (5 + len(send))...  0.79 us
  transfers between devices with their start and end apart: 15, of which 11 were waited for; matrix products, arithmetic and copies ran while one was open for 0% of the time, Pallas kernels for 14%

profile of v4, /device:TPU:0, one launch (start us, length us, event | category | flops | bytes accessed | tf_op | source)
XLA Modules:
  0.0 37.8 jit_solution(10357062089571931974)
XLA Ops:
  0.6 1.8 %place.1 = (bf16[1024,768]{1,0:T(8,128)(2,1)S(1)}, f32[40,1024]{1,0:T(8,128)S(1)}, bf16[1,1024,1024]{2,1,0:T(8,128)(2,1)S(1)}, s32[1,1024]{1,0:T(1,128)S(1)}, f3...) custom-call(s32[1,1024]{1,0:T(1,128)} %route_hbm.1, s32[1,32]{1,0:T(1,128)} %bitcast.4, ...), custom_call_target="tpu_custom_call" | custom-call | bytes 1048576 | tf_op jit(solution)/shard_map/place/pallas_call | solution.py:460
  2.4 3.4 %collective-permute-start = (f32[80,128]{1,0:T(8,128)S(1)}, f32[80,128]{1,0:T(8,128)S(1)}, u32[]{:S(2)}, u32[]{:S(2)}) collective-permute-start(f32[80,128]{1,0:T(8,128)S(1)} %get-tuple-element.48.refs_0_), channel_id=1, source_target_pairs={{0,28},{1,29},{2,30},{3,31},{4,24},{5,25},{6,26},{7,27},{8,20},{9,... | collective-permute-start | bytes 122888 | tf_op jit(solution)/shard_map/ppermute | solution.py:411
  5.8 0.8 %collective-permute-start.1 = (f32[80,128]{1,0:T(8,128)S(1)}, f32[80,128]{1,0:T(8,128)S(1)}, u32[]{:S(2)}, u32[]{:S(2)}) collective-permute-start(f32[80,128]{1,0:T(8,128)S(1)} %get-tuple-element.49.refs_1_), channel_id=1, source_target_pairs={{0,20},{1,21},{2,22},{3,23},{4,16},{5,17},{6,18},{7,19},{8,28},{9,... | collective-permute-start | bytes 122888 | tf_op jit(solution)/shard_map/ppermute | solution.py:411
  6.6 0.1 collective-permute-start.2
  6.7 2.9 %ready.1 = (bf16[1024,384]{1,0:T(8,128)(2,1)S(1)}, bf16[2,1024,512]{2,1,0:T(8,128)(2,1)S(1)}, bf16[2,1024,512]{2,1,0:T(8,128)(2,1)S(1)}, f32[40,128]{1,0:T(8,128...) custom-call(s32[1,1024]{1,0:T(1,128)S(1)} %get-tuple-element.39.route_ref, ...), custom_call_target="tpu_custom_call" | custom-call | flops 2147483648 | bytes 1048576 | tf_op jit(solution)/shard_map/ready/pallas_call | solution.py:475
  9.6 0.0 collective-permute-done.refs_3_
  9.6 0.0 collective-permute-done.1.refs_4_
  9.7 0.7 %collective-permute-done.2.refs_5_ = f32[80,128]{1,0:T(8,128)S(1)} collective-permute-done((f32[80,128]{1,0:T(8,128)S(1)}, f32[80,128]{1,0:T(8,128)S(1)}, u32[]{:S(2)}, u32[]{:S(2)}) %collective-permute-start.2) | collective-permute-done | bytes 40992 | tf_op jit(solution)/shard_map/ppermute | solution.py:411
  10.4 0.2 collective-permute-start.3
  10.6 0.4 %first_half.1 = (f32[48,512]{1,0:T(8,128)S(1)}, f32[48,1024]{1,0:T(8,128)S(1)}) custom-call(bf16[2,1024,512]{2,1,0:T(8,128)(2,1)S(1)} %get-tuple-element.44.placed_ref, f32[40,128]{1,0:T(8,128)S(1)} %get-tuple-element.46.stay_ref, f32[40,128]{1,0:T(8,128)S(1)} %get-tuple-element.47.back_ref, f32[80,128]{1,0:T(8,128)S(1)} %get-tuple-element.48.refs_0_, ...), custom_call_target="tpu_custom_call" | custom-call | flops 100663296 | bytes 1048576 | tf_op jit(solution)/shard_map/first_half/pallas_call | solution.py:484
  11.0 0.7 %collective-permute-done.3.got_ref = f32[160,128]{1,0:T(8,128)S(1)} collective-permute-done((f32[160,128]{1,0:T(8,128)S(1)}, f32[160,128]{1,0:T(8,128)S(1)}, u32[]{:S(2)}, u32[]{:S(2)}) %collective-permute-start.3) | collective-permute-done | bytes 81952 | tf_op jit(solution)/shard_map/ppermute | solution.py:411
  11.7 0.8 %first.1 = (f32[48,512]{1,0:T(8,128)S(1)}, f32[48,1024]{1,0:T(8,128)S(1)}, f32[96,128]{1,0:T(8,128)S(1)}, f32[96,128]{1,0:T(8,128)S(1)}, f32[96,128]{1,0:T(8,128)S(1)}) custom-call(bf16[1024,768]{1,0:T(8,128)(2,1)S(1)} %get-tuple-element.40.far_ref, bf16[2,1024,512]{2,1,0:T(8,128)(2,1)S(1)} %get-tuple-element.44.placed_ref, ...), custom_call_target="tpu_custom_call" | custom-call | bytes 1048576 | tf_op jit(solution)/shard_map/first/pallas_call | solution.py:487
  12.5 1.9 %collective-permute-start.4 = (f32[96,128]{1,0:T(8,128)S(1)}, f32[96,128]{1,0:T(8,128)S(1)}, u32[]{:S(2)}, u32[]{:S(2)}) collective-permute-start(f32[96,128]{1,0:T(8,128)S(1)} %get-tuple-element.59.refs_0_), channel_id=1, source_target_pairs={{0,28},{1,29},{2,30},{3,31},{4,24},{5,25},{6,26},{7,27},{8,20},{9,... | collective-permute-start | bytes 147464 | tf_op jit(solution)/shard_map/ppermute | solution.py:411
  14.4 0.3 collective-permute-start.5
  14.7 0.8 %collective-permute-start.6 = (f32[96,128]{1,0:T(8,128)S(1)}, f32[96,128]{1,0:T(8,128)S(1)}, u32[]{:S(2)}, u32[]{:S(2)}) collective-permute-start(f32[96,128]{1,0:T(8,128)S(1)} %get-tuple-element.61.refs_2_), channel_id=1, source_target_pairs={{0,12},{1,13},{2,14},{3,15},{4,8},{5,9},{6,10},{7,11},{8,4},{9,5},... | collective-permute-start | bytes 147464 | tf_op jit(solution)/shard_map/ppermute | solution.py:411
  15.5 1.2 %middle.1 = (f32[48,1024]{1,0:T(8,128)S(1)}, f32[48,128]{1,0:T(8,128)S(1)}, f32[48,128]{1,0:T(8,128)S(1)}, f32[48,128]{1,0:T(8,128)S(1)}, f32[48,128]{1,0:T(8,128)S(1)}) custom-call(bf16[1024,384]{1,0:T(8,128)(2,1)S(1)} %get-tuple-element.45.edge_ref, bf16[2,1024,512]{2,1,0:T(8,128)(2,1)S(1)} %get-tuple-element.43.slots_ref, ...), custom_call_target="tpu_custom_call" | custom-call | flops 201326592 | bytes 1048576 | tf_op jit(solution)/shard_map/middle/pallas_call | solution.py:491
  16.7 0.4 %collective-permute-done.4.refs_3_ = f32[96,128]{1,0:T(8,128)S(1)} collective-permute-done((f32[96,128]{1,0:T(8,128)S(1)}, f32[96,128]{1,0:T(8,128)S(1)}, u32[]{:S(2)}, u32[]{:S(2)}) %collective-permute-start.4) | collective-permute-done | bytes 49184 | tf_op jit(solution)/shard_map/ppermute | solution.py:411
  17.1 1.1 %collective-permute-done.5.refs_4_ = f32[96,128]{1,0:T(8,128)S(1)} collective-permute-done((f32[96,128]{1,0:T(8,128)S(1)}, f32[96,128]{1,0:T(8,128)S(1)}, u32[]{:S(2)}, u32[]{:S(2)}) %collective-permute-start.5) | collective-permute-done | bytes 49184 | tf_op jit(solution)/shard_map/ppermute | solution.py:411
  18.3 0.0 collective-permute-done.6.refs_5_
  18.3 0.3 collective-permute-start.7
  18.6 0.7 %second_half.1 = (f32[48,1024]{1,0:T(8,128)S(1)}, f32[48,1024]{1,0:T(8,128)S(1)}) custom-call(bf16[2,1024,512]{2,1,0:T(8,128)(2,1)S(1)} %get-tuple-element.43.slots_ref, bf16[2,1024,512]{2,1,0:T(8,128)(2,1)S(1)} %get-tuple-element.44.placed_ref, f32[48,128]{1,0:T(8,128)S(1)} %get-tuple-element.57.stay_ref, f32[48,128]{1,0:T(8,128)S(1)} %get-tuple-element.58.back_ref, ...), custom_call_target="tpu_custom_call" | custom-call | flops 201326592 | bytes 1048576 | tf_op jit(solution)/shard_map/second_half/pallas_call | solution.py:495
  19.4 0.3 collective-permute-done.7.got_ref
  19.7 1.2 %second.1 = (f32[48,1024]{1,0:T(8,128)S(1)}, f32[48,128]{1,0:T(8,128)S(1)}) custom-call(bf16[2,1024,512]{2,1,0:T(8,128)(2,1)S(1)} %get-tuple-element.43.slots_ref, bf16[2,1024,512]{2,1,0:T(8,128)(2,1)S(1)} %get-tuple-element.44.placed_ref, f32[48,1024]{1,0:T(8,128)S(1)} %get-tuple-element.56.basis_ref, f32[48,1024]{1,0:T(8,128)S(1)} %get-tuple-element.62.half_jump_ref, ...), custom_call_target="tpu_custom_call" | custom-call | bytes 1048576 | tf_op jit(solution)/shard_map/second/pallas_call | solution.py:498
  20.9 0.3 collective-permute-start.8
  21.2 1.0 %collective-permute-done.8.refs_0_ = f32[48,128]{1,0:T(8,128)S(1)} collective-permute-done((f32[48,128]{1,0:T(8,128)S(1)}, f32[48,128]{1,0:T(8,128)S(1)}, u32[]{:S(2)}, u32[]{:S(2)}) %collective-permute-start.8) | collective-permute-done | bytes 24608 | tf_op jit(solution)/shard_map/ppermute | solution.py:411
  22.2 2.0 %collective-permute-start.10 = (f32[48,128]{1,0:T(8,128)S(1)}, f32[48,128]{1,0:T(8,128)S(1)}, u32[]{:S(2)}, u32[]{:S(2)}) collective-permute-start(f32[48,128]{1,0:T(8,128)S(1)} %get-tuple-element.68), channel_id=1, source_target_pairs={{0,28},{1,29},{2,30},{3,31},{4,24},{5,25},{6,26},{7,27},{8,20},{9,... | collective-permute-start | bytes 73736 | tf_op jit(solution)/shard_map/ppermute | solution.py:411
  24.2 0.4 %collective-permute-start.11 = (f32[48,128]{1,0:T(8,128)S(1)}, f32[48,128]{1,0:T(8,128)S(1)}, u32[]{:S(2)}, u32[]{:S(2)}) collective-permute-start(f32[48,128]{1,0:T(8,128)S(1)} %get-tuple-element.69), channel_id=1, source_target_pairs={{0,20},{1,21},{2,22},{3,23},{4,16},{5,17},{6,18},{7,19},{8,28},{9,... | collective-permute-start | bytes 73736 | tf_op jit(solution)/shard_map/ppermute | solution.py:411
  24.6 0.7 %collective-permute-start.9 = (f32[48,128]{1,0:T(8,128)S(1)}, f32[48,128]{1,0:T(8,128)S(1)}, u32[]{:S(2)}, u32[]{:S(2)}) collective-permute-start(f32[48,128]{1,0:T(8,128)S(1)} %get-tuple-element.67.refs_3_), channel_id=1, source_target_pairs={{0,12},{1,13},{2,14},{3,15},{4,8},{5,9},{6,10},{7,11},{8,4},{9,5},... | collective-permute-start | bytes 73736 | tf_op jit(solution)/shard_map/ppermute | solution.py:411
  25.3 1.1 %collective-permute-done.10.refs_1_ = f32[48,128]{1,0:T(8,128)S(1)} collective-permute-done((f32[48,128]{1,0:T(8,128)S(1)}, f32[48,128]{1,0:T(8,128)S(1)}, u32[]{:S(2)}, u32[]{:S(2)}) %collective-permute-start.10) | collective-permute-done | bytes 24608 | tf_op jit(solution)/shard_map/ppermute | solution.py:411
  26.4 1.0 %collective-permute-done.11.refs_2_ = f32[48,128]{1,0:T(8,128)S(1)} collective-permute-done((f32[48,128]{1,0:T(8,128)S(1)}, f32[48,128]{1,0:T(8,128)S(1)}, u32[]{:S(2)}, u32[]{:S(2)}) %collective-permute-start.11) | collective-permute-done | bytes 24608 | tf_op jit(solution)/shard_map/ppermute | solution.py:411
  27.4 0.4 %collective-permute-done.9.refs_0_ = f32[48,128]{1,0:T(8,128)S(1)} collective-permute-done((f32[48,128]{1,0:T(8,128)S(1)}, f32[48,128]{1,0:T(8,128)S(1)}, u32[]{:S(2)}, u32[]{:S(2)}) %collective-permute-start.9) | collective-permute-done | bytes 24608 | tf_op jit(solution)/shard_map/ppermute | solution.py:411
  27.9 2.4 %collective-permute-start.12 = (f32[48,128]{1,0:T(8,128)S(1)}, f32[48,128]{1,0:T(8,128)S(1)}, u32[]{:S(2)}, u32[]{:S(2)}) collective-permute-start(f32[48,128]{1,0:T(8,128)S(1)} %get-tuple-element.70.refs_3_), channel_id=1, source_target_pairs={{0,6},{1,7},{2,4},{3,5},{4,2},{5,3},{6,0},{7,1},{8,14},{9,15},{10,... | collective-permute-start | bytes 73736 | tf_op jit(solution)/shard_map/ppermute | solution.py:411
  30.3 1.3 %collective-permute-start.13 = (f32[48,128]{1,0:T(8,128)S(1)}, f32[48,128]{1,0:T(8,128)S(1)}, u32[]{:S(2)}, u32[]{:S(2)}) collective-permute-start(f32[48,128]{1,0:T(8,128)S(1)} %get-tuple-element.71), channel_id=1, source_target_pairs={{0,7},{1,6},{2,5},{3,4},{4,3},{5,2},{6,1},{7,0},{8,15},{9,14},{10,... | collective-permute-start | bytes 73736 | tf_op jit(solution)/shard_map/ppermute | solution.py:411
  31.6 0.2 collective-permute-start.14
  31.8 0.3 collective-permute-done.12.refs_0_
  32.1 3.4 %collective-permute-done.13.refs_1_ = f32[48,128]{1,0:T(8,128)S(1)} collective-permute-done((f32[48,128]{1,0:T(8,128)S(1)}, f32[48,128]{1,0:T(8,128)S(1)}, u32[]{:S(2)}, u32[]{:S(2)}) %collective-permute-start.13) | collective-permute-done | bytes 24608 | tf_op jit(solution)/shard_map/ppermute | solution.py:411
  35.4 0.0 collective-permute-done.14.refs_2_
  35.5 2.4 %final.1 = (f32[32,1024]{1,0:T(8,128)}, f32[12,32]{1,0:T(8,128)}) custom-call(f32[48,128]{1,0:T(8,128)S(1)} %sum.5.terms_ref, f32[48,1024]{1,0:T(8,128)S(1)} %get-tuple-element.56.basis_ref, f32[48,1024]{1,0:T(8,128)S(1)} %get-tuple-element.73.jump_ref), custom_call_target="tpu_custom_call" | custom-call | bytes 1048576 | tf_op jit(solution)/shard_map/final/pallas_call | solution.py:502
  (11 shorter events, 0.1 us)
Async XLA Ops:
  2.4 7.2 %collective-permute-start = (f32[80,128]{1,0:T(8,128)S(1)}, f32[80,128]{1,0:T(8,128)S(1)}, u32[]{:S(2)}, u32[]{:S(2)}) collective-permute-start(f32[80,128]{1,0:T(8,128)S(1)} %get-tuple-element.48.refs_0_), channel_id=1, source_target_pairs={{0,28},{1,29},{2,30},{3,31},{4,24},{5,25},{6,26},{7,27},{8,20},{9,... | collective-permute-start | bytes 122888 | tf_op jit(solution)/shard_map/ppermute | solution.py:411
  5.8 3.8 %collective-permute-start.1 = (f32[80,128]{1,0:T(8,128)S(1)}, f32[80,128]{1,0:T(8,128)S(1)}, u32[]{:S(2)}, u32[]{:S(2)}) collective-permute-start(f32[80,128]{1,0:T(8,128)S(1)} %get-tuple-element.49.refs_1_), channel_id=1, source_target_pairs={{0,20},{1,21},{2,22},{3,23},{4,16},{5,17},{6,18},{7,19},{8,28},{9,... | collective-permute-start | bytes 122888 | tf_op jit(solution)/shard_map/ppermute | solution.py:411
  6.6 3.8 %collective-permute-start.2 = (f32[80,128]{1,0:T(8,128)S(1)}, f32[80,128]{1,0:T(8,128)S(1)}, u32[]{:S(2)}, u32[]{:S(2)}) collective-permute-start(f32[80,128]{1,0:T(8,128)S(1)} %get-tuple-element.50.refs_2_), channel_id=1, source_target_pairs={{0,12},{1,13},{2,14},{3,15},{4,8},{5,9},{6,10},{7,11},{8,4},{9,5},... | collective-permute-start | bytes 122888 | tf_op jit(solution)/shard_map/ppermute | solution.py:411
  10.4 1.3 %collective-permute-start.3 = (f32[160,128]{1,0:T(8,128)S(1)}, f32[160,128]{1,0:T(8,128)S(1)}, u32[]{:S(2)}, u32[]{:S(2)}) collective-permute-start(f32[160,128]{1,0:T(8,128)S(1)} %pad_maximum_fusion.1), channel_id=1, source_target_pairs={{0,4},{1,5},{2,6},{3,7},{4,0},{5,1},{6,2},{7,3},{8,12},{9,13},{10,... | collective-permute-start | bytes 245768 | tf_op jit(solution)/shard_map/ppermute | solution.py:411
  12.5 4.6 %collective-permute-start.4 = (f32[96,128]{1,0:T(8,128)S(1)}, f32[96,128]{1,0:T(8,128)S(1)}, u32[]{:S(2)}, u32[]{:S(2)}) collective-permute-start(f32[96,128]{1,0:T(8,128)S(1)} %get-tuple-element.59.refs_0_), channel_id=1, source_target_pairs={{0,28},{1,29},{2,30},{3,31},{4,24},{5,25},{6,26},{7,27},{8,20},{9,... | collective-permute-start | bytes 147464 | tf_op jit(solution)/shard_map/ppermute | solution.py:411
  14.4 3.9 %collective-permute-start.5 = (f32[96,128]{1,0:T(8,128)S(1)}, f32[96,128]{1,0:T(8,128)S(1)}, u32[]{:S(2)}, u32[]{:S(2)}) collective-permute-start(f32[96,128]{1,0:T(8,128)S(1)} %get-tuple-element.60.refs_1_), channel_id=1, source_target_pairs={{0,20},{1,21},{2,22},{3,23},{4,16},{5,17},{6,18},{7,19},{8,28},{9,... | collective-permute-start | bytes 147464 | tf_op jit(solution)/shard_map/ppermute | solution.py:411
  14.7 3.6 %collective-permute-start.6 = (f32[96,128]{1,0:T(8,128)S(1)}, f32[96,128]{1,0:T(8,128)S(1)}, u32[]{:S(2)}, u32[]{:S(2)}) collective-permute-start(f32[96,128]{1,0:T(8,128)S(1)} %get-tuple-element.61.refs_2_), channel_id=1, source_target_pairs={{0,12},{1,13},{2,14},{3,15},{4,8},{5,9},{6,10},{7,11},{8,4},{9,5},... | collective-permute-start | bytes 147464 | tf_op jit(solution)/shard_map/ppermute | solution.py:411
  18.3 1.4 %collective-permute-start.7 = (f32[192,128]{1,0:T(8,128)S(1)}, f32[192,128]{1,0:T(8,128)S(1)}, u32[]{:S(2)}, u32[]{:S(2)}) collective-permute-start(f32[192,128]{1,0:T(8,128)S(1)} %pad_maximum_fusion), channel_id=1, source_target_pairs={{0,4},{1,5},{2,6},{3,7},{4,0},{5,1},{6,2},{7,3},{8,12},{9,13},{10,... | collective-permute-start | bytes 294920 | tf_op jit(solution)/shard_map/ppermute | solution.py:411
  20.9 1.3 %collective-permute-start.8 = (f32[48,128]{1,0:T(8,128)S(1)}, f32[48,128]{1,0:T(8,128)S(1)}, u32[]{:S(2)}, u32[]{:S(2)}) collective-permute-start(f32[48,128]{1,0:T(8,128)S(1)} %get-tuple-element.66.refs_1_), channel_id=1, source_target_pairs={{0,4},{1,5},{2,6},{3,7},{4,0},{5,1},{6,2},{7,3},{8,12},{9,13},{10,... | collective-permute-start | bytes 73736 | tf_op jit(solution)/shard_map/ppermute | solution.py:411
  22.2 4.2 %collective-permute-start.10 = (f32[48,128]{1,0:T(8,128)S(1)}, f32[48,128]{1,0:T(8,128)S(1)}, u32[]{:S(2)}, u32[]{:S(2)}) collective-permute-start(f32[48,128]{1,0:T(8,128)S(1)} %get-tuple-element.68), channel_id=1, source_target_pairs={{0,28},{1,29},{2,30},{3,31},{4,24},{5,25},{6,26},{7,27},{8,20},{9,... | collective-permute-start | bytes 73736 | tf_op jit(solution)/shard_map/ppermute | solution.py:411
  24.2 3.3 %collective-permute-start.11 = (f32[48,128]{1,0:T(8,128)S(1)}, f32[48,128]{1,0:T(8,128)S(1)}, u32[]{:S(2)}, u32[]{:S(2)}) collective-permute-start(f32[48,128]{1,0:T(8,128)S(1)} %get-tuple-element.69), channel_id=1, source_target_pairs={{0,20},{1,21},{2,22},{3,23},{4,16},{5,17},{6,18},{7,19},{8,28},{9,... | collective-permute-start | bytes 73736 | tf_op jit(solution)/shard_map/ppermute | solution.py:411
  24.6 3.3 %collective-permute-start.9 = (f32[48,128]{1,0:T(8,128)S(1)}, f32[48,128]{1,0:T(8,128)S(1)}, u32[]{:S(2)}, u32[]{:S(2)}) collective-permute-start(f32[48,128]{1,0:T(8,128)S(1)} %get-tuple-element.67.refs_3_), channel_id=1, source_target_pairs={{0,12},{1,13},{2,14},{3,15},{4,8},{5,9},{6,10},{7,11},{8,4},{9,5},... | collective-permute-start | bytes 73736 | tf_op jit(solution)/shard_map/ppermute | solution.py:411
  27.9 4.2 %collective-permute-start.12 = (f32[48,128]{1,0:T(8,128)S(1)}, f32[48,128]{1,0:T(8,128)S(1)}, u32[]{:S(2)}, u32[]{:S(2)}) collective-permute-start(f32[48,128]{1,0:T(8,128)S(1)} %get-tuple-element.70.refs_3_), channel_id=1, source_target_pairs={{0,6},{1,7},{2,4},{3,5},{4,2},{5,3},{6,0},{7,1},{8,14},{9,15},{10,... | collective-permute-start | bytes 73736 | tf_op jit(solution)/shard_map/ppermute | solution.py:411
  30.3 5.2 %collective-permute-start.13 = (f32[48,128]{1,0:T(8,128)S(1)}, f32[48,128]{1,0:T(8,128)S(1)}, u32[]{:S(2)}, u32[]{:S(2)}) collective-permute-start(f32[48,128]{1,0:T(8,128)S(1)} %get-tuple-element.71), channel_id=1, source_target_pairs={{0,7},{1,6},{2,5},{3,4},{4,3},{5,2},{6,1},{7,0},{8,15},{9,14},{10,... | collective-permute-start | bytes 73736 | tf_op jit(solution)/shard_map/ppermute | solution.py:411
  31.6 3.9 %collective-permute-start.14 = (f32[48,128]{1,0:T(8,128)S(1)}, f32[48,128]{1,0:T(8,128)S(1)}, u32[]{:S(2)}, u32[]{:S(2)}) collective-permute-start(f32[48,128]{1,0:T(8,128)S(1)} %get-tuple-element.72), channel_id=1, source_target_pairs={{0,5},{1,4},{2,7},{3,6},{4,1},{5,0},{6,3},{7,2},{8,13},{9,12},{10,... | collective-permute-start | bytes 73736 | tf_op jit(solution)/shard_map/ppermute | solution.py:411

commit v5 on v1

--- a/solution.py
+++ b/solution.py
@@ -11,7 +11,6 @@
 AGG_SUBS = 16
 ITERS = 2
 GROUP = 8
-SCALAR_LANES = (MODES, MODES + 1, GROUP + MODES, GROUP + MODES + 1, 2 * GROUP + MODES)
 
 HIGHEST = lax.Precision.HIGHEST
 VMEM = pl.BlockSpec(memory_space=pltpu.VMEM)
@@ -183,16 +182,16 @@
 
 
 def products_of(left, right):
+    rows, columns = left.shape[0], right.shape[0]
     both = lax.dot_general(split(left), split(right), NT, preferred_element_type=jnp.float32)
-    both = both[: left.shape[0]] + both[left.shape[0] :]
-    return both + pltpu.roll(both, right.shape[0], 1)
-
-
-def with_scalars(top, products, lanes):
-    lane = lax.broadcasted_iota(jnp.int32, top.shape, 1)
-    for at, product in zip(lanes, products):
-        top = jnp.where(lane == at, jnp.sum(product, axis=1, keepdims=True), top)
-    return top
+    both = both[:rows] + both[rows:]
+    return both[:, :columns] + both[:, columns:]
+
+
+def by_load(products):
+    sums = [jnp.sum(product, axis=1, keepdims=True) for product in products]
+    empty = [jnp.zeros_like(sums[0])] * (GROUP - len(sums))
+    return jnp.concatenate(sums + empty, axis=1).T
 
 
 def middle_kernel(
@@ -200,20 +199,26 @@
 ):
     image = image_ref[...]
     send_near(image, edge_ref, near_ref, back_ref, stay_ref)
-    coarse = terms_ref.shape[1] // 8
+    coarse = terms_ref.shape[0] // 3
     loads = image.shape[0] - coarse
     basis = split_dot(straight_ref[...], slots_ref[0], NT) + split_dot(handed_ref[...], slots_ref[1], NT)
     basis_ref[...] = basis
-    left = jnp.concatenate([basis[:loads], image[:loads], basis[loads:]])
-    empty = jnp.zeros((2 * coarse, basis.shape[1]), jnp.float32)
-    both = products_of(left, jnp.concatenate([basis[loads:], image[loads:], empty]))
-    strip = lax.broadcasted_iota(jnp.int32, (loads, 8 * coarse), 1) // coarse
-    top = jnp.where(strip < 2, both[:loads], 0.0)
-    top = jnp.where(strip == 4, both[loads : 2 * loads], top)
-    residual = basis[:loads]
-    terms_ref[:loads] = with_scalars(top, (residual * residual, residual * image[:loads]), SCALAR_LANES[:2])
-    strip = lax.broadcasted_iota(jnp.int32, (coarse, 8 * coarse), 1) // coarse
-    terms_ref[loads:] = jnp.where(strip < 2, both[2 * loads :], 0.0)
+    residual, residual_image = basis[:loads], image[:loads]
+    lanes = terms_ref.shape[1]
+    empty = jnp.zeros((lanes - 2 * loads - 2 * coarse, basis.shape[1]), jnp.float32)
+    both = products_of(
+        jnp.concatenate([basis[loads:], image[loads:]]),
+        jnp.concatenate([residual, basis[loads:], image[loads:], empty, residual_image]),
+    )
+    by_g, by_h = both[:coarse], both[coarse:]
+    lane = lax.broadcasted_iota(jnp.int32, (coarse, lanes), 1)
+    first, last = lane < loads, lane >= lanes - loads
+    terms_ref[:coarse] = jnp.where(first | last, by_g, 0.0)
+    terms_ref[coarse : 2 * coarse] = jnp.where(last, pltpu.roll(by_h, lanes - loads, 1), 0.0)
+    terms_ref[2 * coarse :] = jnp.where((lane >= loads) & (lane < loads + 2 * coarse), by_g, 0.0)
+    terms_ref[2 * coarse : 2 * coarse + GROUP, :loads] = by_load(
+        [residual * residual, residual * residual_image]
+    )
 
 
 def second_half_kernel(slots_ref, placed_ref, stay_ref, back_ref, *refs):
@@ -226,29 +231,31 @@
 
 def second_kernel(slots_ref, placed_ref, basis_ref, half_jump_ref, half_second_ref, early_ref, got_ref, near_ref, *refs):
     *sent_refs, jump_ref, terms_ref = refs
-    coarse = terms_ref.shape[1] // 8
+    coarse = terms_ref.shape[0] // 3
     loads = basis_ref.shape[0] - coarse
     jump = for_other(near_ref, sent_refs) - handed(got_ref, loads + coarse)
     second = half_second_ref[...] + split_dot(jump, placed_ref[1], NT)
     jump = half_jump_ref[...] + split_dot(jump, slots_ref[1], NT)
     jump_ref[...] = jump
     basis = basis_ref[...]
-    left = jnp.concatenate([basis[:loads], jump[:loads], second[:loads], basis[loads:], jump[loads:]])
-    empty = jnp.zeros((coarse, basis.shape[1]), jnp.float32)
-    both = products_of(left, jnp.concatenate([basis[loads:], empty, jump[loads:], second[loads:]]))
-    along, jumped, doubled = (both[at * loads : (at + 1) * loads] for at in range(3))
-    base, far = both[3 * loads : 3 * loads + coarse], both[3 * loads + coarse :]
-    strip = lax.broadcasted_iota(jnp.int32, (loads, 8 * coarse), 1) // coarse
-    top = jnp.where(strip == 2, doubled, 0.0)
-    top = jnp.where(strip == 3, along, top)
-    top = jnp.where(strip == 5, pltpu.roll(doubled, coarse, 1), top)
-    top = jnp.where(strip >= 6, jumped, top)
     residual, jump_loads, second_loads = basis[:loads], jump[:loads], second[:loads]
-    products = (jump_loads * jump_loads, jump_loads * second_loads, residual * second_loads)
-    terms_ref[:loads] = early_ref[:loads] + with_scalars(top, products, SCALAR_LANES[2:])
-    strip = lax.broadcasted_iota(jnp.int32, (coarse, 8 * coarse), 1) // coarse
-    base = jnp.where((strip == 2) | (strip == 3), base, 0.0)
-    terms_ref[loads:] = early_ref[loads:] + jnp.where(strip < 4, base, far)
+    both = products_of(
+        jnp.concatenate([basis[loads:], jump[loads:], second[loads:]]),
+        jnp.concatenate([residual, jump_loads, second_loads, jump[loads:], second[loads:]]),
+    )
+    by_g, by_z, by_dz = (both[at * coarse : (at + 1) * coarse] for at in range(3))
+    lanes = terms_ref.shape[1]
+    lane = lax.broadcasted_iota(jnp.int32, (coarse, lanes), 1)
+    group = lane // loads
+    top = jnp.where(group == 1, by_z, jnp.where(group == 2, by_g, 0.0))
+    low = jnp.where(group < 2, by_dz, jnp.where(group == 2, by_z, 0.0))
+    last = jnp.where(group == 2, pltpu.roll(by_z, lanes - loads, 1), jnp.where(lane >= lanes - coarse, by_g, 0.0))
+    terms_ref[:coarse] = early_ref[:coarse] + top
+    terms_ref[coarse : 2 * coarse] = early_ref[coarse : 2 * coarse] + low
+    terms_ref[2 * coarse :] = early_ref[2 * coarse :] + last
+    sums = by_load([jump_loads * jump_loads, jump_loads * second_loads, residual * second_loads])
+    start = 2 * coarse + GROUP
+    terms_ref[start : start + GROUP, :loads] = sums
 
 
 def sum_kernel(count, *refs):
@@ -295,30 +302,29 @@
 
 
 def final_kernel(terms_ref, basis_ref, jump_ref, multipliers_ref, amplitudes_ref):
-    coarse = terms_ref.shape[1] // 8
+    coarse = terms_ref.shape[0] // 3
     loads = basis_ref.shape[0] - coarse
     groups = coarse // GROUP
-    by_load = terms_ref[:loads].T
-    used = lax.broadcasted_iota(jnp.int32, (coarse, loads), 0) % GROUP < MODES
-
-    def strip(at):
-        return by_load[at * coarse : (at + 1) * coarse]
-
-    def block(at):
-        return terms_ref[loads:, at * coarse : (at + 1) * coarse]
+
+    def part(block, start, width):
+        return terms_ref[block * coarse : (block + 1) * coarse, start : start + width]
 
     def total(values):
         return jnp.sum(values, axis=0, keepdims=True)
 
-    res_res, res_image, jump_jump, jump_second, res_second = (by_load[at : at + 1] for at in SCALAR_LANES)
-    coarse_res, res_h = (jnp.where(used, strip(at), 0.0) for at in (0, 1))
-    second_z, res_dz, image_g, second_g, jump_z, jump_dz = (strip(at) for at in range(2, 8))
-    g_h, g_dz, z_z, z_dz = block(1), block(3), block(6), block(7)
+    def scalar(at):
+        return terms_ref[2 * coarse + at : 2 * coarse + at + 1, :loads]
+
+    res_res, res_image, jump_jump, jump_second, res_second = (scalar(at) for at in (0, 1, 8, 9, 10))
+    coarse_res, jump_z, second_g, image_g = (part(0, at * loads, loads) for at in range(4))
+    res_dz, jump_dz, second_z, res_h = (part(1, at * loads, loads) for at in range(4))
+    gram, g_h, z_z, z_dz = (part(2, loads + at * coarse, coarse) for at in range(4))
+    g_dz = part(2, terms_ref.shape[1] - coarse, coarse)
     row = lax.broadcasted_iota(jnp.int32, (coarse, coarse), 0)
     unit = jnp.where(row == lax.broadcasted_iota(jnp.int32, (coarse, coarse), 1), 1.0, 0.0)
     empty = jnp.zeros((coarse, 5 * coarse - 2 * loads), jnp.float32)
     solved = eliminate(
-        jnp.concatenate([terms_ref[loads:, : 2 * coarse], coarse_res, image_g, unit, empty], axis=1), coarse
+        jnp.concatenate([gram, g_h, coarse_res, image_g, unit, empty], axis=1), coarse
     )
     inverse_h = solved[:, coarse : 2 * coarse]
     amounts = solved[:, 2 * coarse : 2 * coarse + loads]
@@ -407,7 +413,7 @@
     height = loads + GROUP * groups
     f32, i32 = jnp.float32, jnp.int32
     tall = ((height, rows), f32)
-    wide = ((height, 8 * GROUP * groups), f32)
+    wide = ((3 * GROUP * groups, 4 * loads), f32)
 
     def pairs(height):
         return [((2 * height, per_peer), f32)] * (peers // 2 - 1)
@@ -585,7 +591,8 @@
     peers, planes = mesh.shape["sub"], mesh.shape["rep"]
     powers = all(size & (size - 1) == 0 for size in (peers, planes))
     whole = dual_ops.shape[1] % (128 * peers) == 0 and local_gap.shape[0] % 16 == 0
-    return powers and whole and 8 * GROUP * (mode_block.shape[0] // AGG_SUBS) == 128
+    coarse = GROUP * (mode_block.shape[0] // AGG_SUBS)
+    return powers and whole and 4 * local_gap.shape[0] == 128 and 8 * coarse == 128
 
 
 def solution(mesh):

time: 37.9 us -> 37.9 us (level)
  no operation moved by 1% of the time
where the time goes in v5:
time: 37.9 us; the launch traced here: 37.7 us
  starting transfers between devices  15.5 us (41%)
  Pallas kernels  11.5 us (30%)
  waiting for transfers between devices  9.95 us (26%)
  between operations  0.74 us (2%)
    ppermute x15, starting transfers between devices, permute(): lax.ppermute(values, ('sub', 'rep'), [(at, at ^ offset) for at in range(p...  15.5 us
    ppermute x15, waiting for transfers between devices, permute(): lax.ppermute(values, ('sub', 'rep'), [(at, at ^ offset) for at in range(p...  9.95 us
    pallas_call x1, Pallas kernels, fused_body(): call(ready_kernel, [((rows, 3 * per_peer), jnp.bfloat16), halves, halves,...  2.97 us
    pallas_call x1, Pallas kernels, fused_body(): call(final_kernel, [((loads, rows), f32), ((MODES * groups, loads), f32)]...  2.34 us
    pallas_call x1, Pallas kernels, fused_body(): call(place_kernel, [((rows, rows - 2 * per_peer), jnp.bfloat16), ((short,...  1.77 us
    pallas_call x1, Pallas kernels, fused_body(): call(middle_kernel, [tall, wide, *singles(height)], [VMEM] * 5, 'middle',...  1.28 us
    pallas_call x1, Pallas kernels, fused_body(): call(second_kernel, [tall, wide], [VMEM] * (8 + len(got)), 'second')  1.15 us
    pallas_call x1, Pallas kernels, fused_body(): call(first_kernel, [half, tall, *pairs(height)], [VMEM] * (5 + len(send))...  0.79 us
  transfers between devices with their start and end apart: 15, of which 12 were waited for; matrix products, arithmetic and copies ran while one was open for 0% of the time, Pallas kernels for 14%

profile of v5, /device:TPU:0, one launch (start us, length us, event | category | flops | bytes accessed | tf_op | source)
XLA Modules:
  0.0 37.7 jit_solution(2478837377938758807)
XLA Ops:
  0.6 1.8 %place.1 = (bf16[1024,768]{1,0:T(8,128)(2,1)S(1)}, f32[40,1024]{1,0:T(8,128)S(1)}, bf16[1,1024,1024]{2,1,0:T(8,128)(2,1)S(1)}, s32[1,1024]{1,0:T(1,128)S(1)}, f3...) custom-call(s32[1,1024]{1,0:T(1,128)} %route_hbm.1, s32[1,32]{1,0:T(1,128)} %bitcast.4, ...), custom_call_target="tpu_custom_call" | custom-call | bytes 1048576 | tf_op jit(solution)/shard_map/place/pallas_call | solution.py:429
  2.4 3.4 %collective-permute-start = (f32[80,128]{1,0:T(8,128)S(1)}, f32[80,128]{1,0:T(8,128)S(1)}, u32[]{:S(2)}, u32[]{:S(2)}) collective-permute-start(f32[80,128]{1,0:T(8,128)S(1)} %get-tuple-element.48.refs_0_), channel_id=1, source_target_pairs={{0,28},{1,29},{2,30},{3,31},{4,24},{5,25},{6,26},{7,27},{8,20},{9,... | collective-permute-start | bytes 122888 | tf_op jit(solution)/shard_map/ppermute | solution.py:381
  5.8 0.8 %collective-permute-start.1 = (f32[80,128]{1,0:T(8,128)S(1)}, f32[80,128]{1,0:T(8,128)S(1)}, u32[]{:S(2)}, u32[]{:S(2)}) collective-permute-start(f32[80,128]{1,0:T(8,128)S(1)} %get-tuple-element.49.refs_1_), channel_id=1, source_target_pairs={{0,20},{1,21},{2,22},{3,23},{4,16},{5,17},{6,18},{7,19},{8,28},{9,... | collective-permute-start | bytes 122888 | tf_op jit(solution)/shard_map/ppermute | solution.py:381
  6.6 0.1 collective-permute-start.2
  6.7 3.0 %ready.1 = (bf16[1024,384]{1,0:T(8,128)(2,1)S(1)}, bf16[2,1024,512]{2,1,0:T(8,128)(2,1)S(1)}, bf16[2,1024,512]{2,1,0:T(8,128)(2,1)S(1)}, f32[40,128]{1,0:T(8,128...) custom-call(s32[1,1024]{1,0:T(1,128)S(1)} %get-tuple-element.39.route_ref, ...), custom_call_target="tpu_custom_call" | custom-call | flops 2147483648 | bytes 1048576 | tf_op jit(solution)/shard_map/ready/pallas_call | solution.py:444
  9.7 0.0 collective-permute-done.refs_3_
  9.7 0.0 collective-permute-done.1.refs_4_
  9.7 0.6 %collective-permute-done.2.refs_5_ = f32[80,128]{1,0:T(8,128)S(1)} collective-permute-done((f32[80,128]{1,0:T(8,128)S(1)}, f32[80,128]{1,0:T(8,128)S(1)}, u32[]{:S(2)}, u32[]{:S(2)}) %collective-permute-start.2) | collective-permute-done | bytes 40992 | tf_op jit(solution)/shard_map/ppermute | solution.py:381
  10.4 0.2 collective-permute-start.3
  10.6 0.4 %first_half.1 = (f32[48,512]{1,0:T(8,128)S(1)}, f32[48,1024]{1,0:T(8,128)S(1)}) custom-call(bf16[2,1024,512]{2,1,0:T(8,128)(2,1)S(1)} %get-tuple-element.44.placed_ref, f32[40,128]{1,0:T(8,128)S(1)} %get-tuple-element.46.stay_ref, f32[40,128]{1,0:T(8,128)S(1)} %get-tuple-element.47.back_ref, f32[80,128]{1,0:T(8,128)S(1)} %get-tuple-element.48.refs_0_, ...), custom_call_target="tpu_custom_call" | custom-call | flops 100663296 | bytes 1048576 | tf_op jit(solution)/shard_map/first_half/pallas_call | solution.py:453
  11.0 0.7 %collective-permute-done.3.got_ref = f32[160,128]{1,0:T(8,128)S(1)} collective-permute-done((f32[160,128]{1,0:T(8,128)S(1)}, f32[160,128]{1,0:T(8,128)S(1)}, u32[]{:S(2)}, u32[]{:S(2)}) %collective-permute-start.3) | collective-permute-done | bytes 81952 | tf_op jit(solution)/shard_map/ppermute | solution.py:381
  11.7 0.8 %first.1 = (f32[48,512]{1,0:T(8,128)S(1)}, f32[48,1024]{1,0:T(8,128)S(1)}, f32[96,128]{1,0:T(8,128)S(1)}, f32[96,128]{1,0:T(8,128)S(1)}, f32[96,128]{1,0:T(8,128)S(1)}) custom-call(bf16[1024,768]{1,0:T(8,128)(2,1)S(1)} %get-tuple-element.40.far_ref, bf16[2,1024,512]{2,1,0:T(8,128)(2,1)S(1)} %get-tuple-element.44.placed_ref, ...), custom_call_target="tpu_custom_call" | custom-call | bytes 1048576 | tf_op jit(solution)/shard_map/first/pallas_call | solution.py:456
  12.5 2.0 %collective-permute-start.4 = (f32[96,128]{1,0:T(8,128)S(1)}, f32[96,128]{1,0:T(8,128)S(1)}, u32[]{:S(2)}, u32[]{:S(2)}) collective-permute-start(f32[96,128]{1,0:T(8,128)S(1)} %get-tuple-element.59.refs_0_), channel_id=1, source_target_pairs={{0,28},{1,29},{2,30},{3,31},{4,24},{5,25},{6,26},{7,27},{8,20},{9,... | collective-permute-start | bytes 147464 | tf_op jit(solution)/shard_map/ppermute | solution.py:381
  14.5 0.3 collective-permute-start.5
  14.8 0.8 %collective-permute-start.6 = (f32[96,128]{1,0:T(8,128)S(1)}, f32[96,128]{1,0:T(8,128)S(1)}, u32[]{:S(2)}, u32[]{:S(2)}) collective-permute-start(f32[96,128]{1,0:T(8,128)S(1)} %get-tuple-element.61.refs_2_), channel_id=1, source_target_pairs={{0,12},{1,13},{2,14},{3,15},{4,8},{5,9},{6,10},{7,11},{8,4},{9,5},... | collective-permute-start | bytes 147464 | tf_op jit(solution)/shard_map/ppermute | solution.py:381
  15.5 1.3 %middle.1 = (f32[48,1024]{1,0:T(8,128)S(1)}, f32[48,128]{1,0:T(8,128)S(1)}, f32[48,128]{1,0:T(8,128)S(1)}, f32[48,128]{1,0:T(8,128)S(1)}, f32[48,128]{1,0:T(8,128)S(1)}) custom-call(bf16[1024,384]{1,0:T(8,128)(2,1)S(1)} %get-tuple-element.45.edge_ref, bf16[2,1024,512]{2,1,0:T(8,128)(2,1)S(1)} %get-tuple-element.43.slots_ref, ...), custom_call_target="tpu_custom_call" | custom-call | flops 201326592 | bytes 1048576 | tf_op jit(solution)/shard_map/middle/pallas_call | solution.py:460
  16.8 0.3 collective-permute-done.4.refs_3_
  17.2 1.0 %collective-permute-done.5.refs_4_ = f32[96,128]{1,0:T(8,128)S(1)} collective-permute-done((f32[96,128]{1,0:T(8,128)S(1)}, f32[96,128]{1,0:T(8,128)S(1)}, u32[]{:S(2)}, u32[]{:S(2)}) %collective-permute-start.5) | collective-permute-done | bytes 49184 | tf_op jit(solution)/shard_map/ppermute | solution.py:381
  18.2 0.1 collective-permute-done.6.refs_5_
  18.3 0.4 %collective-permute-start.7 = (f32[192,128]{1,0:T(8,128)S(1)}, f32[192,128]{1,0:T(8,128)S(1)}, u32[]{:S(2)}, u32[]{:S(2)}) collective-permute-start(f32[192,128]{1,0:T(8,128)S(1)} %pad_maximum_fusion), channel_id=1, source_target_pairs={{0,4},{1,5},{2,6},{3,7},{4,0},{5,1},{6,2},{7,3},{8,12},{9,13},{10,... | collective-permute-start | bytes 294920 | tf_op jit(solution)/shard_map/ppermute | solution.py:381
  18.7 0.7 %second_half.1 = (f32[48,1024]{1,0:T(8,128)S(1)}, f32[48,1024]{1,0:T(8,128)S(1)}) custom-call(bf16[2,1024,512]{2,1,0:T(8,128)(2,1)S(1)} %get-tuple-element.43.slots_ref, bf16[2,1024,512]{2,1,0:T(8,128)(2,1)S(1)} %get-tuple-element.44.placed_ref, f32[48,128]{1,0:T(8,128)S(1)} %get-tuple-element.57.stay_ref, f32[48,128]{1,0:T(8,128)S(1)} %get-tuple-element.58.back_ref, ...), custom_call_target="tpu_custom_call" | custom-call | flops 201326592 | bytes 1048576 | tf_op jit(solution)/shard_map/second_half/pallas_call | solution.py:464
  19.5 0.2 collective-permute-done.7.got_ref
  19.7 1.2 %second.1 = (f32[48,1024]{1,0:T(8,128)S(1)}, f32[48,128]{1,0:T(8,128)S(1)}) custom-call(bf16[2,1024,512]{2,1,0:T(8,128)(2,1)S(1)} %get-tuple-element.43.slots_ref, bf16[2,1024,512]{2,1,0:T(8,128)(2,1)S(1)} %get-tuple-element.44.placed_ref, f32[48,1024]{1,0:T(8,128)S(1)} %get-tuple-element.56.basis_ref, f32[48,1024]{1,0:T(8,128)S(1)} %get-tuple-element.62.half_jump_ref, ...), custom_call_target="tpu_custom_call" | custom-call | bytes 1048576 | tf_op jit(solution)/shard_map/second/pallas_call | solution.py:467
  20.8 0.4 collective-permute-start.8
  21.2 0.8 %collective-permute-done.8.refs_0_ = f32[48,128]{1,0:T(8,128)S(1)} collective-permute-done((f32[48,128]{1,0:T(8,128)S(1)}, f32[48,128]{1,0:T(8,128)S(1)}, u32[]{:S(2)}, u32[]{:S(2)}) %collective-permute-start.8) | collective-permute-done | bytes 24608 | tf_op jit(solution)/shard_map/ppermute | solution.py:381
  22.1 2.0 %collective-permute-start.10 = (f32[48,128]{1,0:T(8,128)S(1)}, f32[48,128]{1,0:T(8,128)S(1)}, u32[]{:S(2)}, u32[]{:S(2)}) collective-permute-start(f32[48,128]{1,0:T(8,128)S(1)} %get-tuple-element.68), channel_id=1, source_target_pairs={{0,28},{1,29},{2,30},{3,31},{4,24},{5,25},{6,26},{7,27},{8,20},{9,... | collective-permute-start | bytes 73736 | tf_op jit(solution)/shard_map/ppermute | solution.py:381
  24.1 0.5 %collective-permute-start.11 = (f32[48,128]{1,0:T(8,128)S(1)}, f32[48,128]{1,0:T(8,128)S(1)}, u32[]{:S(2)}, u32[]{:S(2)}) collective-permute-start(f32[48,128]{1,0:T(8,128)S(1)} %get-tuple-element.69), channel_id=1, source_target_pairs={{0,20},{1,21},{2,22},{3,23},{4,16},{5,17},{6,18},{7,19},{8,28},{9,... | collective-permute-start | bytes 73736 | tf_op jit(solution)/shard_map/ppermute | solution.py:381
  24.6 0.7 %collective-permute-start.9 = (f32[48,128]{1,0:T(8,128)S(1)}, f32[48,128]{1,0:T(8,128)S(1)}, u32[]{:S(2)}, u32[]{:S(2)}) collective-permute-start(f32[48,128]{1,0:T(8,128)S(1)} %get-tuple-element.67.refs_3_), channel_id=1, source_target_pairs={{0,12},{1,13},{2,14},{3,15},{4,8},{5,9},{6,10},{7,11},{8,4},{9,5},... | collective-permute-start | bytes 73736 | tf_op jit(solution)/shard_map/ppermute | solution.py:381
  25.3 1.0 %collective-permute-done.10.refs_1_ = f32[48,128]{1,0:T(8,128)S(1)} collective-permute-done((f32[48,128]{1,0:T(8,128)S(1)}, f32[48,128]{1,0:T(8,128)S(1)}, u32[]{:S(2)}, u32[]{:S(2)}) %collective-permute-start.10) | collective-permute-done | bytes 24608 | tf_op jit(solution)/shard_map/ppermute | solution.py:381
  26.3 1.1 %collective-permute-done.11.refs_2_ = f32[48,128]{1,0:T(8,128)S(1)} collective-permute-done((f32[48,128]{1,0:T(8,128)S(1)}, f32[48,128]{1,0:T(8,128)S(1)}, u32[]{:S(2)}, u32[]{:S(2)}) %collective-permute-start.11) | collective-permute-done | bytes 24608 | tf_op jit(solution)/shard_map/ppermute | solution.py:381
  27.3 0.5 %collective-permute-done.9.refs_0_ = f32[48,128]{1,0:T(8,128)S(1)} collective-permute-done((f32[48,128]{1,0:T(8,128)S(1)}, f32[48,128]{1,0:T(8,128)S(1)}, u32[]{:S(2)}, u32[]{:S(2)}) %collective-permute-start.9) | collective-permute-done | bytes 24608 | tf_op jit(solution)/shard_map/ppermute | solution.py:381
  27.8 3.3 %collective-permute-start.12 = (f32[48,128]{1,0:T(8,128)S(1)}, f32[48,128]{1,0:T(8,128)S(1)}, u32[]{:S(2)}, u32[]{:S(2)}) collective-permute-start(f32[48,128]{1,0:T(8,128)S(1)} %get-tuple-element.70.refs_3_), channel_id=1, source_target_pairs={{0,7},{1,6},{2,5},{3,4},{4,3},{5,2},{6,1},{7,0},{8,15},{9,14},{10,... | collective-permute-start | bytes 73736 | tf_op jit(solution)/shard_map/ppermute | solution.py:381
  31.2 0.0 collective-permute-start.13
  31.2 0.6 %collective-permute-start.14 = (f32[48,128]{1,0:T(8,128)S(1)}, f32[48,128]{1,0:T(8,128)S(1)}, u32[]{:S(2)}, u32[]{:S(2)}) collective-permute-start(f32[48,128]{1,0:T(8,128)S(1)} %get-tuple-element.72), channel_id=1, source_target_pairs={{0,5},{1,4},{2,7},{3,6},{4,1},{5,0},{6,3},{7,2},{8,13},{9,12},{10,... | collective-permute-start | bytes 73736 | tf_op jit(solution)/shard_map/ppermute | solution.py:381
  31.8 1.2 %collective-permute-done.12.refs_0_ = f32[48,128]{1,0:T(8,128)S(1)} collective-permute-done((f32[48,128]{1,0:T(8,128)S(1)}, f32[48,128]{1,0:T(8,128)S(1)}, u32[]{:S(2)}, u32[]{:S(2)}) %collective-permute-start.12) | collective-permute-done | bytes 24608 | tf_op jit(solution)/shard_map/ppermute | solution.py:381
  32.9 2.4 %collective-permute-done.13.refs_1_ = f32[48,128]{1,0:T(8,128)S(1)} collective-permute-done((f32[48,128]{1,0:T(8,128)S(1)}, f32[48,128]{1,0:T(8,128)S(1)}, u32[]{:S(2)}, u32[]{:S(2)}) %collective-permute-start.13) | collective-permute-done | bytes 24608 | tf_op jit(solution)/shard_map/ppermute | solution.py:381
  35.3 0.0 collective-permute-done.14.refs_2_
  35.3 2.3 %final.1 = (f32[32,1024]{1,0:T(8,128)}, f32[12,32]{1,0:T(8,128)}) custom-call(f32[48,128]{1,0:T(8,128)S(1)} %sum.5.terms_ref, f32[48,1024]{1,0:T(8,128)S(1)} %get-tuple-element.56.basis_ref, f32[48,1024]{1,0:T(8,128)S(1)} %get-tuple-element.73.jump_ref), custom_call_target="tpu_custom_call" | custom-call | bytes 1048576 | tf_op jit(solution)/shard_map/final/pallas_call | solution.py:470
  (11 shorter events, 0.1 us)
Async XLA Ops:
  2.4 7.3 %collective-permute-start = (f32[80,128]{1,0:T(8,128)S(1)}, f32[80,128]{1,0:T(8,128)S(1)}, u32[]{:S(2)}, u32[]{:S(2)}) collective-permute-start(f32[80,128]{1,0:T(8,128)S(1)} %get-tuple-element.48.refs_0_), channel_id=1, source_target_pairs={{0,28},{1,29},{2,30},{3,31},{4,24},{5,25},{6,26},{7,27},{8,20},{9,... | collective-permute-start | bytes 122888 | tf_op jit(solution)/shard_map/ppermute | solution.py:381
  5.8 3.9 %collective-permute-start.1 = (f32[80,128]{1,0:T(8,128)S(1)}, f32[80,128]{1,0:T(8,128)S(1)}, u32[]{:S(2)}, u32[]{:S(2)}) collective-permute-start(f32[80,128]{1,0:T(8,128)S(1)} %get-tuple-element.49.refs_1_), channel_id=1, source_target_pairs={{0,20},{1,21},{2,22},{3,23},{4,16},{5,17},{6,18},{7,19},{8,28},{9,... | collective-permute-start | bytes 122888 | tf_op jit(solution)/shard_map/ppermute | solution.py:381
  6.6 3.8 %collective-permute-start.2 = (f32[80,128]{1,0:T(8,128)S(1)}, f32[80,128]{1,0:T(8,128)S(1)}, u32[]{:S(2)}, u32[]{:S(2)}) collective-permute-start(f32[80,128]{1,0:T(8,128)S(1)} %get-tuple-element.50.refs_2_), channel_id=1, source_target_pairs={{0,12},{1,13},{2,14},{3,15},{4,8},{5,9},{6,10},{7,11},{8,4},{9,5},... | collective-permute-start | bytes 122888 | tf_op jit(solution)/shard_map/ppermute | solution.py:381
  10.4 1.3 %collective-permute-start.3 = (f32[160,128]{1,0:T(8,128)S(1)}, f32[160,128]{1,0:T(8,128)S(1)}, u32[]{:S(2)}, u32[]{:S(2)}) collective-permute-start(f32[160,128]{1,0:T(8,128)S(1)} %pad_maximum_fusion.1), channel_id=1, source_target_pairs={{0,4},{1,5},{2,6},{3,7},{4,0},{5,1},{6,2},{7,3},{8,12},{9,13},{10,... | collective-permute-start | bytes 245768 | tf_op jit(solution)/shard_map/ppermute | solution.py:381
  12.5 4.6 %collective-permute-start.4 = (f32[96,128]{1,0:T(8,128)S(1)}, f32[96,128]{1,0:T(8,128)S(1)}, u32[]{:S(2)}, u32[]{:S(2)}) collective-permute-start(f32[96,128]{1,0:T(8,128)S(1)} %get-tuple-element.59.refs_0_), channel_id=1, source_target_pairs={{0,28},{1,29},{2,30},{3,31},{4,24},{5,25},{6,26},{7,27},{8,20},{9,... | collective-permute-start | bytes 147464 | tf_op jit(solution)/shard_map/ppermute | solution.py:381
  14.5 3.7 %collective-permute-start.5 = (f32[96,128]{1,0:T(8,128)S(1)}, f32[96,128]{1,0:T(8,128)S(1)}, u32[]{:S(2)}, u32[]{:S(2)}) collective-permute-start(f32[96,128]{1,0:T(8,128)S(1)} %get-tuple-element.60.refs_1_), channel_id=1, source_target_pairs={{0,20},{1,21},{2,22},{3,23},{4,16},{5,17},{6,18},{7,19},{8,28},{9,... | collective-permute-start | bytes 147464 | tf_op jit(solution)/shard_map/ppermute | solution.py:381
  14.8 3.5 %collective-permute-start.6 = (f32[96,128]{1,0:T(8,128)S(1)}, f32[96,128]{1,0:T(8,128)S(1)}, u32[]{:S(2)}, u32[]{:S(2)}) collective-permute-start(f32[96,128]{1,0:T(8,128)S(1)} %get-tuple-element.61.refs_2_), channel_id=1, source_target_pairs={{0,12},{1,13},{2,14},{3,15},{4,8},{5,9},{6,10},{7,11},{8,4},{9,5},... | collective-permute-start | bytes 147464 | tf_op jit(solution)/shard_map/ppermute | solution.py:381
  18.3 1.4 %collective-permute-start.7 = (f32[192,128]{1,0:T(8,128)S(1)}, f32[192,128]{1,0:T(8,128)S(1)}, u32[]{:S(2)}, u32[]{:S(2)}) collective-permute-start(f32[192,128]{1,0:T(8,128)S(1)} %pad_maximum_fusion), channel_id=1, source_target_pairs={{0,4},{1,5},{2,6},{3,7},{4,0},{5,1},{6,2},{7,3},{8,12},{9,13},{10,... | collective-permute-start | bytes 294920 | tf_op jit(solution)/shard_map/ppermute | solution.py:381
  20.8 1.2 %collective-permute-start.8 = (f32[48,128]{1,0:T(8,128)S(1)}, f32[48,128]{1,0:T(8,128)S(1)}, u32[]{:S(2)}, u32[]{:S(2)}) collective-permute-start(f32[48,128]{1,0:T(8,128)S(1)} %get-tuple-element.66.refs_1_), channel_id=1, source_target_pairs={{0,4},{1,5},{2,6},{3,7},{4,0},{5,1},{6,2},{7,3},{8,12},{9,13},{10,... | collective-permute-start | bytes 73736 | tf_op jit(solution)/shard_map/ppermute | solution.py:381
  22.1 4.2 %collective-permute-start.10 = (f32[48,128]{1,0:T(8,128)S(1)}, f32[48,128]{1,0:T(8,128)S(1)}, u32[]{:S(2)}, u32[]{:S(2)}) collective-permute-start(f32[48,128]{1,0:T(8,128)S(1)} %get-tuple-element.68), channel_id=1, source_target_pairs={{0,28},{1,29},{2,30},{3,31},{4,24},{5,25},{6,26},{7,27},{8,20},{9,... | collective-permute-start | bytes 73736 | tf_op jit(solution)/shard_map/ppermute | solution.py:381
  24.1 3.3 %collective-permute-start.11 = (f32[48,128]{1,0:T(8,128)S(1)}, f32[48,128]{1,0:T(8,128)S(1)}, u32[]{:S(2)}, u32[]{:S(2)}) collective-permute-start(f32[48,128]{1,0:T(8,128)S(1)} %get-tuple-element.69), channel_id=1, source_target_pairs={{0,20},{1,21},{2,22},{3,23},{4,16},{5,17},{6,18},{7,19},{8,28},{9,... | collective-permute-start | bytes 73736 | tf_op jit(solution)/shard_map/ppermute | solution.py:381
  24.6 3.3 %collective-permute-start.9 = (f32[48,128]{1,0:T(8,128)S(1)}, f32[48,128]{1,0:T(8,128)S(1)}, u32[]{:S(2)}, u32[]{:S(2)}) collective-permute-start(f32[48,128]{1,0:T(8,128)S(1)} %get-tuple-element.67.refs_3_), channel_id=1, source_target_pairs={{0,12},{1,13},{2,14},{3,15},{4,8},{5,9},{6,10},{7,11},{8,4},{9,5},... | collective-permute-start | bytes 73736 | tf_op jit(solution)/shard_map/ppermute | solution.py:381
  27.8 5.1 %collective-permute-start.12 = (f32[48,128]{1,0:T(8,128)S(1)}, f32[48,128]{1,0:T(8,128)S(1)}, u32[]{:S(2)}, u32[]{:S(2)}) collective-permute-start(f32[48,128]{1,0:T(8,128)S(1)} %get-tuple-element.70.refs_3_), channel_id=1, source_target_pairs={{0,7},{1,6},{2,5},{3,4},{4,3},{5,2},{6,1},{7,0},{8,15},{9,14},{10,... | collective-permute-start | bytes 73736 | tf_op jit(solution)/shard_map/ppermute | solution.py:381
  31.2 4.2 %collective-permute-start.13 = (f32[48,128]{1,0:T(8,128)S(1)}, f32[48,128]{1,0:T(8,128)S(1)}, u32[]{:S(2)}, u32[]{:S(2)}) collective-permute-start(f32[48,128]{1,0:T(8,128)S(1)} %get-tuple-element.71), channel_id=1, source_target_pairs={{0,6},{1,7},{2,4},{3,5},{4,2},{5,3},{6,0},{7,1},{8,14},{9,15},{10,... | collective-permute-start | bytes 73736 | tf_op jit(solution)/shard_map/ppermute | solution.py:381
  31.2 4.2 %collective-permute-start.14 = (f32[48,128]{1,0:T(8,128)S(1)}, f32[48,128]{1,0:T(8,128)S(1)}, u32[]{:S(2)}, u32[]{:S(2)}) collective-permute-start(f32[48,128]{1,0:T(8,128)S(1)} %get-tuple-element.72), channel_id=1, source_target_pairs={{0,5},{1,4},{2,7},{3,6},{4,1},{5,0},{6,3},{7,2},{8,13},{9,12},{10,... | collective-permute-start | bytes 73736 | tf_op jit(solution)/shard_map/ppermute | solution.py:381

commit v6 on v5

--- a/solution.py
+++ b/solution.py
@@ -194,8 +194,42 @@
     return jnp.concatenate(sums + empty, axis=1).T
 
 
+def pack(by_mode, scalars, blocks):
+    by_mode = by_mode + pltpu.roll(by_mode, by_mode.shape[1] // 2, 1)
+    upper, lower = by_mode[:GROUP], by_mode[GROUP:]
+    row = lax.broadcasted_iota(jnp.int32, upper.shape, 0)
+    left = lax.broadcasted_iota(jnp.int32, upper.shape, 1) < upper.shape[1] // 2
+    spare = [
+        jnp.where(left, pltpu.roll(upper, 6, 0), pltpu.roll(upper, 4, 0)),
+        jnp.where(left, pltpu.roll(upper, 2, 0), pltpu.roll(lower, 6, 0)),
+        jnp.where(left, pltpu.roll(lower, 4, 0), pltpu.roll(lower, 2, 0)),
+        jnp.where(row == MODES, *scalars),
+    ]
+    rows = jnp.concatenate(blocks, axis=0)
+    parts = [jnp.where(row < MODES, rows[at * GROUP : (at + 1) * GROUP], spare[at]) for at in range(4)]
+    return jnp.concatenate(parts, axis=0)
+
+
+def unpack(terms):
+    parts = [terms[at * GROUP : (at + 1) * GROUP] for at in range(4)]
+    row = lax.broadcasted_iota(jnp.int32, parts[0].shape, 0)
+    lane = lax.broadcasted_iota(jnp.int32, parts[0].shape, 1)
+    half = terms.shape[1] // 2
+    turned = [pltpu.roll(part, half, 1) for part in parts[:3]]
+    upper = jnp.where(
+        row < 2, pltpu.roll(parts[0], 2, 0), jnp.where(row < 4, pltpu.roll(turned[0], 4, 0), pltpu.roll(parts[1], 6, 0))
+    )
+    lower = jnp.where(
+        row < 2, pltpu.roll(turned[1], 2, 0), jnp.where(row < 4, pltpu.roll(parts[2], 4, 0), pltpu.roll(turned[2], 6, 0))
+    )
+    by_mode = [jnp.where((row < MODES) & (lane < half), part, 0.0) for part in (upper, lower)]
+    blocks = [jnp.where(row < MODES, part, 0.0) for part in parts]
+    scalars = parts[3][MODES : MODES + 1], parts[3][MODES + 1 : MODES + 2]
+    return jnp.concatenate(by_mode, axis=0), scalars, [jnp.concatenate(blocks[at : at + 2], axis=0) for at in (0, 2)]
+
+
 def middle_kernel(
-    edge_ref, slots_ref, straight_ref, handed_ref, image_ref, basis_ref, terms_ref, near_ref, back_ref, stay_ref
+    edge_ref, slots_ref, straight_ref, handed_ref, image_ref, basis_ref, terms_ref, sums_ref, near_ref, back_ref, stay_ref
 ):
     image = image_ref[...]
     send_near(image, edge_ref, near_ref, back_ref, stay_ref)
@@ -215,10 +249,10 @@
     first, last = lane < loads, lane >= lanes - loads
     terms_ref[:coarse] = jnp.where(first | last, by_g, 0.0)
     terms_ref[coarse : 2 * coarse] = jnp.where(last, pltpu.roll(by_h, lanes - loads, 1), 0.0)
-    terms_ref[2 * coarse :] = jnp.where((lane >= loads) & (lane < loads + 2 * coarse), by_g, 0.0)
-    terms_ref[2 * coarse : 2 * coarse + GROUP, :loads] = by_load(
-        [residual * residual, residual * residual_image]
-    )
+    row = lax.broadcasted_iota(jnp.int32, (coarse, lanes), 0)
+    by_mode = jnp.where((lane <= row) | ((lane >= coarse) & (lane < 2 * coarse)), pltpu.roll(by_g, lanes - loads, 1), 0.0)
+    terms_ref[2 * coarse :] = by_mode
+    sums_ref[...] = by_load([residual * residual, residual * residual_image])
 
 
 def second_half_kernel(slots_ref, placed_ref, stay_ref, back_ref, *refs):
@@ -229,9 +263,11 @@
     second_ref[...] = split_dot(jump, placed_ref[0], NT)
 
 
-def second_kernel(slots_ref, placed_ref, basis_ref, half_jump_ref, half_second_ref, early_ref, got_ref, near_ref, *refs):
+def second_kernel(
+    slots_ref, placed_ref, basis_ref, half_jump_ref, half_second_ref, early_ref, sums_ref, got_ref, near_ref, *refs
+):
     *sent_refs, jump_ref, terms_ref = refs
-    coarse = terms_ref.shape[0] // 3
+    coarse = terms_ref.shape[0] // 2
     loads = basis_ref.shape[0] - coarse
     jump = for_other(near_ref, sent_refs) - handed(got_ref, loads + coarse)
     second = half_second_ref[...] + split_dot(jump, placed_ref[1], NT)
@@ -249,13 +285,21 @@
     group = lane // loads
     top = jnp.where(group == 1, by_z, jnp.where(group == 2, by_g, 0.0))
     low = jnp.where(group < 2, by_dz, jnp.where(group == 2, by_z, 0.0))
-    last = jnp.where(group == 2, pltpu.roll(by_z, lanes - loads, 1), jnp.where(lane >= lanes - coarse, by_g, 0.0))
-    terms_ref[:coarse] = early_ref[:coarse] + top
-    terms_ref[coarse : 2 * coarse] = early_ref[coarse : 2 * coarse] + low
-    terms_ref[2 * coarse :] = early_ref[2 * coarse :] + last
+    row = lax.broadcasted_iota(jnp.int32, (coarse, lanes), 0)
+    z_z = pltpu.roll(by_z, 2 * coarse, 1)
+    strip = lane // coarse
+    by_mode = jnp.where((lane > row) & (strip == 0), z_z, 0.0)
+    by_mode = jnp.where(strip == 2, pltpu.roll(by_z, 3 * coarse, 1), by_mode)
+    by_mode = jnp.where(strip == 3, pltpu.roll(by_g, 4 * coarse, 1), by_mode)
+    diagonal = jnp.sum(jnp.where(lane == row, z_z, 0.0), axis=0, keepdims=True)
     sums = by_load([jump_loads * jump_loads, jump_loads * second_loads, residual * second_loads])
-    start = 2 * coarse + GROUP
-    terms_ref[start : start + GROUP, :loads] = sums
+    scalars = (
+        jnp.concatenate([sums_ref[0:1], sums_ref[1:2], sums[0:1], sums[1:2]], axis=1),
+        jnp.concatenate([sums[2:3], diagonal[:, : lanes - loads]], axis=1),
+    )
+    terms_ref[...] = pack(
+        early_ref[2 * coarse :] + by_mode, scalars, [early_ref[:coarse] + top, early_ref[coarse : 2 * coarse] + low]
+    )
 
 
 def sum_kernel(count, *refs):
@@ -302,26 +346,25 @@
 
 
 def final_kernel(terms_ref, basis_ref, jump_ref, multipliers_ref, amplitudes_ref):
-    coarse = terms_ref.shape[0] // 3
+    coarse = terms_ref.shape[0] // 2
     loads = basis_ref.shape[0] - coarse
     groups = coarse // GROUP
 
-    def part(block, start, width):
-        return terms_ref[block * coarse : (block + 1) * coarse, start : start + width]
-
     def total(values):
         return jnp.sum(values, axis=0, keepdims=True)
 
-    def scalar(at):
-        return terms_ref[2 * coarse + at : 2 * coarse + at + 1, :loads]
-
-    res_res, res_image, jump_jump, jump_second, res_second = (scalar(at) for at in (0, 1, 8, 9, 10))
-    coarse_res, jump_z, second_g, image_g = (part(0, at * loads, loads) for at in range(4))
-    res_dz, jump_dz, second_z, res_h = (part(1, at * loads, loads) for at in range(4))
-    gram, g_h, z_z, z_dz = (part(2, loads + at * coarse, coarse) for at in range(4))
-    g_dz = part(2, terms_ref.shape[1] - coarse, coarse)
+    by_mode, (sums, last_sums), (top, low) = unpack(terms_ref[...])
+    res_res, res_image, jump_jump, jump_second = (sums[:, at * loads : (at + 1) * loads] for at in range(4))
+    res_second, diagonal = last_sums[:, :loads], last_sums[:, loads : loads + coarse]
+    coarse_res, jump_z, second_g, image_g = (top[:, at * loads : (at + 1) * loads] for at in range(4))
+    res_dz, jump_dz, second_z, res_h = (low[:, at * loads : (at + 1) * loads] for at in range(4))
+    triangles, g_h, z_dz, g_dz = (by_mode[:, at * coarse : (at + 1) * coarse] for at in range(4))
     row = lax.broadcasted_iota(jnp.int32, (coarse, coarse), 0)
-    unit = jnp.where(row == lax.broadcasted_iota(jnp.int32, (coarse, coarse), 1), 1.0, 0.0)
+    column = lax.broadcasted_iota(jnp.int32, (coarse, coarse), 1)
+    unit = jnp.where(row == column, 1.0, 0.0)
+    other = triangles.T
+    gram = jnp.where(row >= column, triangles, other)
+    z_z = jnp.where(row < column, triangles, jnp.where(row == column, diagonal, other))
     empty = jnp.zeros((coarse, 5 * coarse - 2 * loads), jnp.float32)
     solved = eliminate(
         jnp.concatenate([gram, g_h, coarse_res, image_g, unit, empty], axis=1), coarse
@@ -457,15 +500,16 @@
         first_kernel, [half, tall, *pairs(height)], [VMEM] * (5 + len(send)), "first"
     )(far, placed, half_image, got_near, near, *send)
     got = to_chips(*image_send)
-    basis, terms, near, back, stay = call(
-        middle_kernel, [tall, wide, *singles(height)], [VMEM] * 5, "middle", flops=4 * rows * rows * height
+    basis, terms, sums, near, back, stay = call(
+        middle_kernel, [tall, wide, ((GROUP, loads), f32), *singles(height)], [VMEM] * 5, "middle", flops=4 * rows * rows * height
     )(edge, slots, straight_jump, handed_jump, image)
     got_near = to_core(near, *got)
     half_jump, half_second = call(
         second_half_kernel, [tall, tall], [VMEM] * (4 + 2 * len(got)), "second_half", flops=4 * rows * rows * height
     )(slots, placed, stay, back, *image_send, *got)
-    jump, terms = call(second_kernel, [tall, wide], [VMEM] * (8 + len(got)), "second")(
-        slots, placed, basis, half_jump, half_second, terms, got_near, near, *image_send
+    packed = ((2 * GROUP * groups, 4 * loads), f32)
+    jump, terms = call(second_kernel, [tall, packed], [VMEM] * (9 + len(got)), "second")(
+        slots, placed, basis, half_jump, half_second, terms, sums, got_near, near, *image_send
     )
     multipliers, amplitudes = call(
         final_kernel, [((loads, rows), f32), ((MODES * groups, loads), f32)], [VMEM] * 3, "final"

time: 37.9 us -> 37.9 us (level)
  no operation moved by 1% of the time
where the time goes in v6:
time: 37.9 us; the launch traced here: 37.7 us
  starting transfers between devices  15.4 us (41%)
  Pallas kernels  11.7 us (31%)
  waiting for transfers between devices  9.77 us (26%)
  between operations  0.74 us (2%)
    ppermute x15, starting transfers between devices, permute(): lax.ppermute(values, ('sub', 'rep'), [(at, at ^ offset) for at in range(p...  15.4 us
    ppermute x15, waiting for transfers between devices, permute(): lax.ppermute(values, ('sub', 'rep'), [(at, at ^ offset) for at in range(p...  9.77 us
    pallas_call x1, Pallas kernels, fused_body(): call(ready_kernel, [((rows, 3 * per_peer), jnp.bfloat16), halves, halves,...  2.97 us
    pallas_call x1, Pallas kernels, fused_body(): call(final_kernel, [((loads, rows), f32), ((MODES * groups, loads), f32)]...  2.47 us
    pallas_call x1, Pallas kernels, fused_body(): call(place_kernel, [((rows, rows - 2 * per_peer), jnp.bfloat16), ((short,...  1.77 us
    pallas_call x1, Pallas kernels, fused_body(): call(middle_kernel, [tall, wide, ((GROUP, loads), f32), *singles(height)]...  1.29 us
    pallas_call x1, Pallas kernels, fused_body(): call(second_kernel, [tall, packed], [VMEM] * (9 + len(got)), 'second')  1.25 us
    pallas_call x1, Pallas kernels, fused_body(): call(first_kernel, [half, tall, *pairs(height)], [VMEM] * (5 + len(send))...  0.79 us
  transfers between devices with their start and end apart: 15, of which 12 were waited for; matrix products, arithmetic and copies ran while one was open for 0% of the time, Pallas kernels for 14%

profile of v6, /device:TPU:0, one launch (start us, length us, event | category | flops | bytes accessed | tf_op | source)
XLA Modules:
  0.0 37.7 jit_solution(4674416153947334856)
XLA Ops:
  0.6 1.8 %place.1 = (bf16[1024,768]{1,0:T(8,128)(2,1)S(1)}, f32[40,1024]{1,0:T(8,128)S(1)}, bf16[1,1024,1024]{2,1,0:T(8,128)(2,1)S(1)}, s32[1,1024]{1,0:T(1,128)S(1)}, f3...) custom-call(s32[1,1024]{1,0:T(1,128)} %route_hbm.1, s32[1,32]{1,0:T(1,128)} %bitcast.4, ...), custom_call_target="tpu_custom_call" | custom-call | bytes 1048576 | tf_op jit(solution)/shard_map/place/pallas_call | solution.py:472
  2.4 3.4 %collective-permute-start = (f32[80,128]{1,0:T(8,128)S(1)}, f32[80,128]{1,0:T(8,128)S(1)}, u32[]{:S(2)}, u32[]{:S(2)}) collective-permute-start(f32[80,128]{1,0:T(8,128)S(1)} %get-tuple-element.49.refs_0_), channel_id=1, source_target_pairs={{0,28},{1,29},{2,30},{3,31},{4,24},{5,25},{6,26},{7,27},{8,20},{9,... | collective-permute-start | bytes 122888 | tf_op jit(solution)/shard_map/ppermute | solution.py:424
  5.8 0.8 %collective-permute-start.1 = (f32[80,128]{1,0:T(8,128)S(1)}, f32[80,128]{1,0:T(8,128)S(1)}, u32[]{:S(2)}, u32[]{:S(2)}) collective-permute-start(f32[80,128]{1,0:T(8,128)S(1)} %get-tuple-element.50.refs_1_), channel_id=1, source_target_pairs={{0,20},{1,21},{2,22},{3,23},{4,16},{5,17},{6,18},{7,19},{8,28},{9,... | collective-permute-start | bytes 122888 | tf_op jit(solution)/shard_map/ppermute | solution.py:424
  6.6 0.1 collective-permute-start.2
  6.7 3.0 %ready.1 = (bf16[1024,384]{1,0:T(8,128)(2,1)S(1)}, bf16[2,1024,512]{2,1,0:T(8,128)(2,1)S(1)}, bf16[2,1024,512]{2,1,0:T(8,128)(2,1)S(1)}, f32[40,128]{1,0:T(8,128...) custom-call(s32[1,1024]{1,0:T(1,128)S(1)} %get-tuple-element.40.route_ref, ...), custom_call_target="tpu_custom_call" | custom-call | flops 2147483648 | bytes 1048576 | tf_op jit(solution)/shard_map/ready/pallas_call | solution.py:487
  9.7 0.0 collective-permute-done.refs_3_
  9.7 0.0 collective-permute-done.1.refs_4_
  9.7 0.6 %collective-permute-done.2.refs_5_ = f32[80,128]{1,0:T(8,128)S(1)} collective-permute-done((f32[80,128]{1,0:T(8,128)S(1)}, f32[80,128]{1,0:T(8,128)S(1)}, u32[]{:S(2)}, u32[]{:S(2)}) %collective-permute-start.2) | collective-permute-done | bytes 40992 | tf_op jit(solution)/shard_map/ppermute | solution.py:424
  10.4 0.2 collective-permute-start.3
  10.6 0.4 %first_half.1 = (f32[48,512]{1,0:T(8,128)S(1)}, f32[48,1024]{1,0:T(8,128)S(1)}) custom-call(bf16[2,1024,512]{2,1,0:T(8,128)(2,1)S(1)} %get-tuple-element.45.placed_ref, f32[40,128]{1,0:T(8,128)S(1)} %get-tuple-element.47.stay_ref, f32[40,128]{1,0:T(8,128)S(1)} %get-tuple-element.48.back_ref, f32[80,128]{1,0:T(8,128)S(1)} %get-tuple-element.49.refs_0_, ...), custom_call_target="tpu_custom_call" | custom-call | flops 100663296 | bytes 1048576 | tf_op jit(solution)/shard_map/first_half/pallas_call | solution.py:496
  11.0 0.7 %collective-permute-done.3.got_ref = f32[160,128]{1,0:T(8,128)S(1)} collective-permute-done((f32[160,128]{1,0:T(8,128)S(1)}, f32[160,128]{1,0:T(8,128)S(1)}, u32[]{:S(2)}, u32[]{:S(2)}) %collective-permute-start.3) | collective-permute-done | bytes 81952 | tf_op jit(solution)/shard_map/ppermute | solution.py:424
  11.7 0.8 %first.1 = (f32[48,512]{1,0:T(8,128)S(1)}, f32[48,1024]{1,0:T(8,128)S(1)}, f32[96,128]{1,0:T(8,128)S(1)}, f32[96,128]{1,0:T(8,128)S(1)}, f32[96,128]{1,0:T(8,128)S(1)}) custom-call(bf16[1024,768]{1,0:T(8,128)(2,1)S(1)} %get-tuple-element.41.far_ref, bf16[2,1024,512]{2,1,0:T(8,128)(2,1)S(1)} %get-tuple-element.45.placed_ref, ...), custom_call_target="tpu_custom_call" | custom-call | bytes 1048576 | tf_op jit(solution)/shard_map/first/pallas_call | solution.py:499
  12.5 2.0 %collective-permute-start.4 = (f32[96,128]{1,0:T(8,128)S(1)}, f32[96,128]{1,0:T(8,128)S(1)}, u32[]{:S(2)}, u32[]{:S(2)}) collective-permute-start(f32[96,128]{1,0:T(8,128)S(1)} %get-tuple-element.60.refs_0_), channel_id=1, source_target_pairs={{0,28},{1,29},{2,30},{3,31},{4,24},{5,25},{6,26},{7,27},{8,20},{9,... | collective-permute-start | bytes 147464 | tf_op jit(solution)/shard_map/ppermute | solution.py:424
  14.5 0.3 collective-permute-start.5
  14.8 0.8 %collective-permute-start.6 = (f32[96,128]{1,0:T(8,128)S(1)}, f32[96,128]{1,0:T(8,128)S(1)}, u32[]{:S(2)}, u32[]{:S(2)}) collective-permute-start(f32[96,128]{1,0:T(8,128)S(1)} %get-tuple-element.62.refs_2_), channel_id=1, source_target_pairs={{0,12},{1,13},{2,14},{3,15},{4,8},{5,9},{6,10},{7,11},{8,4},{9,5},... | collective-permute-start | bytes 147464 | tf_op jit(solution)/shard_map/ppermute | solution.py:424
  15.5 1.3 %middle.1 = (f32[48,1024]{1,0:T(8,128)S(1)}, f32[48,128]{1,0:T(8,128)S(1)}, f32[8,32]{1,0:T(8,128)S(1)}, f32[48,128]{1,0:T(8,128)S(1)}, f32[48,128]{1,0:T(8,128)S(1)}, /*index=5*/f32[48,128]{1,0:T(8,128)S(1)}) custom-call(bf16[1024,384]{1,0:T(8,128)(2,1)S(1)} %get-tuple-element.46.edge_ref, bf16[2,1024,512]{2,1,0:T(8,128)(2,1)S(1)} %get-tuple-element.44.slots_ref, ...), custom_call_target="tpu_custom_call" | custom-call | flops 201326592 | bytes 1048576 | tf_op jit(solution)/shard_map/middle/pallas_call | solution.py:503
  16.8 0.3 collective-permute-done.4.refs_3_
  17.2 1.0 %collective-permute-done.5.refs_4_ = f32[96,128]{1,0:T(8,128)S(1)} collective-permute-done((f32[96,128]{1,0:T(8,128)S(1)}, f32[96,128]{1,0:T(8,128)S(1)}, u32[]{:S(2)}, u32[]{:S(2)}) %collective-permute-start.5) | collective-permute-done | bytes 49184 | tf_op jit(solution)/shard_map/ppermute | solution.py:424
  18.2 0.1 collective-permute-done.6.refs_5_
  18.3 0.4 %collective-permute-start.7 = (f32[192,128]{1,0:T(8,128)S(1)}, f32[192,128]{1,0:T(8,128)S(1)}, u32[]{:S(2)}, u32[]{:S(2)}) collective-permute-start(f32[192,128]{1,0:T(8,128)S(1)} %pad_maximum_fusion), channel_id=1, source_target_pairs={{0,4},{1,5},{2,6},{3,7},{4,0},{5,1},{6,2},{7,3},{8,12},{9,13},{10,... | collective-permute-start | bytes 294920 | tf_op jit(solution)/shard_map/ppermute | solution.py:424
  18.7 0.7 %second_half.1 = (f32[48,1024]{1,0:T(8,128)S(1)}, f32[48,1024]{1,0:T(8,128)S(1)}) custom-call(bf16[2,1024,512]{2,1,0:T(8,128)(2,1)S(1)} %get-tuple-element.44.slots_ref, bf16[2,1024,512]{2,1,0:T(8,128)(2,1)S(1)} %get-tuple-element.45.placed_ref, f32[48,128]{1,0:T(8,128)S(1)} %get-tuple-element.58.stay_ref, f32[48,128]{1,0:T(8,128)S(1)} %get-tuple-element.59.back_ref, ...), custom_call_target="tpu_custom_call" | custom-call | flops 201326592 | bytes 1048576 | tf_op jit(solution)/shard_map/second_half/pallas_call | solution.py:507
  19.5 0.2 collective-permute-done.7.got_ref
  19.7 1.3 %second.1 = (f32[48,1024]{1,0:T(8,128)S(1)}, f32[32,128]{1,0:T(8,128)S(1)}) custom-call(bf16[2,1024,512]{2,1,0:T(8,128)(2,1)S(1)} %get-tuple-element.44.slots_ref, bf16[2,1024,512]{2,1,0:T(8,128)(2,1)S(1)} %get-tuple-element.45.placed_ref, f32[48,1024]{1,0:T(8,128)S(1)} %get-tuple-element.57.basis_ref, f32[48,1024]{1,0:T(8,128)S(1)} %get-tuple-element.63.half_jump_ref, ...), custom_call_target="tpu_custom_call" | custom-call | bytes 1048576 | tf_op jit(solution)/shard_map/second/pallas_call | solution.py:511
  20.9 0.4 %collective-permute-start.8 = (f32[32,128]{1,0:T(8,128)S(1)}, f32[32,128]{1,0:T(8,128)S(1)}, u32[]{:S(2)}, u32[]{:S(2)}) collective-permute-start(f32[32,128]{1,0:T(8,128)S(1)} %get-tuple-element.68.refs_1_), channel_id=1, source_target_pairs={{0,4},{1,5},{2,6},{3,7},{4,0},{5,1},{6,2},{7,3},{8,12},{9,13},{10,... | collective-permute-start | bytes 49160 | tf_op jit(solution)/shard_map/ppermute | solution.py:424
  21.3 0.8 %collective-permute-done.8.refs_0_ = f32[32,128]{1,0:T(8,128)S(1)} collective-permute-done((f32[32,128]{1,0:T(8,128)S(1)}, f32[32,128]{1,0:T(8,128)S(1)}, u32[]{:S(2)}, u32[]{:S(2)}) %collective-permute-start.8) | collective-permute-done | bytes 16416 | tf_op jit(solution)/shard_map/ppermute | solution.py:424
  22.2 2.0 %collective-permute-start.10 = (f32[32,128]{1,0:T(8,128)S(1)}, f32[32,128]{1,0:T(8,128)S(1)}, u32[]{:S(2)}, u32[]{:S(2)}) collective-permute-start(f32[32,128]{1,0:T(8,128)S(1)} %get-tuple-element.70), channel_id=1, source_target_pairs={{0,28},{1,29},{2,30},{3,31},{4,24},{5,25},{6,26},{7,27},{8,20},{9,... | collective-permute-start | bytes 49160 | tf_op jit(solution)/shard_map/ppermute | solution.py:424
  24.1 0.5 %collective-permute-start.11 = (f32[32,128]{1,0:T(8,128)S(1)}, f32[32,128]{1,0:T(8,128)S(1)}, u32[]{:S(2)}, u32[]{:S(2)}) collective-permute-start(f32[32,128]{1,0:T(8,128)S(1)} %get-tuple-element.71), channel_id=1, source_target_pairs={{0,20},{1,21},{2,22},{3,23},{4,16},{5,17},{6,18},{7,19},{8,28},{9,... | collective-permute-start | bytes 49160 | tf_op jit(solution)/shard_map/ppermute | solution.py:424
  24.6 0.7 %collective-permute-start.9 = (f32[32,128]{1,0:T(8,128)S(1)}, f32[32,128]{1,0:T(8,128)S(1)}, u32[]{:S(2)}, u32[]{:S(2)}) collective-permute-start(f32[32,128]{1,0:T(8,128)S(1)} %get-tuple-element.69.refs_3_), channel_id=1, source_target_pairs={{0,12},{1,13},{2,14},{3,15},{4,8},{5,9},{6,10},{7,11},{8,4},{9,5},... | collective-permute-start | bytes 49160 | tf_op jit(solution)/shard_map/ppermute | solution.py:424
  25.3 0.9 %collective-permute-done.10.refs_1_ = f32[32,128]{1,0:T(8,128)S(1)} collective-permute-done((f32[32,128]{1,0:T(8,128)S(1)}, f32[32,128]{1,0:T(8,128)S(1)}, u32[]{:S(2)}, u32[]{:S(2)}) %collective-permute-start.10) | collective-permute-done | bytes 16416 | tf_op jit(solution)/shard_map/ppermute | solution.py:424
  26.2 1.1 %collective-permute-done.11.refs_2_ = f32[32,128]{1,0:T(8,128)S(1)} collective-permute-done((f32[32,128]{1,0:T(8,128)S(1)}, f32[32,128]{1,0:T(8,128)S(1)}, u32[]{:S(2)}, u32[]{:S(2)}) %collective-permute-start.11) | collective-permute-done | bytes 16416 | tf_op jit(solution)/shard_map/ppermute | solution.py:424
  27.3 0.5 %collective-permute-done.9.refs_0_ = f32[32,128]{1,0:T(8,128)S(1)} collective-permute-done((f32[32,128]{1,0:T(8,128)S(1)}, f32[32,128]{1,0:T(8,128)S(1)}, u32[]{:S(2)}, u32[]{:S(2)}) %collective-permute-start.9) | collective-permute-done | bytes 16416 | tf_op jit(solution)/shard_map/ppermute | solution.py:424
  27.8 3.4 %collective-permute-start.12 = (f32[32,128]{1,0:T(8,128)S(1)}, f32[32,128]{1,0:T(8,128)S(1)}, u32[]{:S(2)}, u32[]{:S(2)}) collective-permute-start(f32[32,128]{1,0:T(8,128)S(1)} %get-tuple-element.72.refs_3_), channel_id=1, source_target_pairs={{0,7},{1,6},{2,5},{3,4},{4,3},{5,2},{6,1},{7,0},{8,15},{9,14},{10,... | collective-permute-start | bytes 49160 | tf_op jit(solution)/shard_map/ppermute | solution.py:424
  31.2 0.0 collective-permute-start.13
  31.2 0.6 %collective-permute-start.14 = (f32[32,128]{1,0:T(8,128)S(1)}, f32[32,128]{1,0:T(8,128)S(1)}, u32[]{:S(2)}, u32[]{:S(2)}) collective-permute-start(f32[32,128]{1,0:T(8,128)S(1)} %get-tuple-element.74), channel_id=1, source_target_pairs={{0,5},{1,4},{2,7},{3,6},{4,1},{5,0},{6,3},{7,2},{8,13},{9,12},{10,... | collective-permute-start | bytes 49160 | tf_op jit(solution)/shard_map/ppermute | solution.py:424
  31.7 1.1 %collective-permute-done.12.refs_0_ = f32[32,128]{1,0:T(8,128)S(1)} collective-permute-done((f32[32,128]{1,0:T(8,128)S(1)}, f32[32,128]{1,0:T(8,128)S(1)}, u32[]{:S(2)}, u32[]{:S(2)}) %collective-permute-start.12) | collective-permute-done | bytes 16416 | tf_op jit(solution)/shard_map/ppermute | solution.py:424
  32.8 2.4 %collective-permute-done.13.refs_1_ = f32[32,128]{1,0:T(8,128)S(1)} collective-permute-done((f32[32,128]{1,0:T(8,128)S(1)}, f32[32,128]{1,0:T(8,128)S(1)}, u32[]{:S(2)}, u32[]{:S(2)}) %collective-permute-start.13) | collective-permute-done | bytes 16416 | tf_op jit(solution)/shard_map/ppermute | solution.py:424
  35.2 0.0 collective-permute-done.14.refs_2_
  35.2 2.5 %final.1 = (f32[32,1024]{1,0:T(8,128)}, f32[12,32]{1,0:T(8,128)}) custom-call(f32[32,128]{1,0:T(8,128)S(1)} %sum.5.terms_ref, f32[48,1024]{1,0:T(8,128)S(1)} %get-tuple-element.57.basis_ref, f32[48,1024]{1,0:T(8,128)S(1)} %get-tuple-element.75.jump_ref), custom_call_target="tpu_custom_call" | custom-call | bytes 1048576 | tf_op jit(solution)/shard_map/final/pallas_call | solution.py:514
  (11 shorter events, 0.1 us)
Async XLA Ops:
  2.4 7.3 %collective-permute-start = (f32[80,128]{1,0:T(8,128)S(1)}, f32[80,128]{1,0:T(8,128)S(1)}, u32[]{:S(2)}, u32[]{:S(2)}) collective-permute-start(f32[80,128]{1,0:T(8,128)S(1)} %get-tuple-element.49.refs_0_), channel_id=1, source_target_pairs={{0,28},{1,29},{2,30},{3,31},{4,24},{5,25},{6,26},{7,27},{8,20},{9,... | collective-permute-start | bytes 122888 | tf_op jit(solution)/shard_map/ppermute | solution.py:424
  5.8 3.9 %collective-permute-start.1 = (f32[80,128]{1,0:T(8,128)S(1)}, f32[80,128]{1,0:T(8,128)S(1)}, u32[]{:S(2)}, u32[]{:S(2)}) collective-permute-start(f32[80,128]{1,0:T(8,128)S(1)} %get-tuple-element.50.refs_1_), channel_id=1, source_target_pairs={{0,20},{1,21},{2,22},{3,23},{4,16},{5,17},{6,18},{7,19},{8,28},{9,... | collective-permute-start | bytes 122888 | tf_op jit(solution)/shard_map/ppermute | solution.py:424
  6.6 3.8 %collective-permute-start.2 = (f32[80,128]{1,0:T(8,128)S(1)}, f32[80,128]{1,0:T(8,128)S(1)}, u32[]{:S(2)}, u32[]{:S(2)}) collective-permute-start(f32[80,128]{1,0:T(8,128)S(1)} %get-tuple-element.51.refs_2_), channel_id=1, source_target_pairs={{0,12},{1,13},{2,14},{3,15},{4,8},{5,9},{6,10},{7,11},{8,4},{9,5},... | collective-permute-start | bytes 122888 | tf_op jit(solution)/shard_map/ppermute | solution.py:424
  10.4 1.3 %collective-permute-start.3 = (f32[160,128]{1,0:T(8,128)S(1)}, f32[160,128]{1,0:T(8,128)S(1)}, u32[]{:S(2)}, u32[]{:S(2)}) collective-permute-start(f32[160,128]{1,0:T(8,128)S(1)} %pad_maximum_fusion.1), channel_id=1, source_target_pairs={{0,4},{1,5},{2,6},{3,7},{4,0},{5,1},{6,2},{7,3},{8,12},{9,13},{10,... | collective-permute-start | bytes 245768 | tf_op jit(solution)/shard_map/ppermute | solution.py:424
  12.5 4.6 %collective-permute-start.4 = (f32[96,128]{1,0:T(8,128)S(1)}, f32[96,128]{1,0:T(8,128)S(1)}, u32[]{:S(2)}, u32[]{:S(2)}) collective-permute-start(f32[96,128]{1,0:T(8,128)S(1)} %get-tuple-element.60.refs_0_), channel_id=1, source_target_pairs={{0,28},{1,29},{2,30},{3,31},{4,24},{5,25},{6,26},{7,27},{8,20},{9,... | collective-permute-start | bytes 147464 | tf_op jit(solution)/shard_map/ppermute | solution.py:424
  14.5 3.7 %collective-permute-start.5 = (f32[96,128]{1,0:T(8,128)S(1)}, f32[96,128]{1,0:T(8,128)S(1)}, u32[]{:S(2)}, u32[]{:S(2)}) collective-permute-start(f32[96,128]{1,0:T(8,128)S(1)} %get-tuple-element.61.refs_1_), channel_id=1, source_target_pairs={{0,20},{1,21},{2,22},{3,23},{4,16},{5,17},{6,18},{7,19},{8,28},{9,... | collective-permute-start | bytes 147464 | tf_op jit(solution)/shard_map/ppermute | solution.py:424
  14.8 3.5 %collective-permute-start.6 = (f32[96,128]{1,0:T(8,128)S(1)}, f32[96,128]{1,0:T(8,128)S(1)}, u32[]{:S(2)}, u32[]{:S(2)}) collective-permute-start(f32[96,128]{1,0:T(8,128)S(1)} %get-tuple-element.62.refs_2_), channel_id=1, source_target_pairs={{0,12},{1,13},{2,14},{3,15},{4,8},{5,9},{6,10},{7,11},{8,4},{9,5},... | collective-permute-start | bytes 147464 | tf_op jit(solution)/shard_map/ppermute | solution.py:424
  18.3 1.4 %collective-permute-start.7 = (f32[192,128]{1,0:T(8,128)S(1)}, f32[192,128]{1,0:T(8,128)S(1)}, u32[]{:S(2)}, u32[]{:S(2)}) collective-permute-start(f32[192,128]{1,0:T(8,128)S(1)} %pad_maximum_fusion), channel_id=1, source_target_pairs={{0,4},{1,5},{2,6},{3,7},{4,0},{5,1},{6,2},{7,3},{8,12},{9,13},{10,... | collective-permute-start | bytes 294920 | tf_op jit(solution)/shard_map/ppermute | solution.py:424
  20.9 1.3 %collective-permute-start.8 = (f32[32,128]{1,0:T(8,128)S(1)}, f32[32,128]{1,0:T(8,128)S(1)}, u32[]{:S(2)}, u32[]{:S(2)}) collective-permute-start(f32[32,128]{1,0:T(8,128)S(1)} %get-tuple-element.68.refs_1_), channel_id=1, source_target_pairs={{0,4},{1,5},{2,6},{3,7},{4,0},{5,1},{6,2},{7,3},{8,12},{9,13},{10,... | collective-permute-start | bytes 49160 | tf_op jit(solution)/shard_map/ppermute | solution.py:424
  22.2 4.1 %collective-permute-start.10 = (f32[32,128]{1,0:T(8,128)S(1)}, f32[32,128]{1,0:T(8,128)S(1)}, u32[]{:S(2)}, u32[]{:S(2)}) collective-permute-start(f32[32,128]{1,0:T(8,128)S(1)} %get-tuple-element.70), channel_id=1, source_target_pairs={{0,28},{1,29},{2,30},{3,31},{4,24},{5,25},{6,26},{7,27},{8,20},{9,... | collective-permute-start | bytes 49160 | tf_op jit(solution)/shard_map/ppermute | solution.py:424
  24.1 3.2 %collective-permute-start.11 = (f32[32,128]{1,0:T(8,128)S(1)}, f32[32,128]{1,0:T(8,128)S(1)}, u32[]{:S(2)}, u32[]{:S(2)}) collective-permute-start(f32[32,128]{1,0:T(8,128)S(1)} %get-tuple-element.71), channel_id=1, source_target_pairs={{0,20},{1,21},{2,22},{3,23},{4,16},{5,17},{6,18},{7,19},{8,28},{9,... | collective-permute-start | bytes 49160 | tf_op jit(solution)/shard_map/ppermute | solution.py:424
  24.6 3.2 %collective-permute-start.9 = (f32[32,128]{1,0:T(8,128)S(1)}, f32[32,128]{1,0:T(8,128)S(1)}, u32[]{:S(2)}, u32[]{:S(2)}) collective-permute-start(f32[32,128]{1,0:T(8,128)S(1)} %get-tuple-element.69.refs_3_), channel_id=1, source_target_pairs={{0,12},{1,13},{2,14},{3,15},{4,8},{5,9},{6,10},{7,11},{8,4},{9,5},... | collective-permute-start | bytes 49160 | tf_op jit(solution)/shard_map/ppermute | solution.py:424
  27.8 5.0 %collective-permute-start.12 = (f32[32,128]{1,0:T(8,128)S(1)}, f32[32,128]{1,0:T(8,128)S(1)}, u32[]{:S(2)}, u32[]{:S(2)}) collective-permute-start(f32[32,128]{1,0:T(8,128)S(1)} %get-tuple-element.72.refs_3_), channel_id=1, source_target_pairs={{0,7},{1,6},{2,5},{3,4},{4,3},{5,2},{6,1},{7,0},{8,15},{9,14},{10,... | collective-permute-start | bytes 49160 | tf_op jit(solution)/shard_map/ppermute | solution.py:424
  31.2 4.1 %collective-permute-start.13 = (f32[32,128]{1,0:T(8,128)S(1)}, f32[32,128]{1,0:T(8,128)S(1)}, u32[]{:S(2)}, u32[]{:S(2)}) collective-permute-start(f32[32,128]{1,0:T(8,128)S(1)} %get-tuple-element.73), channel_id=1, source_target_pairs={{0,6},{1,7},{2,4},{3,5},{4,2},{5,3},{6,0},{7,1},{8,14},{9,15},{10,... | collective-permute-start | bytes 49160 | tf_op jit(solution)/shard_map/ppermute | solution.py:424
  31.2 4.1 %collective-permute-start.14 = (f32[32,128]{1,0:T(8,128)S(1)}, f32[32,128]{1,0:T(8,128)S(1)}, u32[]{:S(2)}, u32[]{:S(2)}) collective-permute-start(f32[32,128]{1,0:T(8,128)S(1)} %get-tuple-element.74), channel_id=1, source_target_pairs={{0,5},{1,4},{2,7},{3,6},{4,1},{5,0},{6,3},{7,2},{8,13},{9,12},{10,... | collective-permute-start | bytes 49160 | tf_op jit(solution)/shard_map/ppermute | solution.py:424

commit v7 on v6

--- a/solution.py
+++ b/solution.py
@@ -63,8 +63,10 @@
     return jnp.concatenate([near_ref[...], *(ref[height:] for ref in pair_refs)], axis=1)
 
 
-def handed(got_ref, height):
-    return jnp.concatenate([got_ref[at : at + height] for at in range(0, got_ref.shape[0], height)], axis=1)
+def handed(got_ref, height, backwards=False):
+    starts = list(range(height, got_ref.shape[0], height))
+    starts = [0, *(starts[::-1] if backwards else starts)]
+    return jnp.concatenate([got_ref[at : at + height] for at in starts], axis=1)
 
 
 def spread(values, loads, groups):
@@ -228,8 +230,40 @@
     return jnp.concatenate(by_mode, axis=0), scalars, [jnp.concatenate(blocks[at : at + 2], axis=0) for at in (0, 2)]
 
 
+def powers(coarse, loads):
+    lane = lax.broadcasted_iota(jnp.int32, (coarse, 4 * loads), 1)
+    row = lax.broadcasted_iota(jnp.int32, (coarse, 4 * loads), 0)
+
+    def choose(at, *values):
+        return functools.reduce(lambda rest, pair: jnp.where(at == pair[0], pair[1], rest), enumerate(values), 0.0 * lane)
+
+    strip, group = lane // coarse, lane // loads
+    by_mode = choose(strip, jnp.where(lane > row, 2.0, 0.0), 1.0, 3.0, 2.0)
+    scalars = choose(group, 0.0, 1.0, 2.0, 3.0), choose(group, 2.0, 2.0)
+    blocks = [choose(group, 0.0, 2.0, 2.0, 1.0), choose(group, 2.0, 3.0, 3.0, 1.0)]
+    return pack(by_mode, [line[:1] for line in scalars], blocks)
+
+
+def magnitude(operator_ref):
+    tall = 2 * GROUP
+    largest = jnp.zeros((tall, operator_ref.shape[2]), operator_ref.dtype)
+    for start in range(0, operator_ref.shape[1], tall):
+        part = operator_ref[0, start : start + tall]
+        largest = jnp.maximum(largest, jnp.maximum(part, -part))
+    largest = jnp.max(largest.astype(jnp.float32), axis=0, keepdims=True)
+    return jnp.clip(jnp.max(largest, axis=1, keepdims=True), 1e-30, 1e30)
+
+
+def scale_of(terms):
+    last = terms[-GROUP:]
+    half = last.shape[1] // 2
+    lane = lax.broadcasted_iota(jnp.int32, last.shape, 1)
+    return jnp.where(lane < half, pltpu.roll(last, half, 1), last)[GROUP - 1 :]
+
+
 def middle_kernel(
-    edge_ref, slots_ref, straight_ref, handed_ref, image_ref, basis_ref, terms_ref, sums_ref, near_ref, back_ref, stay_ref
+    edge_ref, slots_ref, operator_ref, straight_ref, handed_ref, image_ref,
+    basis_ref, scale_ref, powers_ref, terms_ref, sums_ref, near_ref, back_ref, stay_ref,
 ):
     image = image_ref[...]
     send_near(image, edge_ref, near_ref, back_ref, stay_ref)
@@ -237,8 +271,12 @@
     loads = image.shape[0] - coarse
     basis = split_dot(straight_ref[...], slots_ref[0], NT) + split_dot(handed_ref[...], slots_ref[1], NT)
     basis_ref[...] = basis
+    scale = magnitude(operator_ref)
+    scale_ref[...] = jnp.broadcast_to(scale, scale_ref.shape)
+    image = image * (1.0 / scale)
     residual, residual_image = basis[:loads], image[:loads]
     lanes = terms_ref.shape[1]
+    powers_ref[...] = powers(coarse, loads)
     empty = jnp.zeros((lanes - 2 * loads - 2 * coarse, basis.shape[1]), jnp.float32)
     both = products_of(
         jnp.concatenate([basis[loads:], image[loads:]]),
@@ -264,14 +302,16 @@
 
 
 def second_kernel(
-    slots_ref, placed_ref, basis_ref, half_jump_ref, half_second_ref, early_ref, sums_ref, got_ref, near_ref, *refs
+    slots_ref, placed_ref, basis_ref, half_jump_ref, half_second_ref, scale_ref, early_ref, sums_ref, got_ref,
+    near_ref, *refs,
 ):
     *sent_refs, jump_ref, terms_ref = refs
     coarse = terms_ref.shape[0] // 2
     loads = basis_ref.shape[0] - coarse
-    jump = for_other(near_ref, sent_refs) - handed(got_ref, loads + coarse)
-    second = half_second_ref[...] + split_dot(jump, placed_ref[1], NT)
-    jump = half_jump_ref[...] + split_dot(jump, slots_ref[1], NT)
+    jump = for_other(near_ref, sent_refs) - handed(got_ref, loads + coarse, backwards=True)
+    inverse = 1.0 / scale_ref[:1]
+    second = (half_second_ref[...] + split_dot(jump, placed_ref[1], NT)) * inverse * inverse
+    jump = (half_jump_ref[...] + split_dot(jump, slots_ref[1], NT)) * inverse
     jump_ref[...] = jump
     basis = basis_ref[...]
     residual, jump_loads, second_loads = basis[:loads], jump[:loads], second[:loads]
@@ -295,19 +335,29 @@
     sums = by_load([jump_loads * jump_loads, jump_loads * second_loads, residual * second_loads])
     scalars = (
         jnp.concatenate([sums_ref[0:1], sums_ref[1:2], sums[0:1], sums[1:2]], axis=1),
-        jnp.concatenate([sums[2:3], diagonal[:, : lanes - loads]], axis=1),
+        jnp.concatenate([sums[2:3], diagonal[:, :loads], scale_ref[:1, : 2 * loads]], axis=1),
     )
     terms_ref[...] = pack(
         early_ref[2 * coarse :] + by_mode, scalars, [early_ref[:coarse] + top, early_ref[coarse : 2 * coarse] + low]
     )
 
 
-def sum_kernel(count, *refs):
+def sum_kernel(count, powers_ref, *refs):
     parts = [ref[...] for ref in reversed(refs[:count])]
+    scales = [scale_of(part) for part in parts]
+    largest = functools.reduce(jnp.maximum, scales)
+    power = powers_ref[...]
+    for at, scale in enumerate(scales):
+        factor = scale / largest
+        for least in range(3):
+            parts[at] = parts[at] * jnp.where(power > least, factor, 1.0)
     while len(parts) > 1:
         parts = [low + high for low, high in zip(parts[::2], parts[1::2])]
+    row = lax.broadcasted_iota(jnp.int32, power.shape, 0)
+    lane = lax.broadcasted_iota(jnp.int32, power.shape, 1)
+    total = jnp.where((row == power.shape[0] - 1) & (lane >= power.shape[1] // 2), largest, parts[0])
     for ref in refs[count:]:
-        ref[...] = parts[0]
+        ref[...] = total
 
 
 def eliminate(work, coarse):
@@ -345,7 +395,7 @@
     )
 
 
-def final_kernel(terms_ref, basis_ref, jump_ref, multipliers_ref, amplitudes_ref):
+def final_kernel(terms_ref, basis_ref, jump_ref, scale_ref, multipliers_ref, amplitudes_ref):
     coarse = terms_ref.shape[0] // 2
     loads = basis_ref.shape[0] - coarse
     groups = coarse // GROUP
@@ -353,6 +403,9 @@
     def total(values):
         return jnp.sum(values, axis=0, keepdims=True)
 
+    scale = scale_of(terms_ref[...])
+    ratio = scale_ref[:1, : scale.shape[1]] / scale
+    jump = jump_ref[...] * jnp.concatenate([ratio] * (jump_ref.shape[1] // ratio.shape[1]), axis=1)
     by_mode, (sums, last_sums), (top, low) = unpack(terms_ref[...])
     res_res, res_image, jump_jump, jump_second = (sums[:, at * loads : (at + 1) * loads] for at in range(4))
     res_second, diagonal = last_sums[:, :loads], last_sums[:, loads : loads + coarse]
@@ -379,9 +432,9 @@
     )
     shares = 2.0 * (inverse_image - inverse_h_amounts)
     both = jnp.concatenate([amounts, shares], axis=0).T
-    basis_g, jump_z_rows = basis_ref[loads:], jump_ref[loads:]
+    basis_g, jump_z_rows = basis_ref[loads:], jump[loads:]
     d = basis_ref[:loads] - thin_dot(both[:, :coarse], basis_g)
-    u = jump_ref[:loads] - thin_dot(both, jnp.concatenate([jump_z_rows, basis_g], axis=0))
+    u = jump[:loads] - thin_dot(both, jnp.concatenate([jump_z_rows, basis_g], axis=0))
     products = small_dot(jnp.concatenate([g_h, z_z], axis=0), shares)
     image_d = image_g - h_amounts
     inner = res_res - total(amounts * coarse_res)
@@ -401,7 +454,8 @@
     amplitudes_ref[...] = jnp.concatenate(
         [amplitudes[label * GROUP : label * GROUP + MODES] for label in range(groups)], axis=0
     )
-    weights = jnp.concatenate([on_d, on_u, jnp.zeros((6, loads), jnp.float32)], axis=0).T
+    inverse = 1.0 / scale[:, :loads]
+    weights = jnp.concatenate([on_d * inverse, on_u * inverse, jnp.zeros((6, loads), jnp.float32)], axis=0).T
     multipliers_ref[...] = weights[:, 0:1] * d - weights[:, 1:2] * u
 
 
@@ -432,16 +486,15 @@
     return permute(jnp.concatenate([near, *(pair[near.shape[0] :] for pair in pairs)], axis=0), 1)
 
 
-def total(terms):
+def total(terms, powers):
     chips = [(offset + 1, 0) for offset in reversed(range(2, lax.axis_size("sub"), 2))]
-    chips = chips[-1:] + chips[:-1]
     planes = [(1, offset) for offset in reversed(range(1, lax.axis_size("rep")))]
     copies = [terms]
     for offsets, following in (([(1, 0)], len(chips)), (chips, len(planes)), (planes, 1)):
         parts = [permute(copy, *offset) for copy, offset in zip(copies, offsets)]
         kernel = functools.partial(sum_kernel, len(parts) + 1)
-        copies = call(kernel, [(terms.shape, terms.dtype)] * following, [VMEM] * (len(parts) + 1), "sum")(
-            *parts, copies[0]
+        copies = call(kernel, [(terms.shape, terms.dtype)] * following, [VMEM] * (len(parts) + 2), "sum")(
+            powers, *parts, copies[0]
         )
     return copies[0]
 
@@ -500,20 +553,24 @@
         first_kernel, [half, tall, *pairs(height)], [VMEM] * (5 + len(send)), "first"
     )(far, placed, half_image, got_near, near, *send)
     got = to_chips(*image_send)
-    basis, terms, sums, near, back, stay = call(
-        middle_kernel, [tall, wide, ((GROUP, loads), f32), *singles(height)], [VMEM] * 5, "middle", flops=4 * rows * rows * height
-    )(edge, slots, straight_jump, handed_jump, image)
-    got_near = to_core(near, *got)
+    packed = ((2 * GROUP * groups, 4 * loads), f32)
+    basis, scale, powers, terms, sums, near, back, stay = call(
+        middle_kernel,
+        [tall, ((GROUP, rows), f32), packed, wide, ((GROUP, loads), f32), *singles(height)],
+        [VMEM] * 6,
+        "middle",
+        flops=4 * rows * rows * height,
+    )(edge, slots, operator, straight_jump, handed_jump, image)
+    got_near = to_core(near, *got[::-1])
     half_jump, half_second = call(
         second_half_kernel, [tall, tall], [VMEM] * (4 + 2 * len(got)), "second_half", flops=4 * rows * rows * height
     )(slots, placed, stay, back, *image_send, *got)
-    packed = ((2 * GROUP * groups, 4 * loads), f32)
-    jump, terms = call(second_kernel, [tall, packed], [VMEM] * (9 + len(got)), "second")(
-        slots, placed, basis, half_jump, half_second, terms, sums, got_near, near, *image_send
+    jump, terms = call(second_kernel, [tall, packed], [VMEM] * (10 + len(got)), "second")(
+        slots, placed, basis, half_jump, half_second, scale, terms, sums, got_near, near, *image_send
     )
     multipliers, amplitudes = call(
-        final_kernel, [((loads, rows), f32), ((MODES * groups, loads), f32)], [VMEM] * 3, "final"
-    )(total(terms), basis, jump)
+        final_kernel, [((loads, rows), f32), ((MODES * groups, loads), f32)], [VMEM] * 4, "final"
+    )(total(terms, powers), basis, jump, scale)
     return multipliers, amplitudes.T
 
 

time: 37.9 us -> 38.3 us (1.011)
  transfers between devices with their start and end apart: 15 -> 15, of which waited for: 12 -> 11; matrix products, arithmetic and copies ran while one was open for 0% -> 0% of each run, Pallas kernels for 14% -> 14%
where the time goes in v7:
time: 38.3 us; the launch traced here: 38.1 us
  starting transfers between devices  15.5 us (40%)
  Pallas kernels  12 us (31%)
  waiting for transfers between devices  9.76 us (25%)
  between operations  0.76 us (2%)
    ppermute x15, starting transfers between devices, permute(): lax.ppermute(values, ('sub', 'rep'), [(at, at ^ offset) for at in range(p...  15.5 us
    ppermute x15, waiting for transfers between devices, permute(): lax.ppermute(values, ('sub', 'rep'), [(at, at ^ offset) for at in range(p...  9.76 us
    pallas_call x1, Pallas kernels, fused_body(): call(ready_kernel, [((rows, 3 * per_peer), jnp.bfloat16), halves, halves,...  2.97 us
    pallas_call x1, Pallas kernels, fused_body(): call(final_kernel, [((loads, rows), f32), ((MODES * groups, loads), f32)]...  2.46 us
    pallas_call x1, Pallas kernels, fused_body(): call(place_kernel, [((rows, rows - 2 * per_peer), jnp.bfloat16), ((short,...  1.77 us
    pallas_call x1, Pallas kernels, fused_body(): call(middle_kernel, [tall, ((GROUP, rows), f32), packed, wide, ((GROUP, l...  1.3 us
    pallas_call x1, Pallas kernels, fused_body(): call(second_kernel, [tall, packed], [VMEM] * (10 + len(got)), 'second')  1.25 us
    pallas_call x1, Pallas kernels, fused_body(): call(first_kernel, [half, tall, *pairs(height)], [VMEM] * (5 + len(send))...  0.79 us
  transfers between devices with their start and end apart: 15, of which 11 were waited for; matrix products, arithmetic and copies ran while one was open for 0% of the time, Pallas kernels for 14%

profile of v7, /device:TPU:0, one launch (start us, length us, event | category | flops | bytes accessed | tf_op | source)
XLA Modules:
  0.0 38.1 jit_solution(13274740446362411975)
XLA Ops:
  0.6 1.8 %place.1 = (bf16[1024,768]{1,0:T(8,128)(2,1)S(1)}, f32[40,1024]{1,0:T(8,128)S(1)}, bf16[1,1024,1024]{2,1,0:T(8,128)(2,1)S(1)}, s32[1,1024]{1,0:T(1,128)S(1)}, f3...) custom-call(s32[1,1024]{1,0:T(1,128)} %route_hbm.1, s32[1,32]{1,0:T(1,128)} %bitcast.4, ...), custom_call_target="tpu_custom_call" | custom-call | bytes 1048576 | tf_op jit(solution)/shard_map/place/pallas_call | solution.py:525
  2.4 3.4 %collective-permute-start = (f32[80,128]{1,0:T(8,128)S(1)}, f32[80,128]{1,0:T(8,128)S(1)}, u32[]{:S(2)}, u32[]{:S(2)}) collective-permute-start(f32[80,128]{1,0:T(8,128)S(1)} %get-tuple-element.51.refs_0_), channel_id=1, source_target_pairs={{0,28},{1,29},{2,30},{3,31},{4,24},{5,25},{6,26},{7,27},{8,20},{9,... | collective-permute-start | bytes 122888 | tf_op jit(solution)/shard_map/ppermute | solution.py:478
  5.8 0.8 %collective-permute-start.1 = (f32[80,128]{1,0:T(8,128)S(1)}, f32[80,128]{1,0:T(8,128)S(1)}, u32[]{:S(2)}, u32[]{:S(2)}) collective-permute-start(f32[80,128]{1,0:T(8,128)S(1)} %get-tuple-element.52.refs_1_), channel_id=1, source_target_pairs={{0,20},{1,21},{2,22},{3,23},{4,16},{5,17},{6,18},{7,19},{8,28},{9,... | collective-permute-start | bytes 122888 | tf_op jit(solution)/shard_map/ppermute | solution.py:478
  6.6 0.1 collective-permute-start.2
  6.7 3.0 %ready.1 = (bf16[1024,384]{1,0:T(8,128)(2,1)S(1)}, bf16[2,1024,512]{2,1,0:T(8,128)(2,1)S(1)}, bf16[2,1024,512]{2,1,0:T(8,128)(2,1)S(1)}, f32[40,128]{1,0:T(8,128...) custom-call(s32[1,1024]{1,0:T(1,128)S(1)} %get-tuple-element.42.route_ref, ...), custom_call_target="tpu_custom_call" | custom-call | flops 2147483648 | bytes 1048576 | tf_op jit(solution)/shard_map/ready/pallas_call | solution.py:540
  9.7 0.7 %collective-permute-done.2.refs_5_ = f32[80,128]{1,0:T(8,128)S(1)} collective-permute-done((f32[80,128]{1,0:T(8,128)S(1)}, f32[80,128]{1,0:T(8,128)S(1)}, u32[]{:S(2)}, u32[]{:S(2)}) %collective-permute-start.2) | collective-permute-done | bytes 40992 | tf_op jit(solution)/shard_map/ppermute | solution.py:478
  10.4 0.0 collective-permute-done.1.refs_4_
  10.4 0.0 collective-permute-done.refs_3_
  10.4 0.2 collective-permute-start.3
  10.6 0.4 %first_half.1 = (f32[48,512]{1,0:T(8,128)S(1)}, f32[48,1024]{1,0:T(8,128)S(1)}) custom-call(bf16[2,1024,512]{2,1,0:T(8,128)(2,1)S(1)} %get-tuple-element.48.placed_ref, f32[40,128]{1,0:T(8,128)S(1)} %get-tuple-element.49.stay_ref, f32[40,128]{1,0:T(8,128)S(1)} %get-tuple-element.50.back_ref, f32[80,128]{1,0:T(8,128)S(1)} %get-tuple-element.51.refs_0_, ...), custom_call_target="tpu_custom_call" | custom-call | flops 100663296 | bytes 1048576 | tf_op jit(solution)/shard_map/first_half/pallas_call | solution.py:549
  11.1 0.7 %collective-permute-done.3.got_ref = f32[160,128]{1,0:T(8,128)S(1)} collective-permute-done((f32[160,128]{1,0:T(8,128)S(1)}, f32[160,128]{1,0:T(8,128)S(1)}, u32[]{:S(2)}, u32[]{:S(2)}) %collective-permute-start.3) | collective-permute-done | bytes 81952 | tf_op jit(solution)/shard_map/ppermute | solution.py:478
  11.8 0.8 %first.1 = (f32[48,512]{1,0:T(8,128)S(1)}, f32[48,1024]{1,0:T(8,128)S(1)}, f32[96,128]{1,0:T(8,128)S(1)}, f32[96,128]{1,0:T(8,128)S(1)}, f32[96,128]{1,0:T(8,128)S(1)}) custom-call(bf16[1024,768]{1,0:T(8,128)(2,1)S(1)} %get-tuple-element.43.far_ref, bf16[2,1024,512]{2,1,0:T(8,128)(2,1)S(1)} %get-tuple-element.48.placed_ref, ...), custom_call_target="tpu_custom_call" | custom-call | bytes 1048576 | tf_op jit(solution)/shard_map/first/pallas_call | solution.py:552
  12.6 1.9 %collective-permute-start.4 = (f32[96,128]{1,0:T(8,128)S(1)}, f32[96,128]{1,0:T(8,128)S(1)}, u32[]{:S(2)}, u32[]{:S(2)}) collective-permute-start(f32[96,128]{1,0:T(8,128)S(1)} %get-tuple-element.63.refs_0_), channel_id=1, source_target_pairs={{0,28},{1,29},{2,30},{3,31},{4,24},{5,25},{6,26},{7,27},{8,20},{9,... | collective-permute-start | bytes 147464 | tf_op jit(solution)/shard_map/ppermute | solution.py:478
  14.5 0.3 collective-permute-start.5
  14.8 0.8 %collective-permute-start.6 = (f32[96,128]{1,0:T(8,128)S(1)}, f32[96,128]{1,0:T(8,128)S(1)}, u32[]{:S(2)}, u32[]{:S(2)}) collective-permute-start(f32[96,128]{1,0:T(8,128)S(1)} %get-tuple-element.65.refs_2_), channel_id=1, source_target_pairs={{0,12},{1,13},{2,14},{3,15},{4,8},{5,9},{6,10},{7,11},{8,4},{9,5},... | collective-permute-start | bytes 147464 | tf_op jit(solution)/shard_map/ppermute | solution.py:478
  15.6 1.3 %middle.1 = (f32[48,1024]{1,0:T(8,128)S(1)}, f32[8,1024]{1,0:T(8,128)S(1)}, f32[32,128]{1,0:T(8,128)S(1)}, f32[48,128]{1,0:T(8,128)S(1)}, f32[8,32]{1,0:T(8,128)...) custom-call(bf16[1024,384]{1,0:T(8,128)(2,1)S(1)} %get-tuple-element.46.edge_ref, ...), custom_call_target="tpu_custom_call" | custom-call | flops 201326592 | bytes 1048576 | tf_op jit(solution)/shard_map/middle/pallas_call | solution.py:557
  16.9 0.3 collective-permute-done.4.refs_3_
  17.2 1.1 %collective-permute-done.5.refs_4_ = f32[96,128]{1,0:T(8,128)S(1)} collective-permute-done((f32[96,128]{1,0:T(8,128)S(1)}, f32[96,128]{1,0:T(8,128)S(1)}, u32[]{:S(2)}, u32[]{:S(2)}) %collective-permute-start.5) | collective-permute-done | bytes 49184 | tf_op jit(solution)/shard_map/ppermute | solution.py:478
  18.3 0.0 collective-permute-done.6.refs_5_
  18.3 0.4 %collective-permute-start.7 = (f32[192,128]{1,0:T(8,128)S(1)}, f32[192,128]{1,0:T(8,128)S(1)}, u32[]{:S(2)}, u32[]{:S(2)}) collective-permute-start(f32[192,128]{1,0:T(8,128)S(1)} %pad_maximum_fusion), channel_id=1, source_target_pairs={{0,4},{1,5},{2,6},{3,7},{4,0},{5,1},{6,2},{7,3},{8,12},{9,13},{10,... | collective-permute-start | bytes 294920 | tf_op jit(solution)/shard_map/ppermute | solution.py:478
  18.7 0.7 %second_half.1 = (f32[48,1024]{1,0:T(8,128)S(1)}, f32[48,1024]{1,0:T(8,128)S(1)}) custom-call(bf16[2,1024,512]{2,1,0:T(8,128)(2,1)S(1)} %get-tuple-element.47.slots_ref, bf16[2,1024,512]{2,1,0:T(8,128)(2,1)S(1)} %get-tuple-element.48.placed_ref, f32[48,128]{1,0:T(8,128)S(1)} %get-tuple-element.61.stay_ref, f32[48,128]{1,0:T(8,128)S(1)} %get-tuple-element.62.back_ref, ...), custom_call_target="tpu_custom_call" | custom-call | flops 201326592 | bytes 1048576 | tf_op jit(solution)/shard_map/second_half/pallas_call | solution.py:565
  19.5 0.2 collective-permute-done.7.got_ref
  19.7 1.3 %second.1 = (f32[48,1024]{1,0:T(8,128)S(1)}, f32[32,128]{1,0:T(8,128)S(1)}) custom-call(bf16[2,1024,512]{2,1,0:T(8,128)(2,1)S(1)} %get-tuple-element.47.slots_ref, bf16[2,1024,512]{2,1,0:T(8,128)(2,1)S(1)} %get-tuple-element.48.placed_ref, f32[48,1024]{1,0:T(8,128)S(1)} %get-tuple-element.60.basis_ref, f32[48,1024]{1,0:T(8,128)S(1)} %get-tuple-element.66.half_jump_ref, ...), custom_call_target="tpu_custom_call" | custom-call | bytes 1048576 | tf_op jit(solution)/shard_map/second/pallas_call | solution.py:568
  20.9 0.4 %collective-permute-start.8 = (f32[32,128]{1,0:T(8,128)S(1)}, f32[32,128]{1,0:T(8,128)S(1)}, u32[]{:S(2)}, u32[]{:S(2)}) collective-permute-start(f32[32,128]{1,0:T(8,128)S(1)} %get-tuple-element.72.refs_1_), channel_id=1, source_target_pairs={{0,4},{1,5},{2,6},{3,7},{4,0},{5,1},{6,2},{7,3},{8,12},{9,13},{10,... | collective-permute-start | bytes 49160 | tf_op jit(solution)/shard_map/ppermute | solution.py:478
  21.3 0.8 %collective-permute-done.8.refs_0_ = f32[32,128]{1,0:T(8,128)S(1)} collective-permute-done((f32[32,128]{1,0:T(8,128)S(1)}, f32[32,128]{1,0:T(8,128)S(1)}, u32[]{:S(2)}, u32[]{:S(2)}) %collective-permute-start.8) | collective-permute-done | bytes 16416 | tf_op jit(solution)/shard_map/ppermute | solution.py:478
  22.2 0.1 sum.3
  22.3 2.0 %collective-permute-start.9 = (f32[32,128]{1,0:T(8,128)S(1)}, f32[32,128]{1,0:T(8,128)S(1)}, u32[]{:S(2)}, u32[]{:S(2)}) collective-permute-start(f32[32,128]{1,0:T(8,128)S(1)} %get-tuple-element.73.refs_3_), channel_id=1, source_target_pairs={{0,28},{1,29},{2,30},{3,31},{4,24},{5,25},{6,26},{7,27},{8,20},{9,... | collective-permute-start | bytes 49160 | tf_op jit(solution)/shard_map/ppermute | solution.py:478
  24.3 0.4 %collective-permute-start.10 = (f32[32,128]{1,0:T(8,128)S(1)}, f32[32,128]{1,0:T(8,128)S(1)}, u32[]{:S(2)}, u32[]{:S(2)}) collective-permute-start(f32[32,128]{1,0:T(8,128)S(1)} %get-tuple-element.74), channel_id=1, source_target_pairs={{0,20},{1,21},{2,22},{3,23},{4,16},{5,17},{6,18},{7,19},{8,28},{9,... | collective-permute-start | bytes 49160 | tf_op jit(solution)/shard_map/ppermute | solution.py:478
  24.7 0.8 %collective-permute-start.11 = (f32[32,128]{1,0:T(8,128)S(1)}, f32[32,128]{1,0:T(8,128)S(1)}, u32[]{:S(2)}, u32[]{:S(2)}) collective-permute-start(f32[32,128]{1,0:T(8,128)S(1)} %get-tuple-element.75), channel_id=1, source_target_pairs={{0,12},{1,13},{2,14},{3,15},{4,8},{5,9},{6,10},{7,11},{8,4},{9,5},... | collective-permute-start | bytes 49160 | tf_op jit(solution)/shard_map/ppermute | solution.py:478
  25.5 0.9 %collective-permute-done.9.refs_0_ = f32[32,128]{1,0:T(8,128)S(1)} collective-permute-done((f32[32,128]{1,0:T(8,128)S(1)}, f32[32,128]{1,0:T(8,128)S(1)}, u32[]{:S(2)}, u32[]{:S(2)}) %collective-permute-start.9) | collective-permute-done | bytes 16416 | tf_op jit(solution)/shard_map/ppermute | solution.py:478
  26.4 1.1 %collective-permute-done.10.refs_1_ = f32[32,128]{1,0:T(8,128)S(1)} collective-permute-done((f32[32,128]{1,0:T(8,128)S(1)}, f32[32,128]{1,0:T(8,128)S(1)}, u32[]{:S(2)}, u32[]{:S(2)}) %collective-permute-start.10) | collective-permute-done | bytes 16416 | tf_op jit(solution)/shard_map/ppermute | solution.py:478
  27.5 0.4 %collective-permute-done.11.refs_2_ = f32[32,128]{1,0:T(8,128)S(1)} collective-permute-done((f32[32,128]{1,0:T(8,128)S(1)}, f32[32,128]{1,0:T(8,128)S(1)}, u32[]{:S(2)}, u32[]{:S(2)}) %collective-permute-start.11) | collective-permute-done | bytes 16416 | tf_op jit(solution)/shard_map/ppermute | solution.py:478
  27.9 0.1 sum.4
  28.0 3.4 %collective-permute-start.12 = (f32[32,128]{1,0:T(8,128)S(1)}, f32[32,128]{1,0:T(8,128)S(1)}, u32[]{:S(2)}, u32[]{:S(2)}) collective-permute-start(f32[32,128]{1,0:T(8,128)S(1)} %get-tuple-element.76.refs_3_), channel_id=1, source_target_pairs={{0,7},{1,6},{2,5},{3,4},{4,3},{5,2},{6,1},{7,0},{8,15},{9,14},{10,... | collective-permute-start | bytes 49160 | tf_op jit(solution)/shard_map/ppermute | solution.py:478
  31.4 0.0 collective-permute-start.13
  31.4 0.6 %collective-permute-start.14 = (f32[32,128]{1,0:T(8,128)S(1)}, f32[32,128]{1,0:T(8,128)S(1)}, u32[]{:S(2)}, u32[]{:S(2)}) collective-permute-start(f32[32,128]{1,0:T(8,128)S(1)} %get-tuple-element.78), channel_id=1, source_target_pairs={{0,5},{1,4},{2,7},{3,6},{4,1},{5,0},{6,3},{7,2},{8,13},{9,12},{10,... | collective-permute-start | bytes 49160 | tf_op jit(solution)/shard_map/ppermute | solution.py:478
  32.0 1.0 %collective-permute-done.12.refs_0_ = f32[32,128]{1,0:T(8,128)S(1)} collective-permute-done((f32[32,128]{1,0:T(8,128)S(1)}, f32[32,128]{1,0:T(8,128)S(1)}, u32[]{:S(2)}, u32[]{:S(2)}) %collective-permute-start.12) | collective-permute-done | bytes 16416 | tf_op jit(solution)/shard_map/ppermute | solution.py:478
  33.0 2.5 %collective-permute-done.13.refs_1_ = f32[32,128]{1,0:T(8,128)S(1)} collective-permute-done((f32[32,128]{1,0:T(8,128)S(1)}, f32[32,128]{1,0:T(8,128)S(1)}, u32[]{:S(2)}, u32[]{:S(2)}) %collective-permute-start.13) | collective-permute-done | bytes 16416 | tf_op jit(solution)/shard_map/ppermute | solution.py:478
  35.5 0.0 collective-permute-done.14.refs_2_
  35.5 0.1 sum.5.terms_ref
  35.6 2.5 %final.1 = (f32[32,1024]{1,0:T(8,128)}, f32[12,32]{1,0:T(8,128)}) custom-call(f32[32,128]{1,0:T(8,128)S(1)} %sum.5.terms_ref, f32[48,1024]{1,0:T(8,128)S(1)} %get-tuple-element.60.basis_ref, f32[48,1024]{1,0:T(8,128)S(1)} %get-tuple-element.79.jump_ref, f32[8,1024]{1,0:T(8,128)S(1)} %get-tuple-element.68.scale_ref), custom_call_target="tpu_custom_call" | custom-call | bytes 1048576 | tf_op jit(solution)/shard_map/final/pallas_call | solution.py:571
  (8 shorter events, 0.0 us)
Async XLA Ops:
  2.4 8.0 %collective-permute-start = (f32[80,128]{1,0:T(8,128)S(1)}, f32[80,128]{1,0:T(8,128)S(1)}, u32[]{:S(2)}, u32[]{:S(2)}) collective-permute-start(f32[80,128]{1,0:T(8,128)S(1)} %get-tuple-element.51.refs_0_), channel_id=1, source_target_pairs={{0,28},{1,29},{2,30},{3,31},{4,24},{5,25},{6,26},{7,27},{8,20},{9,... | collective-permute-start | bytes 122888 | tf_op jit(solution)/shard_map/ppermute | solution.py:478
  5.8 4.6 %collective-permute-start.1 = (f32[80,128]{1,0:T(8,128)S(1)}, f32[80,128]{1,0:T(8,128)S(1)}, u32[]{:S(2)}, u32[]{:S(2)}) collective-permute-start(f32[80,128]{1,0:T(8,128)S(1)} %get-tuple-element.52.refs_1_), channel_id=1, source_target_pairs={{0,20},{1,21},{2,22},{3,23},{4,16},{5,17},{6,18},{7,19},{8,28},{9,... | collective-permute-start | bytes 122888 | tf_op jit(solution)/shard_map/ppermute | solution.py:478
  6.6 3.8 %collective-permute-start.2 = (f32[80,128]{1,0:T(8,128)S(1)}, f32[80,128]{1,0:T(8,128)S(1)}, u32[]{:S(2)}, u32[]{:S(2)}) collective-permute-start(f32[80,128]{1,0:T(8,128)S(1)} %get-tuple-element.53.refs_2_), channel_id=1, source_target_pairs={{0,12},{1,13},{2,14},{3,15},{4,8},{5,9},{6,10},{7,11},{8,4},{9,5},... | collective-permute-start | bytes 122888 | tf_op jit(solution)/shard_map/ppermute | solution.py:478
  10.4 1.3 %collective-permute-start.3 = (f32[160,128]{1,0:T(8,128)S(1)}, f32[160,128]{1,0:T(8,128)S(1)}, u32[]{:S(2)}, u32[]{:S(2)}) collective-permute-start(f32[160,128]{1,0:T(8,128)S(1)} %pad_maximum_fusion.1), channel_id=1, source_target_pairs={{0,4},{1,5},{2,6},{3,7},{4,0},{5,1},{6,2},{7,3},{8,12},{9,13},{10,... | collective-permute-start | bytes 245768 | tf_op jit(solution)/shard_map/ppermute | solution.py:478
  12.6 4.6 %collective-permute-start.4 = (f32[96,128]{1,0:T(8,128)S(1)}, f32[96,128]{1,0:T(8,128)S(1)}, u32[]{:S(2)}, u32[]{:S(2)}) collective-permute-start(f32[96,128]{1,0:T(8,128)S(1)} %get-tuple-element.63.refs_0_), channel_id=1, source_target_pairs={{0,28},{1,29},{2,30},{3,31},{4,24},{5,25},{6,26},{7,27},{8,20},{9,... | collective-permute-start | bytes 147464 | tf_op jit(solution)/shard_map/ppermute | solution.py:478
  14.5 3.8 %collective-permute-start.5 = (f32[96,128]{1,0:T(8,128)S(1)}, f32[96,128]{1,0:T(8,128)S(1)}, u32[]{:S(2)}, u32[]{:S(2)}) collective-permute-start(f32[96,128]{1,0:T(8,128)S(1)} %get-tuple-element.64.refs_1_), channel_id=1, source_target_pairs={{0,20},{1,21},{2,22},{3,23},{4,16},{5,17},{6,18},{7,19},{8,28},{9,... | collective-permute-start | bytes 147464 | tf_op jit(solution)/shard_map/ppermute | solution.py:478
  14.8 3.5 %collective-permute-start.6 = (f32[96,128]{1,0:T(8,128)S(1)}, f32[96,128]{1,0:T(8,128)S(1)}, u32[]{:S(2)}, u32[]{:S(2)}) collective-permute-start(f32[96,128]{1,0:T(8,128)S(1)} %get-tuple-element.65.refs_2_), channel_id=1, source_target_pairs={{0,12},{1,13},{2,14},{3,15},{4,8},{5,9},{6,10},{7,11},{8,4},{9,5},... | collective-permute-start | bytes 147464 | tf_op jit(solution)/shard_map/ppermute | solution.py:478
  18.3 1.4 %collective-permute-start.7 = (f32[192,128]{1,0:T(8,128)S(1)}, f32[192,128]{1,0:T(8,128)S(1)}, u32[]{:S(2)}, u32[]{:S(2)}) collective-permute-start(f32[192,128]{1,0:T(8,128)S(1)} %pad_maximum_fusion), channel_id=1, source_target_pairs={{0,4},{1,5},{2,6},{3,7},{4,0},{5,1},{6,2},{7,3},{8,12},{9,13},{10,... | collective-permute-start | bytes 294920 | tf_op jit(solution)/shard_map/ppermute | solution.py:478
  20.9 1.2 %collective-permute-start.8 = (f32[32,128]{1,0:T(8,128)S(1)}, f32[32,128]{1,0:T(8,128)S(1)}, u32[]{:S(2)}, u32[]{:S(2)}) collective-permute-start(f32[32,128]{1,0:T(8,128)S(1)} %get-tuple-element.72.refs_1_), channel_id=1, source_target_pairs={{0,4},{1,5},{2,6},{3,7},{4,0},{5,1},{6,2},{7,3},{8,12},{9,13},{10,... | collective-permute-start | bytes 49160 | tf_op jit(solution)/shard_map/ppermute | solution.py:478
  22.3 4.1 %collective-permute-start.9 = (f32[32,128]{1,0:T(8,128)S(1)}, f32[32,128]{1,0:T(8,128)S(1)}, u32[]{:S(2)}, u32[]{:S(2)}) collective-permute-start(f32[32,128]{1,0:T(8,128)S(1)} %get-tuple-element.73.refs_3_), channel_id=1, source_target_pairs={{0,28},{1,29},{2,30},{3,31},{4,24},{5,25},{6,26},{7,27},{8,20},{9,... | collective-permute-start | bytes 49160 | tf_op jit(solution)/shard_map/ppermute | solution.py:478
  24.3 3.2 %collective-permute-start.10 = (f32[32,128]{1,0:T(8,128)S(1)}, f32[32,128]{1,0:T(8,128)S(1)}, u32[]{:S(2)}, u32[]{:S(2)}) collective-permute-start(f32[32,128]{1,0:T(8,128)S(1)} %get-tuple-element.74), channel_id=1, source_target_pairs={{0,20},{1,21},{2,22},{3,23},{4,16},{5,17},{6,18},{7,19},{8,28},{9,... | collective-permute-start | bytes 49160 | tf_op jit(solution)/shard_map/ppermute | solution.py:478
  24.7 3.2 %collective-permute-start.11 = (f32[32,128]{1,0:T(8,128)S(1)}, f32[32,128]{1,0:T(8,128)S(1)}, u32[]{:S(2)}, u32[]{:S(2)}) collective-permute-start(f32[32,128]{1,0:T(8,128)S(1)} %get-tuple-element.75), channel_id=1, source_target_pairs={{0,12},{1,13},{2,14},{3,15},{4,8},{5,9},{6,10},{7,11},{8,4},{9,5},... | collective-permute-start | bytes 49160 | tf_op jit(solution)/shard_map/ppermute | solution.py:478
  28.0 5.0 %collective-permute-start.12 = (f32[32,128]{1,0:T(8,128)S(1)}, f32[32,128]{1,0:T(8,128)S(1)}, u32[]{:S(2)}, u32[]{:S(2)}) collective-permute-start(f32[32,128]{1,0:T(8,128)S(1)} %get-tuple-element.76.refs_3_), channel_id=1, source_target_pairs={{0,7},{1,6},{2,5},{3,4},{4,3},{5,2},{6,1},{7,0},{8,15},{9,14},{10,... | collective-permute-start | bytes 49160 | tf_op jit(solution)/shard_map/ppermute | solution.py:478
  31.4 4.1 %collective-permute-start.13 = (f32[32,128]{1,0:T(8,128)S(1)}, f32[32,128]{1,0:T(8,128)S(1)}, u32[]{:S(2)}, u32[]{:S(2)}) collective-permute-start(f32[32,128]{1,0:T(8,128)S(1)} %get-tuple-element.77), channel_id=1, source_target_pairs={{0,6},{1,7},{2,4},{3,5},{4,2},{5,3},{6,0},{7,1},{8,14},{9,15},{10,... | collective-permute-start | bytes 49160 | tf_op jit(solution)/shard_map/ppermute | solution.py:478
  31.4 4.1 %collective-permute-start.14 = (f32[32,128]{1,0:T(8,128)S(1)}, f32[32,128]{1,0:T(8,128)S(1)}, u32[]{:S(2)}, u32[]{:S(2)}) collective-permute-start(f32[32,128]{1,0:T(8,128)S(1)} %get-tuple-element.78), channel_id=1, source_target_pairs={{0,5},{1,4},{2,7},{3,6},{4,1},{5,0},{6,3},{7,2},{8,13},{9,12},{10,... | collective-permute-start | bytes 49160 | tf_op jit(solution)/shard_map/ppermute | solution.py:478
